TPU v7x, 32 devices: a whole 2x2x4 slice. The times are simulated.
32 devices in a mesh: dp: 8 (over z, y), mp: 4 (over x, core).
Axes of the slice: x: 2, y: 2, z: 4, core: 2. Of those that a mesh axis runs over, the one named last changes fastest.
Arguments:
- latents: float32 [64, 256, 1152], P('dp', None, 'mp'), may hold values from -6 to 6
- condition: float32 [64, 1152], P('dp', 'mp'), may hold values from -6 to 6
- cotangent: float32 [64, 256, 1152], P('dp', None, 'mp'), may hold values from -6 to 6
- noise_bins: int32 [64], P('dp'), may hold values from 0 to 7
- image_counts: int32 [8], P('dp'), may hold values from 0 to 8, as said below
- ada_weight: bfloat16 [1152, 6, 1152], P(None, None, 'mp'), may hold values from -0.1875 to 0.1875
- ada_bias: bfloat16 [6, 1152], P(None, 'mp'), may hold values from -3 to 3
- qkv_weight: bfloat16 [1152, 3, 1152], P(None, None, 'mp'), may hold values from -0.1875 to 0.1875
- norm_gains: bfloat16 [2, 72], replicated, may hold values from 0.796875 to 1.59375
- proj_weight: bfloat16 [1152, 1152], P('mp'), may hold values from -0.5 to 0.5
- gate_up_weight: bfloat16 [1152, 2, 3072], P(None, None, 'mp'), may hold values from -0.1875 to 0.1875
- down_weight: bfloat16 [3072, 1152], P('mp'), may hold values from -0.109375 to 0.109375
Outputs:
- output: float32 [64, 256, 1152], P('dp', None, 'mp')
- grad_latents: float32 [64, 256, 1152], P('dp', None, 'mp')
- grad_condition: float32 [64, 1152], P('dp', 'mp')
- grad_ada_weight: float32 [1152, 6, 1152], P(None, None, 'mp')
- grad_ada_bias: float32 [6, 1152], P(None, 'mp')
- grad_qkv_weight: float32 [1152, 3, 1152], P(None, None, 'mp')
- grad_norm_gains: float32 [2, 72], replicated
- grad_proj_weight: float32 [1152, 1152], P('mp')
- grad_gate_up_weight: float32 [1152, 2, 3072], P(None, None, 'mp')
- grad_down_weight: float32 [3072, 1152], P('mp')
Inputs may be any that keep to these rules, and one draw needn't show every extreme that they name: The live slots of a device are its first image_counts ones; the counts sum to 32. Numbering all live images in the order of devices and then slots, from 0, every image's number lies in its own device's block of 4 numbers (device index times 4 onwards) or in the next device's block.
All inputs are finite; a program needn't handle non-finite values.
Results may differ from a plain program's by a relative error of at most 0.013.
Values may be sent and summed in bfloat16 or wider, within the bound.
No kernel may reach another device: no remote copies, remote signals or barrier semaphores. Data moves between devices by JAX's collectives and lax.ppermute only.
A program may use at most 192 MiB of HBM per device.

v0:
```python
import jax
import jax.numpy as jnp
from jax import lax
from jax.sharding import PartitionSpec as P

D = 1152
HEAD = 72
P_SIZE = 256
GRID = 16
IMG_DEV = 4
NBINS = 8


EPSILON = 1e-06


def prefix(value, axis, combine, identity):
    devices, index = (lax.axis_size(axis), lax.axis_index(axis))
    everything = lax.all_gather(value, axis)
    start = jnp.broadcast_to(jnp.asarray(identity, value.dtype), value.shape)

    def turn(k, before):
        reached = k < index
        new = combine(before, everything[k])
        return jnp.where(reached, new, before)

    return lax.fori_loop(0, devices, turn, start)


def from_behind(value, axis, by):
    devices = lax.axis_size(axis)
    pairs = [(i, i + by) for i in range(devices) if 0 <= i + by < devices]
    return lax.ppermute(value, axis, pairs)


def rope_tables():
    quarter = HEAD // 4
    frequency = 10000.0 ** (-jnp.arange(quarter, dtype=jnp.float32) / quarter)
    patches = jnp.arange(P_SIZE, dtype=jnp.int32)
    row_angle = (patches // GRID).astype(jnp.float32)[:, None, None] * frequency
    col_angle = (patches % GRID).astype(jnp.float32)[:, None, None] * frequency
    return (jnp.cos(row_angle), jnp.sin(row_angle), jnp.cos(col_angle), jnp.sin(col_angle))


def rotate(tensor, rotary_tables, direction):
    cos_row, sin_row, cos_col, sin_col = rotary_tables
    part_a, part_b, part_c, part_d = jnp.split(tensor, 4, axis=-1)
    return jnp.concatenate(
        [
            part_a * cos_row - direction * part_b * sin_row,
            part_b * cos_row + direction * part_a * sin_row,
            part_c * cos_col - direction * part_d * sin_col,
            part_d * cos_col + direction * part_c * sin_col,
        ],
        axis=-1,
    )


def spread(tensor):
    return lax.all_gather(tensor, "mp", axis=2, tiled=True)


def reduce_parts(tensor):
    return lax.psum_scatter(tensor, "mp", scatter_dimension=2, tiled=True)


def row_total(tensor):
    return lax.psum(tensor, "mp")


def shard_norm(rows_in):
    inverse = lax.rsqrt(row_total(jnp.sum(rows_in * rows_in, axis=-1, keepdims=True)) / D + EPSILON)
    return (rows_in * inverse, inverse)


def shard_norm_back(grad_normed, normed, inverse):
    inner_mean = row_total(jnp.sum(grad_normed * normed, axis=-1, keepdims=True)) / D
    return inverse * (grad_normed - normed * inner_mean)


def head_norm(tensor):
    inverse = lax.rsqrt(jnp.mean(tensor * tensor, axis=-1, keepdims=True) + EPSILON)
    return (tensor * inverse, inverse)


def head_norm_back(grad_normed, normed, inverse):
    return inverse * (grad_normed - normed * jnp.mean(grad_normed * normed, axis=-1, keepdims=True))


def project_heads(attn_full, qkv_weight, norm_gains, rotary_tables):
    images, patches = (attn_full.shape[0], attn_full.shape[1])
    projected = jnp.einsum(
        "bpd,dkf->bpkf", attn_full, qkv_weight, preferred_element_type=jnp.float32
    )
    projected = projected.reshape(images, patches, 3, -1, HEAD)
    gain_vals = norm_gains.astype(jnp.float32)
    query_hat, query_inv = head_norm(projected[:, :, 0])
    key_hat, key_inv = head_norm(projected[:, :, 1])
    queries = rotate(query_hat * gain_vals[0], rotary_tables, 1.0).astype(jnp.bfloat16)
    keys_rot = rotate(key_hat * gain_vals[1], rotary_tables, 1.0).astype(jnp.bfloat16)
    values = projected[:, :, 2].astype(jnp.bfloat16)
    scores = jnp.einsum(
        "bphe,bqhe->bhpq", queries, keys_rot, preferred_element_type=jnp.float32
    ) * HEAD ** (-0.5)
    return (queries, keys_rot, values, scores, (query_hat, query_inv, key_hat, key_inv, gain_vals))


def forward_block(latent_row_block, condition_row_block, bin_weights, rotary_tables):
    ada_weight, ada_bias, qkv_weight, norm_gains, proj_weight, gate_up_weight, down_weight = (
        bin_weights
    )
    images, patches = (latent_row_block.shape[0], latent_row_block.shape[1])
    silu_full = spread(jax.nn.silu(condition_row_block).astype(jnp.bfloat16)[:, None, :])[:, 0, :]
    modulation = jnp.einsum(
        "bd,dkf->bkf", silu_full, ada_weight, preferred_element_type=jnp.float32
    ) + ada_bias.astype(jnp.float32)
    shift_one, scale_one, gate_one, shift_two, scale_two, gate_two = jnp.split(
        modulation, 6, axis=1
    )
    normed_one, inverse_one = shard_norm(latent_row_block)
    attn_full = spread((normed_one * (1.0 + scale_one) + shift_one).astype(jnp.bfloat16))
    queries, keys_rot, values, scores, norm_parts = project_heads(
        attn_full, qkv_weight, norm_gains, rotary_tables
    )
    highest = jnp.max(scores, axis=-1, keepdims=True)
    log_total = highest + jnp.log(jnp.sum(jnp.exp(scores - highest), axis=-1, keepdims=True))
    attention = jnp.exp(scores - log_total).astype(jnp.bfloat16)
    heads_out = jnp.einsum("bhpq,bqhe->bphe", attention, values, preferred_element_type=jnp.float32)
    heads_out = heads_out.astype(jnp.bfloat16).reshape(images, patches, -1)
    branch_one = reduce_parts(
        jnp.einsum("bpe,ed->bpd", heads_out, proj_weight, preferred_element_type=jnp.float32)
    )
    middle = latent_row_block + gate_one * branch_one
    normed_two, inverse_two = shard_norm(middle)
    mlp_full = spread((normed_two * (1.0 + scale_two) + shift_two).astype(jnp.bfloat16))
    gate_up = jnp.einsum(
        "bpd,dkf->bpkf", mlp_full, gate_up_weight, preferred_element_type=jnp.float32
    )
    hidden = (jax.nn.silu(gate_up[:, :, 0]) * gate_up[:, :, 1]).astype(jnp.bfloat16)
    branch_two = reduce_parts(
        jnp.einsum("bpf,fd->bpd", hidden, down_weight, preferred_element_type=jnp.float32)
    )
    output = middle + gate_two * branch_two
    stored = (
        silu_full,
        modulation,
        normed_one,
        inverse_one,
        attn_full,
        log_total,
        heads_out,
        branch_one,
        normed_two,
        inverse_two,
        mlp_full,
        branch_two,
    )
    return (output, stored)


def backward_block(grad_out, condition_row_block, stored, bin_weights, rotary_tables):
    (
        silu_full,
        modulation,
        normed_one,
        inverse_one,
        attn_full,
        log_total,
        heads_out,
        branch_one,
        normed_two,
        inverse_two,
        mlp_full,
        branch_two,
    ) = stored
    ada_weight, ada_bias, qkv_weight, norm_gains, proj_weight, gate_up_weight, down_weight = (
        bin_weights
    )
    images, patches = (grad_out.shape[0], grad_out.shape[1])
    shift_one, scale_one, gate_one, shift_two, scale_two, gate_two = jnp.split(
        modulation, 6, axis=1
    )
    grad_gate_two = jnp.sum(grad_out * branch_two, axis=1, keepdims=True)
    grad_branch_two = spread((grad_out * gate_two).astype(jnp.bfloat16))
    gate_up = jnp.einsum(
        "bpd,dkf->bpkf", mlp_full, gate_up_weight, preferred_element_type=jnp.float32
    )
    gate_part, up_part = (gate_up[:, :, 0], gate_up[:, :, 1])
    sigmoid_gate = jax.nn.sigmoid(gate_part)
    silu_gate = gate_part * sigmoid_gate
    hidden = (silu_gate * up_part).astype(jnp.bfloat16)
    grad_down = jnp.einsum(
        "bpf,bpd->fd", hidden, grad_branch_two, preferred_element_type=jnp.float32
    )
    grad_hidden = jnp.einsum(
        "bpd,fd->bpf", grad_branch_two, down_weight, preferred_element_type=jnp.float32
    )
    grad_gate = grad_hidden * up_part * sigmoid_gate * (1.0 + gate_part * (1.0 - sigmoid_gate))
    grad_up = grad_hidden * silu_gate
    grad_gate_up_rows = jnp.stack([grad_gate, grad_up], axis=2).astype(jnp.bfloat16)
    grad_gate_up = jnp.einsum(
        "bpd,bpkf->dkf", mlp_full, grad_gate_up_rows, preferred_element_type=jnp.float32
    )
    mlp_sums = (grad_gate_up, grad_down)
    grad_mlp_in = reduce_parts(
        jnp.einsum(
            "bpkf,dkf->bpd", grad_gate_up_rows, gate_up_weight, preferred_element_type=jnp.float32
        )
    )
    grad_shift_two = jnp.sum(grad_mlp_in, axis=1, keepdims=True)
    grad_scale_two = jnp.sum(grad_mlp_in * normed_two, axis=1, keepdims=True)
    grad_middle = grad_out + shard_norm_back(
        grad_mlp_in * (1.0 + scale_two), normed_two, inverse_two
    )
    grad_gate_one = jnp.sum(grad_middle * branch_one, axis=1, keepdims=True)
    grad_branch_one = spread((grad_middle * gate_one).astype(jnp.bfloat16))
    grad_proj = jnp.einsum(
        "bpe,bpd->ed", heads_out, grad_branch_one, preferred_element_type=jnp.float32
    )
    grad_heads = jnp.einsum(
        "bpd,ed->bpe", grad_branch_one, proj_weight, preferred_element_type=jnp.float32
    )
    grad_heads = grad_heads.astype(jnp.bfloat16).reshape(images, patches, -1, HEAD)
    queries, keys_rot, values, scores, norm_parts = project_heads(
        attn_full, qkv_weight, norm_gains, rotary_tables
    )
    query_hat, query_inv, key_hat, key_inv, gain_vals = norm_parts
    attention = jnp.exp(scores - log_total)
    grad_attention = jnp.einsum(
        "bphe,bqhe->bhpq", grad_heads, values, preferred_element_type=jnp.float32
    )
    grad_values = jnp.einsum(
        "bhpq,bphe->bqhe",
        attention.astype(jnp.bfloat16),
        grad_heads,
        preferred_element_type=jnp.float32,
    )
    grad_scores = (
        attention * (grad_attention - jnp.sum(attention * grad_attention, axis=-1, keepdims=True))
    ).astype(jnp.bfloat16)
    score_scale = HEAD ** (-0.5)
    grad_queries = rotate(
        jnp.einsum("bhpq,bqhe->bphe", grad_scores, keys_rot, preferred_element_type=jnp.float32)
        * score_scale,
        rotary_tables,
        -1.0,
    )
    grad_keys = rotate(
        jnp.einsum("bhpq,bphe->bqhe", grad_scores, queries, preferred_element_type=jnp.float32)
        * score_scale,
        rotary_tables,
        -1.0,
    )
    grad_gains = jnp.stack(
        [
            jnp.sum(grad_queries * query_hat, axis=(0, 1, 2)),
            jnp.sum(grad_keys * key_hat, axis=(0, 1, 2)),
        ]
    )
    grad_query_raw = head_norm_back(grad_queries * gain_vals[0], query_hat, query_inv)
    grad_key_raw = head_norm_back(grad_keys * gain_vals[1], key_hat, key_inv)
    grad_rows = (
        jnp.stack([grad_query_raw, grad_key_raw, grad_values], axis=2)
        .reshape(images, patches, 3, -1)
        .astype(jnp.bfloat16)
    )
    grad_qkv = jnp.einsum("bpd,bpkf->dkf", attn_full, grad_rows, preferred_element_type=jnp.float32)
    grad_attn_in = reduce_parts(
        jnp.einsum("bpkf,dkf->bpd", grad_rows, qkv_weight, preferred_element_type=jnp.float32)
    )
    grad_shift_one = jnp.sum(grad_attn_in, axis=1, keepdims=True)
    grad_scale_one = jnp.sum(grad_attn_in * normed_one, axis=1, keepdims=True)
    grad_latent = grad_middle + shard_norm_back(
        grad_attn_in * (1.0 + scale_one), normed_one, inverse_one
    )
    grad_mod = jnp.concatenate(
        [
            grad_shift_one,
            grad_scale_one,
            grad_gate_one,
            grad_shift_two,
            grad_scale_two,
            grad_gate_two,
        ],
        axis=1,
    ).astype(jnp.bfloat16)
    grad_ada = jnp.einsum("bd,bkf->dkf", silu_full, grad_mod, preferred_element_type=jnp.float32)
    grad_bias = jnp.sum(grad_mod.astype(jnp.float32), axis=0).reshape(-1)
    grad_silu = reduce_parts(
        jnp.einsum("bkf,dkf->bd", grad_mod, ada_weight, preferred_element_type=jnp.float32)[
            :, None, :
        ]
    )[:, 0, :]
    sigmoid_cond = jax.nn.sigmoid(condition_row_block)
    grad_cond = grad_silu * sigmoid_cond * (1.0 + condition_row_block * (1.0 - sigmoid_cond))
    partials = (
        lax.psum_scatter(grad_ada, "dp", scatter_dimension=0, tiled=True),
        lax.psum_scatter(grad_bias, "dp", scatter_dimension=0, tiled=True),
        lax.psum_scatter(grad_qkv, "dp", scatter_dimension=0, tiled=True),
        lax.psum_scatter(grad_proj, "dp", scatter_dimension=1, tiled=True),
        lax.psum_scatter(mlp_sums[0], "dp", scatter_dimension=0, tiled=True),
        lax.psum_scatter(mlp_sums[1], "dp", scatter_dimension=1, tiled=True),
    )
    return (grad_latent, grad_cond, partials, grad_gains)


def expand(valid_rows, tensor):
    return valid_rows.reshape(valid_rows.shape + (1,) * (tensor.ndim - 1))


def select_rows(arrays, positions, upper_bound):
    valid_rows = (positions >= 0) & (positions < upper_bound)
    clipped = jnp.clip(positions, 0, arrays[0].shape[0] - 1)
    return tuple(
        (
            jnp.where(expand(valid_rows, member), jnp.take(member, clipped, axis=0), 0.0)
            for member in arrays
        )
    )


def local(
    latents,
    condition,
    cotangent,
    noise_bins,
    image_counts,
    ada_weight,
    ada_bias,
    qkv_weight,
    norm_gains,
    proj_weight,
    gate_up_weight,
    down_weight,
):
    slot_count = latents.shape[0]
    live_mask = (jnp.arange(slot_count) < image_counts[0]).astype(jnp.float32)
    onehot = (noise_bins[:, None] == jnp.arange(NBINS)[None, :]).astype(jnp.float32)
    histogram = lax.psum(jnp.sum(onehot * live_mask[:, None], axis=0), "dp")
    image_total = IMG_DEV * lax.axis_size("dp")
    bin_load = jnp.sum(onehot * histogram[None, :], axis=1)
    scaling = live_mask * image_total / (NBINS * (bin_load + 1.0 - live_mask))
    bin_weights = (
        ada_weight,
        ada_bias,
        qkv_weight,
        norm_gains,
        proj_weight,
        gate_up_weight,
        down_weight,
    )
    rotary_tables = rope_tables()

    def add_counts(earlier, later):
        return earlier + later

    offset = prefix(image_counts, "dp", add_counts, jnp.zeros_like(image_counts))[0]
    device = lax.axis_index("dp")
    share_ids = jnp.arange(IMG_DEV)
    own_pos = device * IMG_DEV + share_ids - offset
    next_pos = own_pos + IMG_DEV
    carried = (latents, condition, cotangent, scaling)
    send_latents, send_cond, send_cot, send_scaling = select_rows(
        carried, next_pos, image_counts[0]
    )
    incoming = from_behind((send_latents, send_cond, send_cot, send_scaling), "dp", 1)
    staying = select_rows(carried, own_pos, image_counts[0])
    moved_latents, moved_cond, moved_cot, moved_scaling = tuple(
        (staying[member] + incoming[member] for member in range(4))
    )
    result, stored = forward_block(moved_latents, moved_cond, bin_weights, rotary_tables)
    grad_moved, grad_cond_moved, partials, grad_gains = backward_block(
        moved_cot * moved_scaling[:, None, None], moved_cond, stored, bin_weights, rotary_tables
    )
    returned = (
        from_behind(result.astype(jnp.bfloat16), "dp", -1).astype(result.dtype),
        from_behind(grad_moved.astype(jnp.bfloat16), "dp", -1).astype(grad_moved.dtype),
        from_behind(grad_cond_moved.astype(jnp.bfloat16), "dp", -1).astype(grad_cond_moved.dtype),
    )
    rank_here = offset + jnp.arange(slot_count) - device * IMG_DEV
    home_rows = select_rows((result, grad_moved, grad_cond_moved), rank_here, IMG_DEV)
    away_rows = select_rows(returned, rank_here - IMG_DEV, IMG_DEV)
    output, grad_latent, grad_cond = tuple(
        (
            (home_rows[member] + away_rows[member]) * expand(live_mask, home_rows[member])
            for member in range(3)
        )
    )
    grad_gains_total = lax.psum(grad_gains, ("dp", "mp"))
    sum_ada, sum_bias, sum_qkv, sum_proj, sum_gate_up, sum_down = partials
    reduced = (
        lax.all_gather(sum_ada.astype(jnp.bfloat16), "dp", axis=0, tiled=True).astype(
            sum_ada.dtype
        ),
        lax.all_gather(sum_bias.astype(jnp.bfloat16), "dp", axis=0, tiled=True).astype(
            sum_bias.dtype
        ),
        lax.all_gather(sum_qkv.astype(jnp.bfloat16), "dp", axis=0, tiled=True).astype(
            sum_qkv.dtype
        ),
        lax.all_gather(sum_proj.astype(jnp.bfloat16), "dp", axis=1, tiled=True).astype(
            sum_proj.dtype
        ),
        lax.all_gather(sum_gate_up.astype(jnp.bfloat16), "dp", axis=0, tiled=True).astype(
            sum_gate_up.dtype
        ),
        lax.all_gather(sum_down.astype(jnp.bfloat16), "dp", axis=1, tiled=True).astype(
            sum_down.dtype
        ),
    )
    grad_ada, grad_bias_flat, grad_qkv, grad_proj, grad_gate_up, grad_down = reduced
    return (
        output,
        grad_latent,
        grad_cond,
        grad_ada,
        grad_bias_flat.reshape(6, -1),
        grad_qkv,
        grad_gains_total,
        grad_proj,
        grad_gate_up,
        grad_down,
    )


def solution(mesh):
    return jax.shard_map(
        local,
        mesh=mesh,
        in_specs=(
            P("dp", None, "mp"),
            P("dp", "mp"),
            P("dp", None, "mp"),
            P("dp"),
            P("dp"),
            P(None, None, "mp"),
            P(None, "mp"),
            P(None, None, "mp"),
            P(),
            P("mp", None),
            P(None, None, "mp"),
            P("mp", None),
        ),
        out_specs=(
            P("dp", None, "mp"),
            P("dp", None, "mp"),
            P("dp", "mp"),
            P(None, None, "mp"),
            P(None, "mp"),
            P(None, None, "mp"),
            P(),
            P("mp", None),
            P(None, None, "mp"),
            P("mp", None),
        ),
        check_vma=False,
    )
```

profile of v0, /device:TPU:0, one launch (start us, length us, event | category | flops | bytes accessed | tf_op | source)
XLA Modules:
  0.0 1399.9 jit_solution(6436843170089847557)
XLA Ops:
  10.1 13.1 all-reduce
  35.1 18.7 %psum.44 = f32[8]{0:T(128)S(1)} all-reduce(f32[8]{0:T(128)S(1)} %select_reduce_fusion.1), channel_id=1, replica_groups=mesh['dp'=8,'mp'=4] {'dp'}, use_global_device_ids=true, to_apply=%region_13.17 | all-reduce | flops 8 | bytes 64 | tf_op jit(solution)/shard_map/psum | solution.py:339
  109.3 22.1 %all-gather.12.cloned.1.call-done = bf16[4,256,1152]{1,2,0:T(8,128)(2,1)} async-done(((bf16[4,256,288]{1,2,0:T(8,128)(2,1)}), bf16[4,256,1152]{1,2,0:T(8,128)(2,1)}) %all-gather.12.cloned.1.call-update) | async-done | bytes 2359312 | tf_op jit(solution)/shard_map/all_gather | solution.py:60
  147.5 48.0 %reduce-scatter.13.cloned.1.call-done = f32[4,256,288]{1,2,0:T(8,128)} async-done(((f32[4,256,1152]{1,2,0:T(8,128)}), f32[4,256,288]{1,2,0:T(8,128)}) %reduce-scatter.13.cloned.1.call-update) | async-done | bytes 1179664 | tf_op jit(solution)/shard_map/reduce_scatter | solution.py:64
  209.2 25.2 %all-gather.14.cloned.1.call-done = bf16[4,256,1152]{1,2,0:T(8,128)(2,1)} async-done(((bf16[4,256,288]{1,2,0:T(8,128)(2,1)}), bf16[4,256,1152]{1,2,0:T(8,128)(2,1)}) %all-gather.14.cloned.1.call-update) | async-done | bytes 2359312 | tf_op jit(solution)/shard_map/all_gather | solution.py:60
  258.1 20.8 %collective-permute-done.3 = f32[4,256,288]{1,2,0:T(8,128)} collective-permute-done((f32[4,256,288]{1,2,0:T(8,128)}, f32[4,256,288]{1,2,0:T(8,128)}, u32[]{:S(2)}, u32[]{:S(2)}) %collective-permute-start.3) | collective-permute-done | bytes 1179680 | tf_op jit(solution)/shard_map/ppermute | solution.py:33
  279.0 18.6 %reduce-scatter.15.cloned.1.call-done = f32[4,256,288]{1,2,0:T(8,128)} async-done(((f32[4,256,1152]{1,2,0:T(8,128)}), f32[4,256,288]{1,2,0:T(8,128)}) %reduce-scatter.15.cloned.1.call-update) | async-done | bytes 1179664 | tf_op jit(solution)/shard_map/reduce_scatter | solution.py:64
  302.7 24.2 %all-gather.16.cloned.1.call-done = bf16[4,256,1152]{1,2,0:T(8,128)(2,1)} async-done(((bf16[4,256,288]{1,2,0:T(8,128)(2,1)}), bf16[4,256,1152]{1,2,0:T(8,128)(2,1)}) %all-gather.16.cloned.1.call-update) | async-done | bytes 2359312 | tf_op jit(solution)/shard_map/all_gather | solution.py:60
  341.4 48.0 %reduce-scatter.17.cloned.1.call-done = f32[4,256,288]{1,2,0:T(8,128)} async-done(((f32[4,256,1152]{1,2,0:T(8,128)}), f32[4,256,288]{1,2,0:T(8,128)}) %reduce-scatter.17.cloned.1.call-update) | async-done | bytes 1179664 | tf_op jit(solution)/shard_map/reduce_scatter | solution.py:64
  406.9 25.1 %all-gather.18.cloned.1.call-done = bf16[4,256,1152]{1,2,0:T(8,128)(2,1)} async-done(((bf16[4,256,288]{1,2,0:T(8,128)(2,1)}), bf16[4,256,1152]{1,2,0:T(8,128)(2,1)}) %all-gather.18.cloned.1.call-update) | async-done | bytes 2359312 | tf_op jit(solution)/shard_map/all_gather | solution.py:60
  478.1 21.8 %reduce-scatter.19.cloned.1.call-done = f32[4,256,288]{1,2,0:T(8,128)} async-done(((f32[4,256,1152]{1,2,0:T(8,128)}), f32[4,256,288]{1,2,0:T(8,128)}) %reduce-scatter.19.cloned.1.call-update) | async-done | bytes 1179664 | tf_op jit(solution)/shard_map/reduce_scatter | solution.py:64
  507.8 75.5 %reduce-scatter.29.cloned.1.call-done = f32[768,144]{0,1:T(8,128)} async-done(((f32[768,1152]{0,1:T(8,128)}), f32[768,144]{0,1:T(8,128)}) %reduce-scatter.29.cloned.1.call-update) | async-done | bytes 442384 | tf_op jit(solution)/shard_map/reduce_scatter | solution.py:302
  589.4 126.5 %reduce-scatter.27.cloned.1.call-done = f32[144,2,768]{2,0,1:T(8,128)} async-done(((f32[1152,2,768]{2,0,1:T(8,128)}), f32[144,2,768]{2,0,1:T(8,128)}) %reduce-scatter.27.cloned.1.call-update) | async-done | bytes 884752 | tf_op jit(solution)/shard_map/reduce_scatter | solution.py:301
  723.2 100.5 %reduce-scatter.23.cloned.1.call-done = f32[144,3,288]{2,0,1:T(8,128)} async-done(((f32[1152,3,288]{2,0,1:T(8,128)}), f32[144,3,288]{2,0,1:T(8,128)}) %reduce-scatter.23.cloned.1.call-update) | async-done | bytes 497680 | tf_op jit(solution)/shard_map/reduce_scatter | solution.py:299
  825.6 181.2 %reduce-scatter.21.cloned.1.call-done = f32[144,6,288]{2,0,1:T(8,128)} async-done(((f32[1152,6,288]{2,0,1:T(8,128)}), f32[144,6,288]{2,0,1:T(8,128)}) %reduce-scatter.21.cloned.1.call-update) | async-done | bytes 995344 | tf_op jit(solution)/shard_map/reduce_scatter | solution.py:297
  1030.9 26.6 %all-gather.26.cloned.1.call-done = bf16[768,1152]{0,1:T(8,128)(2,1)} async-done(((bf16[768,144]{0,1:T(8,128)(2,1)}), bf16[768,1152]{0,1:T(8,128)(2,1)}) %all-gather.26.cloned.1.call-update) | async-done | bytes 1769488 | tf_op jit(solution)/shard_map/all_gather | solution.py:407
  1061.5 40.4 %psum.47 = f32[2,72]{1,0:T(2,128)} all-reduce(f32[2,72]{1,0:T(2,128)S(1)} %pad_maximum_fusion.14), channel_id=1, replica_groups=mesh['dp'=8,'mp'=4] {'dp','mp'}, use_global_device_ids=true, to_apply=%region_37.43 | all-reduce | flops 144 | bytes 1152 | tf_op jit(solution)/shard_map/psum | solution.py:389
  1101.9 25.1 %reduce-scatter.25.cloned.1.call-done = f32[288,144]{0,1:T(8,128)} async-done(((f32[288,1152]{0,1:T(8,128)}), f32[288,144]{0,1:T(8,128)}) %reduce-scatter.25.cloned.1.call-update) | async-done | bytes 165904 | tf_op jit(solution)/shard_map/reduce_scatter | solution.py:300
  1138.0 56.5 %all_gather.49 = bf16[288,1152]{0,1:T(8,128)(2,1)S(1)} all-gather(bf16[288,144]{0,1:T(8,128)(2,1)S(1)} %copy-done.42), channel_id=1, replica_groups=mesh['dp'=8,'mp'=4] {'dp'}, dimensions={1}, use_global_device_ids=true | all-gather | bytes 746496 | tf_op jit(solution)/shard_map/all_gather | solution.py:401
  1195.9 19.8 %all-gather.24.cloned.1.call-done = bf16[1152,2,768]{2,0,1:T(8,128)(2,1)} async-done(((bf16[144,2,768]{2,0,1:T(8,128)(2,1)}), bf16[1152,2,768]{2,0,1:T(8,128)(2,1)}) %all-gather.24.cloned.1.call-update) | async-done | bytes 3538960 | tf_op jit(solution)/shard_map/all_gather | solution.py:404
  1215.7 17.3 %copy.106 = f32[1152,2,768]{2,1,0:T(2,128)} copy(bf16[1152,2,768]{2,0,1:T(8,128)(2,1)} %all-gather.24.cloned.1.call-done) | data formatting | bytes 10616832
  1241.9 22.9 %all-reduce.2 = bf16[1728]{0:T(1024)(128)(2,1)S(1)} all-reduce(f32[1728]{0:T(1024)S(1)} %reshape.470), channel_id=10, replica_groups=mesh['dp'=8,'mp'=4] {'dp'}, use_global_device_ids=true, to_apply=%region_33.39.clone | all-reduce | flops 1728 | bytes 10368
  1267.4 17.7 %all-reduce.1 = bf16[1728]{0:T(1024)(128)(2,1)S(1)} all-reduce(bf16[1728]{0:T(1024)(128)(2,1)S(1)} %dynamic-update-slice.1), channel_id=1, replica_groups=mesh['dp'=8,'mp'=4] {'dp'}, use_global_device_ids=true, to_apply=%add.1 | all-reduce | flops 1728 | bytes 6912
  1302.3 82.8 %all-gather.20.cloned.1.call-done = bf16[1152,6,288]{2,0,1:T(8,128)(2,1)} async-done(((bf16[144,6,288]{2,0,1:T(8,128)(2,1)}), bf16[1152,6,288]{2,0,1:T(8,128)(2,1)}) %all-gather.20.cloned.1.call-update) | async-done | bytes 3981328 | tf_op jit(solution)/shard_map/all_gather | solution.py:392
  (373 shorter events, 308.4 us)
Async XLA Ops:
  7.2 124.1 %all-gather.12.cloned.1.call-start = ((), (), s32[]{:S(2)}) async-start(), calls=%async_computation.10 | async-start | bytes 2949120 | tf_op jit(solution)/shard_map/all_gather | solution.py:60
  65.0 33.3 %collective-permute-start = (f32[4,256,288]{1,2,0:T(8,128)}, f32[4,256,288]{1,2,0:T(8,128)}, u32[]{:S(2)}, u32[]{:S(2)}) collective-permute-start(f32[4,256,288]{1,2,0:T(8,128)} %get-tuple-element.229), channel_id=1, source_target_pairs={{0,4},{4,8},{8,12},{12,16},{16,20},{20,24},{24,28},{1,5},{5,9},{9,... | collective-permute-start | bytes 3538952 | tf_op jit(solution)/shard_map/ppermute | solution.py:33
  68.5 17.9 %collective-permute-start.4 = (f32[4]{0:T(128)}, f32[4]{0:T(128)}, u32[]{:S(2)}, u32[]{:S(2)}) collective-permute-start(f32[4]{0:T(128)} %get-tuple-element.163), channel_id=1, source_target_pairs={{0,4},{4,8},{8,12},{12,16},{16,20},{20,24},{24,28},{1,5},{5,9},{9,... | collective-permute-start | bytes 56 | tf_op jit(solution)/shard_map/ppermute | solution.py:33
  108.2 87.2 %reduce-scatter.13.cloned.1.call-start = ((), (), s32[]{:S(2)}) async-start(), calls=%async_computation.11 | async-start | bytes 5898240 | tf_op jit(solution)/shard_map/reduce_scatter | solution.py:64
  147.4 87.0 %all-gather.14.cloned.1.call-start = ((), (), s32[]{:S(2)}) async-start(), calls=%async_computation.12 | async-start | bytes 2949120 | tf_op jit(solution)/shard_map/all_gather | solution.py:60
  209.2 88.4 %reduce-scatter.15.cloned.1.call-start = ((), (), s32[]{:S(2)}) async-start(), calls=%async_computation.13 | async-start | bytes 5898240 | tf_op jit(solution)/shard_map/reduce_scatter | solution.py:64
  249.6 77.3 %all-gather.16.cloned.1.call-start = ((), (), s32[]{:S(2)}) async-start(), calls=%async_computation.14 | async-start | bytes 2949120 | tf_op jit(solution)/shard_map/all_gather | solution.py:60
  249.7 29.3 %collective-permute-start.3 = (f32[4,256,288]{1,2,0:T(8,128)}, f32[4,256,288]{1,2,0:T(8,128)}, u32[]{:S(2)}, u32[]{:S(2)}) collective-permute-start(f32[4,256,288]{1,2,0:T(8,128)} %get-tuple-element.228), channel_id=1, source_target_pairs={{0,4},{4,8},{8,12},{12,16},{16,20},{20,24},{24,28},{1,5},{5,9},{9,... | collective-permute-start | bytes 3538952 | tf_op jit(solution)/shard_map/ppermute | solution.py:33
  302.7 86.7 %reduce-scatter.17.cloned.1.call-start = ((), (), s32[]{:S(2)}) async-start(), calls=%async_computation.15 | async-start | bytes 5898240 | tf_op jit(solution)/shard_map/reduce_scatter | solution.py:64
  341.4 90.7 %all-gather.18.cloned.1.call-start = ((), (), s32[]{:S(2)}) async-start(), calls=%async_computation.16 | async-start | bytes 2949120 | tf_op jit(solution)/shard_map/all_gather | solution.py:60
  406.7 93.2 %reduce-scatter.19.cloned.1.call-start = ((), (), s32[]{:S(2)}) async-start(), calls=%async_computation.17 | async-start | bytes 5898240 | tf_op jit(solution)/shard_map/reduce_scatter | solution.py:64
  451.9 131.4 %reduce-scatter.29.cloned.1.call-start = ((), (), s32[]{:S(2)}) async-start(), calls=%async_computation.25 | async-start | bytes 3981312 | tf_op jit(solution)/shard_map/reduce_scatter | solution.py:302
  458.0 257.9 %reduce-scatter.27.cloned.1.call-start = ((), (), s32[]{:S(2)}) async-start(), calls=%async_computation.23 | async-start | bytes 7962624 | tf_op jit(solution)/shard_map/reduce_scatter | solution.py:301
  468.7 355.0 %reduce-scatter.23.cloned.1.call-start = ((), (), s32[]{:S(2)}) async-start(), calls=%async_computation.20 | async-start | bytes 5971968 | tf_op jit(solution)/shard_map/reduce_scatter | solution.py:299
  478.0 528.8 %reduce-scatter.21.cloned.1.call-start = ((), (), s32[]{:S(2)}) async-start(), calls=%async_computation.18 | async-start | bytes 11943936 | tf_op jit(solution)/shard_map/reduce_scatter | solution.py:297
  507.7 549.8 %all-gather.26.cloned.1.call-start = ((), (), s32[]{:S(2)}) async-start(), calls=%async_computation.26 | async-start | bytes 1990656 | tf_op jit(solution)/shard_map/all_gather | solution.py:407
  585.0 542.0 %reduce-scatter.25.cloned.1.call-start = ((), (), s32[]{:S(2)}) async-start(), calls=%async_computation.22 | async-start | bytes 1990656 | tf_op jit(solution)/shard_map/reduce_scatter | solution.py:300
  589.4 626.4 %all-gather.24.cloned.1.call-start = ((), (), s32[]{:S(2)}) async-start(), calls=%async_computation.24 | async-start | bytes 3981312 | tf_op jit(solution)/shard_map/all_gather | solution.py:404
  717.9 521.7 %reduce-scatter.31.cloned.1.call-start = ((), (), s32[]{:S(2)}) async-start(), calls=%async_computation.27 | async-start | bytes 737280
  723.1 574.6 %all-gather.22.cloned.1.call-start = ((), (), s32[]{:S(2)}) async-start(), calls=%async_computation.21 | async-start | bytes 2985984 | tf_op jit(solution)/shard_map/all_gather | solution.py:398
  825.6 559.6 %all-gather.20.cloned.1.call-start = ((), (), s32[]{:S(2)}) async-start(), calls=%async_computation.19 | async-start | bytes 5971968 | tf_op jit(solution)/shard_map/all_gather | solution.py:392
  1009.1 19.4 %collective-permute-start.2 = (bf16[4,256,288]{1,2,0:T(8,128)(2,1)S(1)}, bf16[4,256,288]{1,2,0:T(8,128)(2,1)S(1)}, u32[]{:S(2)}, u32[]{:S(2)}) collective-permute-start(bf16[4,256,288]{1,2,0:T(8,128)(2,1)S(1)} %copy-done.35), channel_id=1, source_target_pairs={{4,0},{8,4},{12,8},{16,12},{20,16},{24,20},{28,24},{5,1},{9,5},{13... | collective-permute-start | bytes 1769480 | tf_op jit(solution)/shard_map/ppermute | solution.py:33
  1136.7 151.2 %collective-permute-start.5 = (bf16[4,256,288]{1,2,0:T(8,128)(2,1)}, bf16[4,256,288]{1,2,0:T(8,128)(2,1)S(1)}, u32[]{:S(2)}, u32[]{:S(2)}) collective-permute-start(bf16[4,256,288]{1,2,0:T(8,128)(2,1)} %get-tuple-element.159), channel_id=1, source_target_pairs={{4,0},{8,4},{12,8},{16,12},{20,16},{24,20},{28,24},{5,1},{9,5},{13... | collective-permute-start | bytes 1769480 | tf_op jit(solution)/shard_map/ppermute | solution.py:33
  1240.6 45.8 %collective-permute-start.6 = (bf16[4,288]{1,0:T(4,128)(2,1)S(1)}, bf16[4,288]{1,0:T(4,128)(2,1)S(1)}, u32[]{:S(2)}, u32[]{:S(2)}) collective-permute-start(bf16[4,288]{1,0:T(4,128)(2,1)S(1)} %get-tuple-element.153), channel_id=1, source_target_pairs={{4,0},{8,4},{12,8},{16,12},{20,16},{24,20},{28,24},{5,1},{9,5},{13... | collective-permute-start | bytes 6920 | tf_op jit(solution)/shard_map/ppermute | solution.py:33
  (91 other events, 1544.3 us)
Sparse Core Ops, SparseCore 0:
  108.3 22.9 all-gather.11
  147.6 47.8 reduce-scatter.12
  209.3 25.1 all-gather.13
  249.7 47.8 reduce-scatter.14
  302.8 24.0 all-gather.15
  341.5 47.8 reduce-scatter.16
  406.8 25.1 all-gather.17
  452.0 47.8 reduce-scatter.18
  504.1 79.1 reduce-scatter.28
  587.4 128.5 reduce-scatter.26
  720.5 103.1 reduce-scatter.22
  827.1 179.6 reduce-scatter.20
  1009.8 47.5 all-gather.25
  1061.8 65.1 reduce-scatter.24
  1129.6 86.0 all-gather.23
  1218.7 20.8 reduce-scatter.30
  1241.7 55.5 all-gather.21
  1299.4 85.7 all-gather.19
where the time goes:
time: 1410 us; the launch traced here: 1400 us
  waiting for transfers between devices  919 us (65%)
  blocking collectives  200 us (14%)
  matrix products  89.3 us (6%)
  local copies, waits for them, and re-layouts  80.8 us (6%)
  other arithmetic  70.3 us (5%)
  between operations  17.9 us (1%)
  starting transfers between devices  16.6 us (1%)
    reduce_scatter x1, waiting for transfers between devices, backward_block(): lax.psum_scatter(grad_ada, 'dp', scatter_dimension=0, tiled=True)  181 us
    reduce_scatter x4, waiting for transfers between devices, reduce_parts(): return lax.psum_scatter(tensor, 'mp', scatter_dimension=2, tiled=True)  136 us
    reduce_scatter x1, waiting for transfers between devices, backward_block(): lax.psum_scatter(mlp_sums[0], 'dp', scatter_dimension=0, tiled=True)  127 us
    reduce_scatter x1, waiting for transfers between devices, backward_block(): lax.psum_scatter(grad_qkv, 'dp', scatter_dimension=0, tiled=True)  101 us
    all_gather x4, waiting for transfers between devices, spread(): return lax.all_gather(tensor, 'mp', axis=2, tiled=True)  96.6 us
    all_gather x1, waiting for transfers between devices, local(): lax.all_gather(sum_ada.astype(jnp.bfloat16), 'dp', axis=0, tiled=True)  82.8 us
    reduce_scatter x1, waiting for transfers between devices, backward_block(): lax.psum_scatter(mlp_sums[1], 'dp', scatter_dimension=1, tiled=True)  75.5 us
    all_gather x1, blocking collectives, local(): lax.all_gather(sum_proj.astype(jnp.bfloat16), 'dp', axis=1, tiled=True)  56.5 us
  transfers between devices with their start and end apart: 25, of which 20 were waited for; matrix products, arithmetic and copies ran while one was open for 9% of the time, Pallas kernels for 0%

commit v1 on v0

v1 whole, which is shorter than its diff:
```python
import jax
import jax.numpy as jnp
from jax import lax
from jax.sharding import PartitionSpec as P

D = 1152
HEAD = 72
P_SIZE = 256
GRID = 16
IMG_DEV = 4
NBINS = 8

EPSILON = 1e-06
F32 = jnp.float32
BF16 = jnp.bfloat16


def exchange(value, axis, bit):
    pairs = [(i, i ^ bit) for i in range(lax.axis_size(axis))]
    return lax.ppermute(value, axis, pairs)


def shifted(value, axis, by):
    devices = lax.axis_size(axis)
    pairs = [(i, i + by) for i in range(devices) if 0 <= i + by < devices]
    return lax.ppermute(value, axis, pairs)


def bits_of(axis):
    bits, bit = [], 1
    while bit < lax.axis_size(axis):
        bits.append(bit)
        bit *= 2
    return bits


def has_bit(axis, bit):
    return (lax.axis_index(axis) & bit) != 0


def in_order(mine, other, later, axis, join):
    return jnp.where(later, join([other, mine], axis=axis), join([mine, other], axis=axis))


def gather_small(value, axis, dim):
    for bit in bits_of(axis):
        other = exchange(value, axis, bit)
        value = in_order(value, other, has_bit(axis, bit), dim, jnp.concatenate)
    return value


def sum_small(value, axis):
    for bit in bits_of(axis):
        value = value + exchange(value, axis, bit)
    return value


def spread(piece):
    pair = in_order(piece, exchange(piece, "mp", 2), has_bit("mp", 2), 1, jnp.stack)
    full = in_order(pair, exchange(pair, "mp", 1), has_bit("mp", 1), 2, jnp.stack)
    return full.reshape(piece.shape[0], -1, piece.shape[2])


def pick(value, index, dim):
    return lax.dynamic_index_in_dim(value, index, dim, keepdims=False)


def reduce_parts(partial):
    images, features, patches = partial.shape
    high = has_bit("mp", 2).astype(jnp.int32)
    low = has_bit("mp", 1).astype(jnp.int32)
    value = partial.reshape(images, 2, 2, features // 4, patches)
    received = exchange(pick(value, 1 - low, 2).astype(BF16), "mp", 1)
    value = pick(value, low, 2) + received.astype(F32)
    received = exchange(pick(value, 1 - high, 1).astype(BF16), "mp", 2)
    return pick(value, high, 1) + received.astype(F32)


def reduce_images(total, dim):
    steps = []
    for bit in bits_of("dp"):
        later = has_bit("dp", bit)
        rows = total.shape[dim]
        if rows % 2:
            total = total + exchange(total.astype(BF16), "dp", bit).astype(F32)
            continue
        halves = total.reshape(total.shape[:dim] + (2, rows // 2) + total.shape[dim + 1 :])
        index = later.astype(jnp.int32)
        received = exchange(pick(halves, 1 - index, dim).astype(BF16), "dp", bit)
        total = pick(halves, index, dim) + received.astype(F32)
        steps.append((bit, later))
    total = total.astype(BF16)
    for bit, later in reversed(steps):
        total = in_order(total, exchange(total, "dp", bit), later, dim, jnp.concatenate)
    return total.astype(F32)


def rope_tables():
    quarter = HEAD // 4
    frequency = 10000.0 ** (-jnp.arange(quarter, dtype=F32) / quarter)
    patches = jnp.arange(P_SIZE, dtype=jnp.int32)
    row_angle = (patches // GRID).astype(F32)[None, :] * frequency[:, None]
    col_angle = (patches % GRID).astype(F32)[None, :] * frequency[:, None]
    return (jnp.cos(row_angle), jnp.sin(row_angle), jnp.cos(col_angle), jnp.sin(col_angle))


def rotate(tensor, rotary_tables, direction):
    cos_row, sin_row, cos_col, sin_col = rotary_tables
    part_a, part_b, part_c, part_d = jnp.split(tensor, 4, axis=-2)
    return jnp.concatenate(
        [
            part_a * cos_row - direction * part_b * sin_row,
            part_b * cos_row + direction * part_a * sin_row,
            part_c * cos_col - direction * part_d * sin_col,
            part_d * cos_col + direction * part_c * sin_col,
        ],
        axis=-2,
    )


def inverse_rms(rows, dim):
    return lax.rsqrt(jnp.mean(rows * rows, axis=dim, keepdims=True) + EPSILON)


def einsum(spec, *operands):
    return jnp.einsum(spec, *operands, preferred_element_type=F32)


def local(
    latents,
    condition,
    cotangent,
    noise_bins,
    image_counts,
    ada_weight,
    ada_bias,
    qkv_weight,
    norm_gains,
    proj_weight,
    gate_up_weight,
    down_weight,
):
    slots = latents.shape[0]
    devices = lax.axis_size("dp")
    device = lax.axis_index("dp")
    part = lax.axis_index("mp")
    width = latents.shape[2]
    rows_in = latents.transpose(0, 2, 1)
    cot_in = cotangent.transpose(0, 2, 1)
    tables = rope_tables()
    gains = norm_gains.astype(F32)

    own_count = image_counts[0]
    last_slots = (own_count - IMG_DEV + jnp.arange(IMG_DEV)) % slots
    rows_came = shifted(jnp.take(rows_in, last_slots, axis=0).astype(BF16), "dp", 1)
    cot_came = shifted(jnp.take(cot_in, last_slots, axis=0).astype(BF16), "dp", 1)

    facts = jnp.zeros((1, width), F32)
    facts = facts.at[0, :slots].set(noise_bins.astype(F32)).at[0, slots].set(own_count.astype(F32))
    message = jnp.concatenate([jax.nn.silu(condition), facts]).astype(BF16)[None]
    message = gather_small(message, "dp", 0)
    facts = message[:, slots, : slots + 1].astype(jnp.int32)
    silu_all = gather_small(message[:, :slots], "mp", 2).reshape(devices * slots, -1)
    bins, counts = facts[:, :slots].reshape(-1), facts[:, slots]

    slot_ids = jnp.arange(devices * slots)
    live = (slot_ids % slots < counts[slot_ids // slots]).astype(F32)
    onehot = (bins[:, None] == jnp.arange(NBINS)[None, :]).astype(F32)
    histogram = jnp.sum(onehot * live[:, None], axis=0)
    bin_load = jnp.sum(onehot * histogram[None, :], axis=1)
    scaling = live * (IMG_DEV * devices) / (NBINS * (bin_load + 1.0 - live))

    ids = jnp.arange(devices)
    excess = jnp.cumsum(counts) - IMG_DEV * (ids + 1)
    came = jnp.concatenate([jnp.zeros((1,), excess.dtype), excess[:-1]])
    before = jnp.concatenate([jnp.zeros((1,), counts.dtype), counts[:-1]])
    places = jnp.arange(IMG_DEV)[None, :]
    from_before = places >= IMG_DEV - came[:, None]
    share_ids = jnp.where(
        from_before,
        (ids[:, None] - 1) * slots + (before[:, None] - IMG_DEV + places) % slots,
        ids[:, None] * slots + places,
    ).reshape(-1)
    silu_share = jnp.take(silu_all, share_ids, axis=0)
    silu_own = lax.dynamic_slice_in_dim(silu_share, device * IMG_DEV, IMG_DEV, 0)
    scale_share = jnp.take(scaling, share_ids)
    scale_own = lax.dynamic_slice_in_dim(scale_share, device * IMG_DEV, IMG_DEV, 0)
    came_here = pick(came, device, 0)
    mask = pick(from_before, device, 0)[:, None, None]

    modulation = einsum("bd,dkf->kbf", silu_own, ada_weight) + ada_bias.astype(F32)[:, None, :]
    everywhere = jnp.stack([modulation[0], modulation[1], modulation[3], modulation[4]])
    everywhere = gather_small(everywhere, "mp", 2)[..., None]
    shift_one_all, scale_one_all, shift_two_all, scale_two_all = everywhere
    modulation = modulation[..., None]
    shift_one, scale_one, gate_one, shift_two, scale_two, gate_two = modulation

    rows = jnp.where(mask, rows_came.astype(F32), rows_in[:IMG_DEV])
    rows_full = spread(jnp.where(mask, rows_came, rows_in[:IMG_DEV].astype(BF16))).astype(F32)
    inverse_one = inverse_rms(rows_full, 1)
    normed_full = rows_full * inverse_one
    attn_full = (normed_full * (1.0 + scale_one_all) + shift_one_all).astype(BF16)
    projected = einsum("dkf,bdp->bkfp", qkv_weight, attn_full)
    projected = projected.reshape(IMG_DEV, 3, -1, HEAD, P_SIZE)
    inverse_heads = inverse_rms(projected[:, :2], 3)
    hats = projected[:, :2] * inverse_heads
    gain_column = gains[None, :, None, :, None]
    rotated = rotate(hats * gain_column, tables, 1.0).astype(BF16)
    queries, keys = rotated[:, 0], rotated[:, 1]
    values = projected[:, 2].astype(BF16)
    scores = einsum("bheq,bhep->bhqp", keys, queries) * HEAD ** (-0.5)
    highest = jnp.max(scores, axis=2, keepdims=True)
    lse = highest + jnp.log(jnp.sum(jnp.exp(scores - highest), axis=2, keepdims=True))
    probability = jnp.exp(scores - lse)
    attention = probability.astype(BF16)
    heads_out = einsum("bheq,bhqp->bhep", values, attention).astype(BF16)
    heads_out = heads_out.reshape(IMG_DEV, -1, P_SIZE)
    branch_one = reduce_parts(einsum("ed,bep->bdp", proj_weight, heads_out))
    middle = rows + gate_one * branch_one

    middle_full = spread(middle.astype(BF16)).astype(F32)
    inverse_two = inverse_rms(middle_full, 1)
    normed_two_full = middle_full * inverse_two
    mlp_full = (normed_two_full * (1.0 + scale_two_all) + shift_two_all).astype(BF16)
    gate_up = einsum("dkf,bdp->kbfp", gate_up_weight, mlp_full)
    gate_part, up_part = gate_up
    sigmoid_gate = jax.nn.sigmoid(gate_part)
    silu_gate = gate_part * sigmoid_gate
    hidden = (silu_gate * up_part).astype(BF16)
    branch_two = reduce_parts(einsum("fd,bfp->bdp", down_weight, hidden))
    result = middle + gate_two * branch_two
    result_back = shifted(result.astype(BF16), "dp", -1)

    grad_out = jnp.where(mask, cot_came.astype(F32), cot_in[:IMG_DEV]) * scale_own[:, None, None]
    grad_gate_two = jnp.sum(grad_out * branch_two, axis=2)
    grad_branch_two = spread((grad_out * gate_two).astype(BF16))
    grad_down = reduce_images(einsum("bfp,bdp->fd", hidden, grad_branch_two), 0)
    grad_hidden = einsum("fd,bdp->bfp", down_weight, grad_branch_two)
    grad_gate = grad_hidden * up_part * sigmoid_gate * (1.0 + gate_part * (1.0 - sigmoid_gate))
    grad_up = grad_hidden * silu_gate
    grad_gu_rows = jnp.stack([grad_gate, grad_up]).astype(BF16)
    grad_gate_weight = reduce_images(einsum("bdp,bfp->df", mlp_full, grad_gu_rows[0]), 0)
    grad_up_weight = reduce_images(einsum("bdp,bfp->df", mlp_full, grad_gu_rows[1]), 0)
    grad_gate_up = jnp.stack([grad_gate_weight, grad_up_weight], axis=1)
    partial = einsum("dkf,kbfp->bdp", gate_up_weight, grad_gu_rows)
    inner = jnp.sum(partial * (1.0 + scale_two_all) * normed_two_full, axis=1, keepdims=True)
    inner = sum_small(inner, "mp") / D
    grad_mlp_in = reduce_parts(partial)
    normed_two = middle * inverse_two
    grad_shift_two = jnp.sum(grad_mlp_in, axis=2)
    grad_scale_two = jnp.sum(grad_mlp_in * normed_two, axis=2)
    grad_middle = grad_out + inverse_two * (grad_mlp_in * (1.0 + scale_two) - normed_two * inner)
    grad_gate_one = jnp.sum(grad_middle * branch_one, axis=2)
    grad_branch_one = spread((grad_middle * gate_one).astype(BF16))
    grad_proj = reduce_images(einsum("bep,bdp->ed", heads_out, grad_branch_one), 0)
    grad_heads = einsum("ed,bdp->bep", proj_weight, grad_branch_one).astype(BF16)
    grad_heads = grad_heads.reshape(IMG_DEV, -1, HEAD, P_SIZE)
    grad_attention = einsum("bheq,bhep->bhqp", values, grad_heads)
    grad_values = einsum("bhqp,bhep->bheq", attention, grad_heads)
    inner = jnp.sum(probability * grad_attention, axis=2, keepdims=True)
    grad_scores = (probability * (grad_attention - inner)).astype(BF16)
    score_scale = HEAD ** (-0.5)
    grad_rotated = jnp.stack(
        [
            einsum("bhqp,bheq->bhep", grad_scores, keys),
            einsum("bhqp,bhep->bheq", grad_scores, queries),
        ],
        axis=1,
    )
    grad_scaled = rotate(grad_rotated * score_scale, tables, -1.0)
    grad_gains = jnp.sum(grad_scaled * hats, axis=(0, 2, 4))
    grad_hats = grad_scaled * gain_column
    inner = jnp.mean(grad_hats * hats, axis=3, keepdims=True)
    grad_raw = inverse_heads * (grad_hats - hats * inner)
    grad_rows = jnp.concatenate([grad_raw, grad_values[:, None]], axis=1).astype(BF16)
    grad_rows = grad_rows.reshape(IMG_DEV, 3, -1, P_SIZE)
    grad_qkv = reduce_images(einsum("bkfp,bdp->kfd", grad_rows, attn_full), 1)
    partial = einsum("dkf,bkfp->bdp", qkv_weight, grad_rows)
    inner = jnp.sum(partial * (1.0 + scale_one_all) * normed_full, axis=1, keepdims=True)
    inner = sum_small(inner, "mp") / D
    grad_attn_in = reduce_parts(partial)
    normed_one = rows * inverse_one
    grad_shift_one = jnp.sum(grad_attn_in, axis=2)
    grad_scale_one = jnp.sum(grad_attn_in * normed_one, axis=2)
    grad_latent = grad_middle + inverse_one * (
        grad_attn_in * (1.0 + scale_one) - normed_one * inner
    )
    latent_back = shifted(grad_latent.astype(BF16), "dp", -1)

    grad_mod = jnp.stack(
        [
            grad_shift_one,
            grad_scale_one,
            grad_gate_one,
            grad_shift_two,
            grad_scale_two,
            grad_gate_two,
        ]
    ).astype(BF16)
    mod_share = gather_small(grad_mod, "dp", 1)
    grad_ada = einsum("kbf,bd->kfd", mod_share, silu_share)
    grad_bias = jnp.sum(mod_share.astype(F32), axis=1)
    grad_gains_total = sum_small(sum_small(grad_gains, "mp"), "dp")

    slot = jnp.arange(slots)
    stays = slot < IMG_DEV - came_here
    live_here = slot < own_count
    away_place = jnp.clip(slot - own_count + IMG_DEV, 0, IMG_DEV - 1)
    share_place = jnp.where(
        stays, device * IMG_DEV + slot, (device + 1) * IMG_DEV + away_place
    )
    share_place = jnp.clip(share_place, 0, devices * IMG_DEV - 1)
    mod_slots = jnp.take(mod_share, share_place, axis=1) * live_here.astype(BF16)[None, :, None]
    grad_silu = sum_small(einsum("kbf,dkf->bd", mod_slots, ada_weight), "mp")
    grad_silu = lax.dynamic_slice_in_dim(grad_silu, part * width, width, 1)
    sigmoid_cond = jax.nn.sigmoid(condition)
    grad_cond = grad_silu * sigmoid_cond * (1.0 + condition * (1.0 - sigmoid_cond))

    def home(here, back):
        kept = jnp.take(here, jnp.clip(slot, 0, IMG_DEV - 1), axis=0)
        away = jnp.take(back, away_place, axis=0).astype(F32)
        chosen = jnp.where(stays[:, None, None], kept, away)
        return jnp.where(live_here[:, None, None], chosen, 0.0).transpose(0, 2, 1)

    return (
        home(result, result_back),
        home(grad_latent, latent_back),
        grad_cond,
        grad_ada.transpose(2, 0, 1),
        grad_bias,
        grad_qkv.transpose(2, 0, 1),
        grad_gains_total,
        grad_proj,
        grad_gate_up,
        grad_down,
    )


def solution(mesh):
    return jax.shard_map(
        local,
        mesh=mesh,
        in_specs=(
            P("dp", None, "mp"),
            P("dp", "mp"),
            P("dp", None, "mp"),
            P("dp"),
            P("dp"),
            P(None, None, "mp"),
            P(None, "mp"),
            P(None, None, "mp"),
            P(),
            P("mp", None),
            P(None, None, "mp"),
            P("mp", None),
        ),
        out_specs=(
            P("dp", None, "mp"),
            P("dp", None, "mp"),
            P("dp", "mp"),
            P(None, None, "mp"),
            P(None, "mp"),
            P(None, None, "mp"),
            P(),
            P("mp", None),
            P(None, None, "mp"),
            P("mp", None),
        ),
        check_vma=False,
    )
```

time: 1410 us -> 634 us (0.45)
  waiting for transfers between devices: 919 us -> 246 us
  blocking collectives: 200 us -> 0 us
  starting transfers between devices: 16.6 us -> 86.6 us
  local copies, waits for them, and re-layouts: 80.8 us -> 119 us
  other arithmetic: 70.3 us -> 107 us
  matrix products: 89.3 us -> 64.9 us
    reduce_scatter x9 -> x0, waiting for transfers between devices: 645 us -> none  [the longest x1 181 us: backward_block(): lax.psum_scatter(grad_ada, 'dp', scatter_dimension=0, tiled=True)]
    all_gather x8 -> x0, waiting for transfers between devices: 226 us -> none  [the longest x4 96.6 us: spread(): return lax.all_gather(tensor, 'mp', axis=2, tiled=True)]
    ppermute x7 -> x71, waiting for transfers between devices: 41.7 us -> 246 us  [the longest x67 233 us: exchange(): return lax.ppermute(value, axis, pairs)]
    psum x6 -> x0, blocking collectives: 85 us -> none  [the longest x1 40.4 us: local(): grad_gains_total = lax.psum(grad_gains, ('dp', 'mp'))]
    ppermute x7 -> x71, starting transfers between devices: 15.4 us -> 86.6 us  [the longest x67 67.3 us: exchange(): return lax.ppermute(value, axis, pairs)]
    all_gather x2 -> x0, blocking collectives: 61.7 us -> none  [the longest x1 56.5 us: local(): lax.all_gather(sum_proj.astype(jnp.bfloat16), 'dp', axis=1, tiled=True)]
    unnamed x3 -> x0, blocking collectives: 53.6 us -> none
    convert_element_type x0 -> x26, local copies, waits for them, and re-layouts: none -> 33.5 us  [the longest x4 9.35 us: reduce_parts(): received = exchange(pick(value, 1 - low, 2).astype(BF16), 'mp', 1)]
  transfers between devices with their start and end apart: 25 -> 71, of which waited for: 20 -> 40; matrix products, arithmetic and copies ran while one was open for 9% -> 28% of each run, Pallas kernels for 0% -> 0%
where the time goes in v1:
time: 634 us; the launch traced here: 628 us
  waiting for transfers between devices  246 us (39%)
  local copies, waits for them, and re-layouts  119 us (19%)
  other arithmetic  107 us (17%)
  starting transfers between devices  86.6 us (14%)
  matrix products  64.9 us (10%)
    ppermute x67, waiting for transfers between devices, exchange(): return lax.ppermute(value, axis, pairs)  233 us
    ppermute x67, starting transfers between devices, exchange(): return lax.ppermute(value, axis, pairs)  67.3 us
    dot_general x22, matrix products, einsum(): return jnp.einsum(spec, *operands, preferred_element_type=F32)  64.9 us
    unnamed x159, local copies, waits for them, and re-layouts  24.4 us
    transpose x4, local copies, waits for them, and re-layouts, einsum(): return jnp.einsum(spec, *operands, preferred_element_type=F32)  24.3 us
    select_n x32, other arithmetic, in_order(): jnp.where(later, join([other, mine], axis=axis), join([mine, other], axis...  20.8 us
    ppermute x4, starting transfers between devices, shifted(): return lax.ppermute(value, axis, pairs)  19.3 us
    ppermute x4, waiting for transfers between devices, shifted(): return lax.ppermute(value, axis, pairs)  13.6 us
  transfers between devices with their start and end apart: 71, of which 40 were waited for; matrix products, arithmetic and copies ran while one was open for 28% of the time, Pallas kernels for 0%

profile of v1, /device:TPU:0, one launch (start us, length us, event | category | flops | bytes accessed | tf_op | source)
XLA Modules:
  0.0 628.5 jit_solution(17737613234888053014)
XLA Ops:
  49.6 9.4 %collective-permute-done.6 = bf16[4,288,256]{2,1,0:T(8,128)(2,1)S(1)} collective-permute-done((bf16[4,288,256]{2,1,0:T(8,128)(2,1)S(1)}, bf16[4,288,256]{2,1,0:T(8,128)(2,1)S(1)}, u32[]{:S(2)}, u32[]{:S(2)}) %collective-permute-start.6) | collective-permute-done | bytes 589856 | tf_op jit(solution)/shard_map/ppermute | solution.py:20
  100.4 14.5 %collective-permute-start.17 = (bf16[4,288,256]{2,1,0:T(8,128)(2,1)}, bf16[4,288,256]{2,1,0:T(8,128)(2,1)}, u32[]{:S(2)}, u32[]{:S(2)}) collective-permute-start(bf16[4,288,256]{2,1,0:T(8,128)(2,1)} %get-tuple-element.145), channel_id=1, source_target_pairs={{0,4},{4,8},{8,12},{12,16},{16,20},{20,24},{24,28},{1,5},{5,9},{9,... | collective-permute-start | bytes 1769480 | tf_op jit(solution)/shard_map/ppermute | solution.py:26
  127.6 7.6 %collective-permute-done.11 = bf16[4,288,256]{2,1,0:T(8,128)(2,1)} collective-permute-done((bf16[4,288,256]{2,1,0:T(8,128)(2,1)}, bf16[4,288,256]{2,1,0:T(8,128)(2,1)}, u32[]{:S(2)}, u32[]{:S(2)}) %collective-permute-start.11) | collective-permute-done | bytes 589856 | tf_op jit(solution)/shard_map/ppermute | solution.py:20
  145.7 10.5 %collective-permute-done.12 = bf16[4,288,256]{2,1,0:T(8,128)(2,1)} collective-permute-done((bf16[4,288,256]{2,1,0:T(8,128)(2,1)}, bf16[4,288,256]{2,1,0:T(8,128)(2,1)}, u32[]{:S(2)}, u32[]{:S(2)}) %collective-permute-start.12) | collective-permute-done | bytes 589856 | tf_op jit(solution)/shard_map/ppermute | solution.py:20
  160.5 6.7 %collective-permute-done.18 = bf16[4,288,256]{2,1,0:T(8,128)(2,1)} collective-permute-done((bf16[4,288,256]{2,1,0:T(8,128)(2,1)}, bf16[4,288,256]{2,1,0:T(8,128)(2,1)}, u32[]{:S(2)}, u32[]{:S(2)}) %collective-permute-start.18) | collective-permute-done | bytes 589856 | tf_op jit(solution)/shard_map/ppermute | solution.py:20
  190.7 7.4 %fusion.13 = f32[2,4,768,256]{2,3,0,1:T(8,128)S(1)} fusion(bf16[1152,2,768]{2,1,0:T(2,128)(2,1)} %param.32, f32[4,1152,256]{1,2,0:T(8,128)} %copy.157, f32[4,1152]{1,0:T(4,128)S(1)} %get-tuple-element.116, f32[4,1152]{1,0:T(4,128)S(1)} %get-tuple-element.117, f32[4,256]{1,0:T(4,128)S(1)} %add_rsqrt_fusion.1), kind=kOutput, calls=%fused_computation.49 | convolution fusion | flops 3628597248 | bytes 14589952 | tf_op jit(solution)/shard_map/dkf,bdp->kbfp/dot_general | solution.py:126
  245.1 6.2 copy.160
  255.0 6.2 collective-permute-done.65
  265.0 15.2 %collective-permute-done.59 = bf16[576,768]{1,0:T(8,128)(2,1)} collective-permute-done((bf16[576,768]{1,0:T(8,128)(2,1)}, bf16[576,768]{1,0:T(8,128)(2,1)}, u32[]{:S(2)}, u32[]{:S(2)}) %collective-permute-start.59) | collective-permute-done | bytes 884768 | tf_op jit(solution)/shard_map/ppermute | solution.py:20
  283.4 15.3 %collective-permute-done.53 = bf16[576,768]{1,0:T(8,128)(2,1)} collective-permute-done((bf16[576,768]{1,0:T(8,128)(2,1)}, bf16[576,768]{1,0:T(8,128)(2,1)}, u32[]{:S(2)}, u32[]{:S(2)}) %collective-permute-start.53) | collective-permute-done | bytes 884768 | tf_op jit(solution)/shard_map/ppermute | solution.py:20
  317.4 15.5 %collective-permute-done.67 = bf16[96,1152]{1,0:T(8,128)(2,1)S(1)} collective-permute-done((bf16[96,1152]{1,0:T(8,128)(2,1)S(1)}, bf16[96,1152]{1,0:T(8,128)(2,1)S(1)}, u32[]{:S(2)}, u32[]{:S(2)}) %collective-permute-start.67) | collective-permute-done | bytes 221216 | tf_op jit(solution)/shard_map/ppermute | solution.py:20
  333.1 9.4 %collective-permute-done.61 = bf16[144,768]{1,0:T(8,128)(2,1)S(1)} collective-permute-done((bf16[144,768]{1,0:T(8,128)(2,1)S(1)}, bf16[144,768]{1,0:T(8,128)(2,1)S(1)}, u32[]{:S(2)}, u32[]{:S(2)}) %collective-permute-start.61) | collective-permute-done | bytes 221216 | tf_op jit(solution)/shard_map/ppermute | solution.py:20
  342.5 9.4 %collective-permute-done.55 = bf16[144,768]{1,0:T(8,128)(2,1)S(1)} collective-permute-done((bf16[144,768]{1,0:T(8,128)(2,1)S(1)}, bf16[144,768]{1,0:T(8,128)(2,1)S(1)}, u32[]{:S(2)}, u32[]{:S(2)}) %collective-permute-start.55) | collective-permute-done | bytes 221216 | tf_op jit(solution)/shard_map/ppermute | solution.py:20
  354.8 9.1 %collective-permute-done.62 = bf16[144,768]{1,0:T(8,128)(2,1)S(1)} collective-permute-done((bf16[144,768]{1,0:T(8,128)(2,1)S(1)}, bf16[144,768]{1,0:T(8,128)(2,1)S(1)}, u32[]{:S(2)}, u32[]{:S(2)}) %collective-permute-start.62) | collective-permute-done | bytes 221216 | tf_op jit(solution)/shard_map/ppermute | solution.py:20
  370.6 6.6 %collective-permute-done.63 = bf16[288,768]{1,0:T(8,128)(2,1)S(1)} collective-permute-done((bf16[288,768]{1,0:T(8,128)(2,1)S(1)}, bf16[288,768]{1,0:T(8,128)(2,1)S(1)}, u32[]{:S(2)}, u32[]{:S(2)}) %collective-permute-start.63) | collective-permute-done | bytes 442400 | tf_op jit(solution)/shard_map/ppermute | solution.py:20
  378.6 8.0 %collective-permute-done.57 = bf16[288,768]{1,0:T(8,128)(2,1)S(1)} collective-permute-done((bf16[288,768]{1,0:T(8,128)(2,1)S(1)}, bf16[288,768]{1,0:T(8,128)(2,1)S(1)}, u32[]{:S(2)}, u32[]{:S(2)}) %collective-permute-start.57) | collective-permute-done | bytes 442400 | tf_op jit(solution)/shard_map/ppermute | solution.py:20
  400.9 18.1 %collective-permute-done.58 = bf16[576,768]{1,0:T(8,128)(2,1)S(1)} collective-permute-done((bf16[576,768]{1,0:T(8,128)(2,1)S(1)}, bf16[576,768]{1,0:T(8,128)(2,1)S(1)}, u32[]{:S(2)}, u32[]{:S(2)}) %collective-permute-start.58) | collective-permute-done | bytes 884768 | tf_op jit(solution)/shard_map/ppermute | solution.py:20
  420.4 12.5 %copy.190 = f32[1152,2,768]{2,1,0:T(2,128)} copy(f32[1152,2,768]{2,0,1:T(8,128)S(1)} %maximum_convert_fusion) | data formatting | bytes 14155776
  511.7 6.7 %collective-permute-done.37 = bf16[3,72,1152]{2,1,0:T(8,128)(2,1)S(1)} collective-permute-done((bf16[3,72,1152]{2,1,0:T(8,128)(2,1)S(1)}, bf16[3,72,1152]{2,1,0:T(8,128)(2,1)S(1)}, u32[]{:S(2)}, u32[]{:S(2)}) %collective-permute-start.37) | collective-permute-done | bytes 497696 | tf_op jit(solution)/shard_map/ppermute | solution.py:20
  542.1 6.3 %collective-permute-done.38 = bf16[3,36,1152]{2,1,0:T(8,128)(2,1)S(1)} collective-permute-done((bf16[3,36,1152]{2,1,0:T(8,128)(2,1)S(1)}, bf16[3,36,1152]{2,1,0:T(8,128)(2,1)S(1)}, u32[]{:S(2)}, u32[]{:S(2)}) %collective-permute-start.38) | collective-permute-done | bytes 248864 | tf_op jit(solution)/shard_map/ppermute | solution.py:20
  549.7 6.8 %collective-permute-done.33 = bf16[6,16,288]{2,0,1:T(8,128)(2,1)S(1)} collective-permute-done((bf16[6,16,288]{2,0,1:T(8,128)(2,1)S(1)}, bf16[6,16,288]{2,0,1:T(8,128)(2,1)S(1)}, u32[]{:S(2)}, u32[]{:S(2)}) %collective-permute-start.33) | collective-permute-done | bytes 55328 | tf_op jit(solution)/shard_map/ppermute | solution.py:20
  591.8 7.5 %collective-permute-done.16 = bf16[4,288,256]{2,1,0:T(8,128)(2,1)} collective-permute-done((bf16[4,288,256]{2,1,0:T(8,128)(2,1)}, bf16[4,288,256]{2,1,0:T(8,128)(2,1)}, u32[]{:S(2)}, u32[]{:S(2)}) %collective-permute-start.16) | collective-permute-done | bytes 589856 | tf_op jit(solution)/shard_map/ppermute | solution.py:26
  602.2 6.4 %fusion.23 = (f32[8,256,288]{1,2,0:T(8,128)}, f32[8,256,288]{1,2,0:T(8,128)}) fusion(f32[8,288,256]{2,1,0:T(8,128)} %gather_fusion.7, bf16[8,288,256]{2,1,0:T(8,128)(2,1)S(1)} %gather_fusion.8, pred[8]{0:T(512)(128)(4,1)S(1)} %copy-done.59, pred[8]{0:T(512)(128)(4,1)S(1)} %copy-done.60, pred[8]{0:T(512)(128)(4,1)S(1)} %copy-done.61, ...), kind=kLoop, calls=%fused_computation.71 | loop fusion | flops 5898240 | bytes 11796512 | tf_op jit(solution)/shard_map/transpose | solution.py:323
  608.6 14.9 %collective-permute-done.41 = bf16[3,144,1152]{2,1,0:T(8,128)(2,1)} collective-permute-done((bf16[3,144,1152]{2,1,0:T(8,128)(2,1)}, bf16[3,144,1152]{2,1,0:T(8,128)(2,1)}, u32[]{:S(2)}, u32[]{:S(2)}) %collective-permute-start.41) | collective-permute-done | bytes 995360 | tf_op jit(solution)/shard_map/ppermute | solution.py:20
  (525 shorter events, 388.0 us)
Async XLA Ops:
  17.0 25.5 %collective-permute-start.3 = (bf16[4,288,256]{2,1,0:T(8,128)(2,1)}, bf16[4,288,256]{2,1,0:T(8,128)(2,1)S(1)}, u32[]{:S(2)}, u32[]{:S(2)}) collective-permute-start(bf16[4,288,256]{2,1,0:T(8,128)(2,1)} %get-tuple-element.146), channel_id=1, source_target_pairs={{0,4},{4,8},{8,12},{12,16},{16,20},{20,24},{24,28},{1,5},{5,9},{9,... | collective-permute-start | bytes 1769480 | tf_op jit(solution)/shard_map/ppermute | solution.py:26
  100.4 27.2 %collective-permute-start.17 = (bf16[4,288,256]{2,1,0:T(8,128)(2,1)}, bf16[4,288,256]{2,1,0:T(8,128)(2,1)}, u32[]{:S(2)}, u32[]{:S(2)}) collective-permute-start(bf16[4,288,256]{2,1,0:T(8,128)(2,1)} %get-tuple-element.145), channel_id=1, source_target_pairs={{0,4},{4,8},{8,12},{12,16},{16,20},{20,24},{24,28},{1,5},{5,9},{9,... | collective-permute-start | bytes 1769480 | tf_op jit(solution)/shard_map/ppermute | solution.py:26
  240.7 61.1 %collective-permute-start.20 = (bf16[4,2,288,256]{3,2,0,1:T(8,128)(2,1)S(1)}, bf16[4,2,288,256]{3,2,0,1:T(8,128)(2,1)}, u32[]{:S(2)}, u32[]{:S(2)}) collective-permute-start(bf16[4,2,288,256]{3,2,0,1:T(8,128)(2,1)S(1)} %fusion.44), channel_id=1, source_target_pairs={{0,1},{1,0},{2,3},{3,2},{4,5},{5,4},{6,7},{7,6},{8,9},{9,8},{10,11... | collective-permute-start | bytes 3538952 | tf_op jit(solution)/shard_map/ppermute | solution.py:20
  243.1 37.1 %collective-permute-start.59 = (bf16[576,768]{1,0:T(8,128)(2,1)}, bf16[576,768]{1,0:T(8,128)(2,1)}, u32[]{:S(2)}, u32[]{:S(2)}) collective-permute-start(bf16[576,768]{1,0:T(8,128)(2,1)} %fusion.50), channel_id=1, source_target_pairs={{0,4},{4,0},{8,12},{12,8},{16,20},{20,16},{24,28},{28,24},{1,5},{5... | collective-permute-start | bytes 2654216 | tf_op jit(solution)/shard_map/ppermute | solution.py:20
  244.8 53.8 %collective-permute-start.53 = (bf16[576,768]{1,0:T(8,128)(2,1)}, bf16[576,768]{1,0:T(8,128)(2,1)}, u32[]{:S(2)}, u32[]{:S(2)}) collective-permute-start(bf16[576,768]{1,0:T(8,128)(2,1)} %fusion.49), channel_id=1, source_target_pairs={{0,4},{4,0},{8,12},{12,8},{16,20},{20,16},{24,28},{28,24},{1,5},{5... | collective-permute-start | bytes 2654216 | tf_op jit(solution)/shard_map/ppermute | solution.py:20
  255.0 50.0 %collective-permute-start.14 = (bf16[4,2,288,256]{3,2,0,1:T(8,128)(2,1)S(1)}, bf16[4,2,288,256]{3,2,0,1:T(8,128)(2,1)S(1)}, u32[]{:S(2)}, u32[]{:S(2)}) collective-permute-start(bf16[4,2,288,256]{3,2,0,1:T(8,128)(2,1)S(1)} %fusion.43), channel_id=1, source_target_pairs={{0,1},{1,0},{2,3},{3,2},{4,5},{5,4},{6,7},{7,6},{8,9},{9,8},{10,11... | collective-permute-start | bytes 3538952 | tf_op jit(solution)/shard_map/ppermute | solution.py:20
  263.3 43.6 %collective-permute-start.66 = (bf16[192,1152]{1,0:T(8,128)(2,1)S(1)}, bf16[192,1152]{1,0:T(8,128)(2,1)S(1)}, u32[]{:S(2)}, u32[]{:S(2)}) collective-permute-start(bf16[192,1152]{1,0:T(8,128)(2,1)S(1)} %fusion.66), channel_id=1, source_target_pairs={{0,8},{4,12},{8,0},{12,4},{16,24},{20,28},{24,16},{28,20},{1,9},{5... | collective-permute-start | bytes 1327112 | tf_op jit(solution)/shard_map/ppermute | solution.py:20
  281.7 27.9 %collective-permute-start.60 = (bf16[288,768]{1,0:T(8,128)(2,1)S(1)}, bf16[288,768]{1,0:T(8,128)(2,1)S(1)}, u32[]{:S(2)}, u32[]{:S(2)}) collective-permute-start(bf16[288,768]{1,0:T(8,128)(2,1)S(1)} %fusion.65), channel_id=1, source_target_pairs={{0,8},{4,12},{8,0},{12,4},{16,24},{20,28},{24,16},{28,20},{1,9},{5... | collective-permute-start | bytes 1327112 | tf_op jit(solution)/shard_map/ppermute | solution.py:20
  303.4 48.6 %collective-permute-start.21 = (bf16[4,288,256]{2,1,0:T(8,128)(2,1)S(1)}, bf16[4,288,256]{2,1,0:T(8,128)(2,1)S(1)}, u32[]{:S(2)}, u32[]{:S(2)}) collective-permute-start(bf16[4,288,256]{2,1,0:T(8,128)(2,1)S(1)} %fusion.58), channel_id=1, source_target_pairs={{0,2},{1,3},{2,0},{3,1},{4,6},{5,7},{6,4},{7,5},{8,10},{9,11},{10,... | collective-permute-start | bytes 1769480 | tf_op jit(solution)/shard_map/ppermute | solution.py:20
  306.4 215.4 %collective-permute-start.15 = (bf16[4,288,256]{2,1,0:T(8,128)(2,1)}, bf16[4,288,256]{2,1,0:T(8,128)(2,1)}, u32[]{:S(2)}, u32[]{:S(2)}) collective-permute-start(bf16[4,288,256]{2,1,0:T(8,128)(2,1)} %fusion.57), channel_id=1, source_target_pairs={{0,2},{1,3},{2,0},{3,1},{4,6},{5,7},{6,4},{7,5},{8,10},{9,11},{10,... | collective-permute-start | bytes 1769480 | tf_op jit(solution)/shard_map/ppermute | solution.py:20
  307.0 25.9 %collective-permute-start.67 = (bf16[96,1152]{1,0:T(8,128)(2,1)S(1)}, bf16[96,1152]{1,0:T(8,128)(2,1)S(1)}, u32[]{:S(2)}, u32[]{:S(2)}) collective-permute-start(bf16[96,1152]{1,0:T(8,128)(2,1)S(1)} %fusion.82), channel_id=1, source_target_pairs={{0,16},{4,20},{8,24},{12,28},{16,0},{20,4},{24,8},{28,12},{1,17},{... | collective-permute-start | bytes 663560 | tf_op jit(solution)/shard_map/ppermute | solution.py:20
  309.8 32.6 %collective-permute-start.61 = (bf16[144,768]{1,0:T(8,128)(2,1)S(1)}, bf16[144,768]{1,0:T(8,128)(2,1)S(1)}, u32[]{:S(2)}, u32[]{:S(2)}) collective-permute-start(bf16[144,768]{1,0:T(8,128)(2,1)S(1)} %fusion.81), channel_id=1, source_target_pairs={{0,16},{4,20},{8,24},{12,28},{16,0},{20,4},{24,8},{28,12},{1,17},{... | collective-permute-start | bytes 663560 | tf_op jit(solution)/shard_map/ppermute | solution.py:20
  316.5 35.4 %collective-permute-start.55 = (bf16[144,768]{1,0:T(8,128)(2,1)S(1)}, bf16[144,768]{1,0:T(8,128)(2,1)S(1)}, u32[]{:S(2)}, u32[]{:S(2)}) collective-permute-start(bf16[144,768]{1,0:T(8,128)(2,1)S(1)} %fusion.80), channel_id=1, source_target_pairs={{0,16},{4,20},{8,24},{12,28},{16,0},{20,4},{24,8},{28,12},{1,17},{... | collective-permute-start | bytes 663560 | tf_op jit(solution)/shard_map/ppermute | solution.py:20
  333.0 35.4 %collective-permute-start.68 = (bf16[96,1152]{1,0:T(8,128)(2,1)S(1)}, bf16[96,1152]{1,0:T(8,128)(2,1)S(1)}, u32[]{:S(2)}, u32[]{:S(2)}) collective-permute-start(bf16[96,1152]{1,0:T(8,128)(2,1)S(1)} %fusion.67), channel_id=1, source_target_pairs={{0,16},{4,20},{8,24},{12,28},{16,0},{20,4},{24,8},{28,12},{1,17},{... | collective-permute-start | bytes 663560 | tf_op jit(solution)/shard_map/ppermute | solution.py:20
  366.9 29.3 %collective-permute-start.24 = (bf16[4,288,256]{2,1,0:T(8,128)(2,1)S(1)}, bf16[4,288,256]{2,1,0:T(8,128)(2,1)S(1)}, u32[]{:S(2)}, u32[]{:S(2)}) collective-permute-start(bf16[4,288,256]{2,1,0:T(8,128)(2,1)S(1)} %multiply_convert_fusion.3), channel_id=1, source_target_pairs={{0,2},{1,3},{2,0},{3,1},{4,6},{5,7},{6,4},{7,5},{8,10},{9,11},{10,... | collective-permute-start | bytes 1769480 | tf_op jit(solution)/shard_map/ppermute | solution.py:20
  368.5 26.3 %collective-permute-start.69 = (bf16[192,1152]{1,0:T(8,128)(2,1)S(1)}, bf16[192,1152]{1,0:T(8,128)(2,1)S(1)}, u32[]{:S(2)}, u32[]{:S(2)}) collective-permute-start(bf16[192,1152]{1,0:T(8,128)(2,1)S(1)} %maximum_select_fusion.23), channel_id=1, source_target_pairs={{0,8},{4,12},{8,0},{12,4},{16,24},{20,28},{24,16},{28,20},{1,9},{5... | collective-permute-start | bytes 1327112 | tf_op jit(solution)/shard_map/ppermute | solution.py:20
  387.0 32.1 %collective-permute-start.58 = (bf16[576,768]{1,0:T(8,128)(2,1)S(1)}, bf16[576,768]{1,0:T(8,128)(2,1)S(1)}, u32[]{:S(2)}, u32[]{:S(2)}) collective-permute-start(bf16[576,768]{1,0:T(8,128)(2,1)S(1)} %maximum_select_fusion.16), channel_id=1, source_target_pairs={{0,4},{4,0},{8,12},{12,8},{16,20},{20,16},{24,28},{28,24},{1,5},{5... | collective-permute-start | bytes 2654216 | tf_op jit(solution)/shard_map/ppermute | solution.py:20
  395.0 39.4 %collective-permute-start.70 = (bf16[384,1152]{1,0:T(8,128)(2,1)S(1)}, bf16[384,1152]{1,0:T(8,128)(2,1)S(1)}, u32[]{:S(2)}, u32[]{:S(2)}) collective-permute-start(bf16[384,1152]{1,0:T(8,128)(2,1)S(1)} %maximum_select_fusion.18), channel_id=1, source_target_pairs={{0,4},{4,0},{8,12},{12,8},{16,20},{20,16},{24,28},{28,24},{1,5},{5... | collective-permute-start | bytes 2654216 | tf_op jit(solution)/shard_map/ppermute | solution.py:20
  396.4 40.2 %collective-permute-start.25 = (bf16[4,2,288,256]{3,2,0,1:T(8,128)(2,1)S(1)}, bf16[4,2,288,256]{3,2,0,1:T(8,128)(2,1)S(1)}, u32[]{:S(2)}, u32[]{:S(2)}) collective-permute-start(bf16[4,2,288,256]{3,2,0,1:T(8,128)(2,1)S(1)} %maximum_select_fusion.14), channel_id=1, source_target_pairs={{0,1},{1,0},{2,3},{3,2},{4,5},{5,4},{6,7},{7,6},{8,9},{9,8},{10,11... | collective-permute-start | bytes 3538952 | tf_op jit(solution)/shard_map/ppermute | solution.py:20
  446.7 36.3 %collective-permute-start.47 = (bf16[144,1152]{1,0:T(8,128)(2,1)S(1)}, bf16[144,1152]{1,0:T(8,128)(2,1)}, u32[]{:S(2)}, u32[]{:S(2)}) collective-permute-start(bf16[144,1152]{1,0:T(8,128)(2,1)S(1)} %fusion.70), channel_id=1, source_target_pairs={{0,4},{4,0},{8,12},{12,8},{16,20},{20,16},{24,28},{28,24},{1,5},{5... | collective-permute-start | bytes 995336 | tf_op jit(solution)/shard_map/ppermute | solution.py:20
  475.4 25.6 %collective-permute-start.36 = (bf16[3,144,1152]{2,1,0:T(8,128)(2,1)}, bf16[3,144,1152]{2,1,0:T(8,128)(2,1)}, u32[]{:S(2)}, u32[]{:S(2)}) collective-permute-start(bf16[3,144,1152]{2,1,0:T(8,128)(2,1)} %fusion.48), channel_id=1, source_target_pairs={{0,4},{4,0},{8,12},{12,8},{16,20},{20,16},{24,28},{28,24},{1,5},{5... | collective-permute-start | bytes 2985992 | tf_op jit(solution)/shard_map/ppermute | solution.py:20
  534.8 32.4 %collective-permute-start.52 = (bf16[144,1152]{1,0:T(8,128)(2,1)S(1)}, bf16[144,1152]{1,0:T(8,128)(2,1)S(1)}, u32[]{:S(2)}, u32[]{:S(2)}) collective-permute-start(bf16[144,1152]{1,0:T(8,128)(2,1)S(1)} %maximum_select_fusion.24), channel_id=1, source_target_pairs={{0,4},{4,0},{8,12},{12,8},{16,20},{20,16},{24,28},{28,24},{1,5},{5... | collective-permute-start | bytes 995336 | tf_op jit(solution)/shard_map/ppermute | solution.py:20
  569.7 29.7 %collective-permute-start.16 = (bf16[4,288,256]{2,1,0:T(8,128)(2,1)}, bf16[4,288,256]{2,1,0:T(8,128)(2,1)}, u32[]{:S(2)}, u32[]{:S(2)}) collective-permute-start(bf16[4,288,256]{2,1,0:T(8,128)(2,1)} %get-tuple-element.97), channel_id=1, source_target_pairs={{4,0},{8,4},{12,8},{16,12},{20,16},{24,20},{28,24},{5,1},{9,5},{13... | collective-permute-start | bytes 1769480 | tf_op jit(solution)/shard_map/ppermute | solution.py:26
  581.6 41.9 %collective-permute-start.41 = (bf16[3,144,1152]{2,1,0:T(8,128)(2,1)}, bf16[3,144,1152]{2,1,0:T(8,128)(2,1)}, u32[]{:S(2)}, u32[]{:S(2)}) collective-permute-start(bf16[3,144,1152]{2,1,0:T(8,128)(2,1)} %maximum_select_fusion.15), channel_id=1, source_target_pairs={{0,4},{4,0},{8,12},{12,8},{16,20},{20,16},{24,28},{28,24},{1,5},{5... | collective-permute-start | bytes 2985992 | tf_op jit(solution)/shard_map/ppermute | solution.py:20
  (126 other events, 1978.2 us)

commit v2 on v1

v2 whole, which is shorter than its diff:
```python
import functools
import types

import jax
import jax.numpy as jnp
import numpy as np
from jax import lax
from jax.experimental import pallas as pl
from jax.experimental.pallas import tpu as pltpu
from jax.sharding import PartitionSpec as P

HEAD = 72
P_SIZE = 256
GRID = 16
IMG_DEV = 4
NBINS = 8

EPSILON = 1e-06
F32 = jnp.float32
BF16 = jnp.bfloat16
MIB = 1 << 20
WEIGHT = 0.1 * 1e9


def exchange(value, axis, bit):
    pairs = [(i, i ^ bit) for i in range(lax.axis_size(axis))]
    return lax.ppermute(value, axis, pairs)


def shifted(value, axis, by):
    devices = lax.axis_size(axis)
    pairs = [(i, i + by) for i in range(devices) if 0 <= i + by < devices]
    return lax.ppermute(value, axis, pairs)


def bits_of(axis):
    bits, bit = [], 1
    while bit < lax.axis_size(axis):
        bits.append(bit)
        bit *= 2
    return bits


def has_bit(axis, bit):
    return (lax.axis_index(axis) & bit) != 0


def in_order(mine, other, later, axis, join):
    return jnp.where(later, join([other, mine], axis=axis), join([mine, other], axis=axis))


def gather_small(value, axis, dim):
    for bit in bits_of(axis):
        other = exchange(value, axis, bit)
        value = in_order(value, other, has_bit(axis, bit), dim, jnp.concatenate)
    return value


def sum_small(value, axis):
    for bit in bits_of(axis):
        value = value + exchange(value, axis, bit)
    return value


def pick(value, index, dim):
    return lax.dynamic_index_in_dim(value, index, dim, keepdims=False)


def spread(piece):
    core = exchange(piece, "mp", 1)
    over = exchange(piece, "mp", 2)
    both = exchange(over, "mp", 1)
    return [piece, core, over, both]


def call(kernel, grid, scalars, ins, outs, scratch=(), vmem=48, us=3.0):
    in_specs = [
        pl.BlockSpec(block, index, pipeline_mode=pl.Buffered(1)) if whole else pl.BlockSpec(block, index)
        for _, block, index, whole in ins
    ]
    return pl.pallas_call(
        kernel,
        grid_spec=pltpu.PrefetchScalarGridSpec(
            num_scalar_prefetch=1,
            grid=grid,
            in_specs=in_specs,
            out_specs=[pl.BlockSpec(block, index) for _, _, block, index in outs],
            scratch_shapes=list(scratch),
        ),
        out_shape=[jax.ShapeDtypeStruct(shape, kind) for shape, kind, _, _ in outs],
        compiler_params=pltpu.CompilerParams(
            dimension_semantics=("arbitrary",) * len(grid), vmem_limit_bytes=vmem * MIB
        ),
        cost_estimate=pl.CostEstimate(flops=int(us * WEIGHT), bytes_accessed=1000, transcendentals=0),
    )(scalars, *(a for a, _, _, _ in ins))


def by_image(array):
    rest = array.shape[1:]
    return (array, (1,) + rest, lambda i, s: (i,) + (0,) * len(rest), False)


def entire(array):
    return (array, array.shape, lambda i, s: (0,) * array.ndim, True)


def image_out(images, rest, kind):
    return ((images,) + rest, kind, (1,) + rest, lambda i, s: (i,) + (0,) * len(rest))


def flat_out(images, rows):
    return ((rows, images * P_SIZE), BF16, (rows, P_SIZE), lambda i, s: (0, i))


def dot(a, b, over=(1, 0)):
    return lax.dot_general(a, b, (((over[0],), (over[1],)), ((), ())), preferred_element_type=F32)


def span(me, relative, width):
    return pl.ds(pl.multiple_of((me ^ relative) * width, 32), width)


def assemble(pieces, full, me):
    width = pieces[0].shape[1]
    for relative, piece in enumerate(pieces):
        full[span(me, relative, width), :] = piece[0]


def inverse_rms(rows):
    return lax.rsqrt(jnp.mean(rows * rows, axis=0, keepdims=True) + EPSILON)


def swap_quarters(v):
    rows = lax.broadcasted_iota(jnp.int32, v.shape, 0)
    quarter = HEAD // 4
    first = (rows % (2 * quarter)) < quarter
    return jnp.where(first, pltpu.roll(v, HEAD - quarter, 0), pltpu.roll(v, quarter, 0))


def head_parts(raw, gain, cos, sin):
    inverse = inverse_rms(raw)
    hat = raw * inverse
    scaled = hat * gain
    return hat, inverse, (scaled * cos + swap_quarters(scaled) * sin).astype(BF16)


def probabilities(queries, keys):
    scores = dot(keys, queries, (0, 0)) * HEAD ** (-0.5)
    weights = jnp.exp(scores - jnp.max(scores, axis=0, keepdims=True))
    return weights * (1.0 / jnp.sum(weights, axis=0, keepdims=True))


def split_out(me, weight, rows, width, near, far, keep, over, weights=None):
    inner = 0.0
    for relative, out in ((3, far), (1, near), (0, keep), (2, over)):
        product = dot(weight[span(me, relative, width), :], rows)
        out[0, :width] = product.astype(out.dtype)
        if weights is not None:
            inner += jnp.sum(product * weights(relative), axis=0, keepdims=True)
    if weights is not None:
        far[0, width:] = two_parts(jnp.broadcast_to(inner, (8, inner.shape[1])))


def two_parts(values):
    high = values.astype(BF16)
    return jnp.concatenate([high.astype(F32), values - high.astype(F32)], axis=0).astype(BF16)


def attention_kernel(
    me_ref, p0, p1, p2, p3, mods, wqkv, wproj, gains, cos_ref, sin_ref,
    near, far, keep, over, attn_out, raw_out, heads_out, inverse_out,
    full, heads,
):
    me = me_ref[0]
    width = p0.shape[1]
    assemble((p0, p1, p2, p3), full, me)
    rows = full[...].astype(F32)
    inverse = inverse_rms(rows)
    inverse_out[0] = inverse
    columns_in = mods[0].T
    attn = (rows * inverse * (1.0 + columns_in[:, 1:2]) + columns_in[:, 0:1]).astype(BF16)
    attn_out[...] = attn
    raw_out[0] = dot(wqkv[...], attn)
    cos, sin = cos_ref[...], sin_ref[...]
    for head in range(width // HEAD):
        low = head * HEAD
        _, _, queries = head_parts(raw_out[0, low : low + HEAD], gains[:, 0:1], cos, sin)
        low += width
        _, _, keys = head_parts(raw_out[0, low : low + HEAD], gains[:, 1:2], cos, sin)
        low += width
        values = raw_out[0, low : low + HEAD].astype(BF16)
        attention = probabilities(queries, keys).astype(BF16)
        heads[head * HEAD : (head + 1) * HEAD] = dot(values, attention)
    out = heads[...].astype(BF16)
    heads_out[...] = out
    split_out(me, wproj, out, width, near, far, keep, over)


def mlp_kernel(
    me_ref, p0, p1, p2, p3, g0, g1, g2, g3, mods, wup_t, wup, wdown_t, wdown,
    near_a, far_a, keep_a, over_a, near_b, far_b, keep_b, over_b, mlp_out, hidden_out, rows_out, grad_out, inverse_out,
    full, modulated,
):
    me = me_ref[0]
    width = p0.shape[1]
    units = wdown.shape[0]
    assemble((p0, p1, p2, p3), full, me)
    rows = full[...].astype(F32)
    inverse = inverse_rms(rows)
    inverse_out[0] = inverse
    columns_in = mods[0].T
    scaled = rows * inverse * (1.0 + columns_in[:, 3:4])
    modulated[...] = scaled
    mlp = (scaled + columns_in[:, 2:3]).astype(BF16)
    mlp_out[...] = mlp
    gate = dot(wup_t[:units], mlp)
    up = dot(wup_t[units:], mlp)
    sigmoid = jax.nn.sigmoid(gate)
    silu = gate * sigmoid
    hidden = (silu * up).astype(BF16)
    hidden_out[...] = hidden
    assemble((g0, g1, g2, g3), full, me)
    grad_out[...] = full[...]
    grad_hidden = dot(wdown[...], full[...])
    rows_out[:units] = (grad_hidden * up * sigmoid * (1.0 + gate * (1.0 - sigmoid))).astype(BF16)
    rows_out[units:] = (grad_hidden * silu).astype(BF16)
    split_out(
        me, wup, rows_out[...], width, near_b, far_b, keep_b, over_b, lambda r: modulated[span(me, r, width), :]
    )
    split_out(me, wdown_t, hidden, width, near_a, far_a, keep_a, over_a)


def attention_back_kernel(
    me_ref, p0, p1, p2, p3, r0, r1, r2, r3, inverse_ref, mods, raw, wproj, wqkv_t, gains, cos_ref, sin_ref,
    near, far, keep, over, rows_out, grad_out, gains_out,
    full, heads, rows, scales, gains_sum,
):
    me = me_ref[0]
    width = p0.shape[1]
    assemble((p0, p1, p2, p3), full, me)
    grad_out[...] = full[...]
    heads[...] = dot(wproj[...], full[...])
    cos, sin = cos_ref[...], sin_ref[...]
    scale = HEAD ** (-0.5)

    @pl.when(pl.program_id(0) == 0)
    def _():
        gains_sum[...] = jnp.zeros_like(gains_sum)

    for head in range(width // HEAD):
        low = head * HEAD
        gain_q, gain_k = gains[:, 0:1], gains[:, 1:2]
        hat_q, inverse_q, queries = head_parts(raw[0, low : low + HEAD], gain_q, cos, sin)
        hat_k, inverse_k, keys = head_parts(raw[0, width + low : width + low + HEAD], gain_k, cos, sin)
        values = raw[0, 2 * width + low : 2 * width + low + HEAD].astype(BF16)
        grad_heads = heads[low : low + HEAD].astype(BF16)
        probability = probabilities(queries, keys)
        grad_attention = dot(values, grad_heads, (0, 0))
        rows[2 * width + low : 2 * width + low + HEAD] = dot(grad_heads, probability.astype(BF16), (1, 1))
        inner = jnp.sum(probability * grad_attention, axis=0, keepdims=True)
        grad_scores = (probability * (grad_attention - inner)).astype(BF16)
        grad_q = dot(keys, grad_scores) * scale
        grad_k = dot(queries, grad_scores, (1, 1)) * scale
        for index, grad, hat, inverse, gain in (
            (0, grad_q, hat_q, inverse_q, gain_q),
            (1, grad_k, hat_k, inverse_k, gain_k),
        ):
            grad = grad * cos - swap_quarters(grad) * sin
            product = grad * hat
            gains_sum[index] += product
            grad = grad * gain
            middle = jnp.mean(product * gain, axis=0, keepdims=True)
            start = index * width + low
            rows[start : start + HEAD] = inverse * (grad - hat * middle)
    rows_out[...] = rows[...].astype(BF16)
    inverse = inverse_ref[0]
    pieces = (r0, r1, r2, r3)
    scales[...] = mods[0].T

    def weights(relative):
        scale = 1.0 + scales[span(me, relative, width), 1:2]
        return pieces[relative][0].astype(F32) * inverse * scale

    split_out(me, wqkv_t, rows_out[...], width, near, far, keep, over, weights)

    @pl.when(pl.program_id(0) == pl.num_programs(0) - 1)
    def _():
        for index in range(2):
            gains_out[index : index + 1] = jnp.sum(gains_sum[index].T, axis=0, keepdims=True)


def columns_of(mods, width):
    return mods[0].T[:width]


def columns(values):
    lanes = lax.broadcasted_iota(jnp.int32, (values[0].shape[0], 128), 1)
    out = jnp.zeros((values[0].shape[0], 128), F32)
    for index, value in enumerate(values):
        out = jnp.where(lanes == index, value, out)
    return out


def sum_parts(values, width):
    return values[0, width : width + 1].astype(F32) + values[0, width + 8 : width + 9].astype(F32)


def total_inner(far, far_core, across, width):
    return (sum_parts(far, width) + sum_parts(far_core, width) + sum_parts(across, width)) / (4 * width)


def middle_back_kernel(
    s_ref, far, far_core, keep, core, across, cot, middle, branch, inverse_ref, mods,
    grad_out, piece_out, sums_out,
):
    width = keep.shape[1]
    modulation = columns_of(mods, width)
    inverse = inverse_ref[0]
    grad = keep[0] + core[0].astype(F32) + across[0, :width].astype(F32)
    normed = middle[0] * inverse
    inner = total_inner(far, far_core, across, width)
    grad_middle = cot[0] + inverse * (grad * (1.0 + modulation[:, 4:5]) - normed * inner)
    grad_out[0] = grad_middle
    piece_out[0] = (grad_middle * modulation[:, 2:3]).astype(BF16)
    sums_out[0] = columns(
        [
            jnp.sum(grad_middle * branch[0], axis=1, keepdims=True),
            jnp.sum(grad, axis=1, keepdims=True),
            jnp.sum(grad * normed, axis=1, keepdims=True),
        ]
    )


def last_kernel(
    s_ref, far, far_core, keep, core, across, grad_middle, latents, inverse_ref, mods,
    grad_out, back_out, sums_out,
):
    width = keep.shape[1]
    modulation = columns_of(mods, width)
    inverse = inverse_ref[0]
    grad = keep[0] + core[0].astype(F32) + across[0, :width].astype(F32)
    normed = latents[0] * inverse
    inner = total_inner(far, far_core, across, width)
    result = grad_middle[0] + inverse * (grad * (1.0 + modulation[:, 1:2]) - normed * inner)
    grad_out[0] = result
    back_out[0] = result.astype(BF16)
    sums_out[0] = columns(
        [jnp.sum(grad, axis=1, keepdims=True), jnp.sum(grad * normed, axis=1, keepdims=True)]
    )


def relay_kernel(s_ref, far, far_core, over, out):
    width = over.shape[1]
    out[0, :width] = (over[0] + far_core[0, :width].astype(F32)).astype(BF16)
    if out.shape[1] > width:
        inner = sum_parts(far, width) + sum_parts(far_core, width)
        out[0, width:] = two_parts(jnp.broadcast_to(inner, (8, inner.shape[1])))


def relay(scalars, far, far_core, over):
    images = over.shape[0]
    return call(
        relay_kernel, (images,), scalars,
        [by_image(far), by_image(far_core), by_image(over)],
        [image_out(images, far.shape[1:], BF16)],
    )[0]


def accumulate(lefts, rights, out):
    total = dot(lefts[0][...], rights[0][...], (1, 1))
    for left, right in zip(lefts[1:], rights[1:]):
        total += dot(left[...], right[...], (1, 1))
    out[...] = total.astype(out.dtype).reshape(out.shape)


def half_kernel(s_ref, *refs):
    parts = len(refs) // 2 - 1
    lefts, rights, out, kept = refs[:parts], refs[parts : 2 * parts], refs[-2], refs[-1]

    @pl.when(pl.program_id(0) == 0)
    def _():
        accumulate(lefts, rights, out)

    @pl.when(pl.program_id(0) == 1)
    def _():
        accumulate(lefts, rights, kept)


def weight_halves(index, lefts, rights, first, rows):
    half = rows // 2
    outer = rights[0].shape[0]
    place = lambda b, s: (first // half + b * s[0] + (1 - b) * (1 - s[0]), 0)
    ins = [(left, (half, left.shape[1]), place, False) for left in lefts] + [entire(right) for right in rights]
    block = (1, half, outer)
    outs = [(block, kind, block, lambda b, s: (0, 0, 0)) for kind in (BF16, F32)]
    return call(half_kernel, (2,), index, ins, outs)


def attention_weight_kernel(s_ref, *refs):
    parts = len(refs) // 4 - 1
    rows, heads, inputs, grads = (refs[i * parts : (i + 1) * parts] for i in range(4))
    out1, kept1, out2, kept2, total = refs[4 * parts :]
    group = pl.program_id(0)
    half = total.shape[0] // 2

    @pl.when(group < 3)
    def _():
        accumulate(rows, inputs, total)

    @pl.when(group == 3)
    def _():
        accumulate(heads, grads, total)

    def store(index, out, kept):
        out[0] = total[pl.ds(pl.multiple_of((1 - index) * half, 16), half)].astype(BF16)
        kept[0] = total[pl.ds(pl.multiple_of(index * half, 16), half)]

    @pl.when(group < 2)
    def _():
        store(s_ref[0], out1, kept1)

    @pl.when(group >= 2)
    def _():
        store(s_ref[1], out2, kept2)


def attention_weight_halves(indices, rows, heads, inputs, grads):
    size = heads[0].shape[0]
    outer = inputs[0].shape[0]
    ins = [(left, (size, left.shape[1]), lambda g, s: (jnp.minimum(g, 2), 0), False) for left in rows]
    ins += [entire(array) for array in heads + inputs + grads]
    shape, block = (2, size // 2, outer), (1, size // 2, outer)
    outs = []
    for place in (lambda g, s: (jnp.minimum(g, 1), 0, 0), lambda g, s: (jnp.maximum(g - 2, 0), 0, 0)):
        outs += [(shape, BF16, block, place), (shape, F32, block, place)]
    return call(attention_weight_kernel, (4,), indices, ins, outs, scratch=[pltpu.VMEM((size, outer), F32)])


def paired_kernel(s_ref, *refs):
    out = refs[-1]
    blocks = pl.num_programs(0) // 4
    units = out.shape[2]
    for index, source in enumerate(refs[:-1]):

        @pl.when(pl.program_id(0) // blocks == index)
        def _():
            values = source[0].astype(F32)
            for pair in range(out.shape[1]):
                out[:, pair, :] = values[:, pair * units : (pair + 1) * units]


def paired(indices, sources, pairs, size):
    _, half, outer = sources[0].shape
    blocks = half // size
    ins = [
        (a, (1, size, outer), lambda b, s, f=i * blocks: (0, jnp.clip(b - f, 0, blocks - 1), 0), False)
        for i, a in enumerate(sources)
    ]
    shape = (4 * half, pairs, outer // pairs)

    def place(b, s):
        chunk, within = b // (2 * blocks), b % (2 * blocks)
        own = jnp.where(chunk == 0, s[0], s[1])
        return (chunk * 2 * blocks + ((within // blocks) ^ own) * blocks + within % blocks, 0, 0)

    return call(paired_kernel, (4 * blocks,), indices, ins, [(shape, F32, (size,) + shape[1:], place)])[0]


def add_split_kernel(s_ref, own_a, got_a, own_b, got_b, out, kept):
    out[...] = (own_a[...] + got_a[...].astype(F32)).astype(BF16)
    kept[...] = own_b[...] + got_b[...].astype(F32)


def add_split(index, own, received, axis):
    groups, rows, outer = own.shape
    cut = 3 if outer % 384 == 0 else 1
    size = outer // cut
    if axis == 1:
        shape = (groups, rows // 2, outer)
        block = (1, rows // 2, size)
        here = lambda g, c, s: (g, s[0], c)
        there = lambda g, c, s: (g, 1 - s[0], c)
    else:
        half = groups // 2
        shape = (half, rows, outer)
        block = (1, rows, size)
        here = lambda g, c, s: (s[0] * half + g, 0, c)
        there = lambda g, c, s: ((1 - s[0]) * half + g, 0, c)
    plain = lambda g, c, s: (g, 0, c)
    ins = [
        (own, block, there, False),
        (received, block, there, False),
        (own, block, here, False),
        (received, block, here, False),
    ]
    outs = [(shape, BF16, block, plain), (shape, F32, block, plain)]
    return call(add_split_kernel, (shape[0], cut), index, ins, outs)


def unfold_kernel(s_ref, *refs):
    out = refs[-1]
    blocks = pl.num_programs(0) // (len(refs) - 1)
    for index, source in enumerate(refs[:-1]):

        @pl.when(pl.program_id(0) // blocks == index)
        def _():
            out[0] = source[0].astype(F32)


def unfold(index, segments):
    rows, outer = segments[0][0].shape[1:]
    ins = []
    for mine, other, group in segments:
        for half in (mine, other):
            ins.append((half, (1, rows, outer), lambda b, s, g=group: (g, 0, 0), False))
    place = lambda b, s: (b // 2, (b % 2) ^ s[0], 0)
    outs = [((len(segments), 2 * rows, outer), F32, (1, rows, outer), place)]
    return call(unfold_kernel, (len(ins),), index, ins, outs)[0]


def unfold_pair_kernel(s_ref, mine1, other1, mine2, other2, qkv, proj):
    step = pl.program_id(0)
    for index, source in enumerate((mine1, other1, mine2, other2)):

        @pl.when((step // 4) * 2 + step % 2 == index)
        def _():
            values = source[0].astype(F32)

            @pl.when(step < 6)
            def _():
                qkv[0] = values

            @pl.when(step >= 6)
            def _():
                proj[...] = values


def unfold_pair(indices, sources):
    _, half, outer = sources[0].shape
    block = (1, half, outer)
    first = lambda b, s: (jnp.minimum(b // 2, 1), 0, 0)
    second = lambda b, s: (jnp.maximum(b // 2 - 2, 0), 0, 0)
    ins = [(a, block, first if i < 2 else second, False) for i, a in enumerate(sources)]

    def row(b, s):
        return (b % 2) ^ jnp.where(b < 4, s[0], s[1])

    outs = [
        (
            (3, 2 * half, outer), F32, block,
            lambda b, s: (jnp.minimum(b // 2, 2), row(jnp.minimum(b, 5), s), 0),
        ),
        ((2 * half, outer), F32, block[1:], lambda b, s: (row(jnp.maximum(b, 6), s), 0)),
    ]
    return call(unfold_pair_kernel, (8,), indices, ins, outs)


class Order:
    def __init__(self):
        self.last = None

    def __call__(self, step, *args):
        if self.last is not None:
            args = lax.optimization_barrier((self.last, *args))[1:]
        result = step(*args)
        self.last = jax.tree.leaves(result)
        return result


class Reduction:
    def __init__(self, order, second_first=False):
        self.order = order
        self.bits = bits_of("dp")
        if second_first and len(self.bits) > 1:
            self.bits[:2] = self.bits[1::-1]
        self.levels = []

    def index(self, bit):
        return has_bit("dp", bit).astype(jnp.int32)[None]

    def first(self):
        return self.index(self.bits[0])

    def begin(self, out, own):
        self.own = own
        self.received = exchange(out, "dp", self.bits[0])

    def halve(self, level):
        if level >= len(self.bits):
            return
        bit = self.bits[level]
        groups, rows, _ = self.own.shape
        if rows % 16 == 0:
            axis = 1
        elif groups % 2 == 0:
            axis = 0
        else:
            axis = None
        if axis is None:
            self.own = self.order(lambda a, b: a + b.astype(F32), self.own, self.received)
            self.received = exchange(self.own.astype(BF16), "dp", bit)
            return
        index = self.index(bit)
        out, self.own = self.order(lambda a, b: add_split(index, a, b, axis), self.own, self.received)
        self.received = exchange(out, "dp", bit)
        self.levels.append((bit, axis))

    def join(self):
        self.own = self.order(lambda a, b: (a + b.astype(F32)).astype(BF16), self.own, self.received)
        bit = self.levels[-1][0] if self.levels else self.bits[0]
        self.received = exchange(self.own, "dp", bit)

    def double(self, level):
        if level >= len(self.levels):
            return
        bit, axis = self.levels[-1 - level]
        later = has_bit("dp", bit)
        self.own = self.order(lambda a, b: in_order(a, b, later, axis, jnp.concatenate), self.own, self.received)
        outer = self.levels[-2 - level][0] if level + 1 < len(self.levels) else self.bits[0]
        self.received = exchange(self.own, "dp", outer)


def rope_tables():
    quarter = HEAD // 4
    frequency = 10000.0 ** (-np.arange(quarter, dtype=np.float32) / quarter)
    patches = np.arange(P_SIZE)
    row = (patches // GRID).astype(np.float32)[None, :] * frequency[:, None]
    col = (patches % GRID).astype(np.float32)[None, :] * frequency[:, None]
    cos = np.concatenate([np.cos(row), np.cos(row), np.cos(col), np.cos(col)])
    sin = np.concatenate([-np.sin(row), np.sin(row), -np.sin(col), np.sin(col)])
    return jnp.asarray(cos, F32), jnp.asarray(sin, F32)


def einsum(spec, *operands):
    return jnp.einsum(spec, *operands, preferred_element_type=F32)


PARTS = ((0, 4),)


def pack_kernel(s_ref, rows, out):
    out[...] = rows[...].astype(BF16)


def last_slots(count, rows):
    slots = rows.shape[0]
    place = lambda i, s: (lax.rem(s[0] - IMG_DEV + i + slots, slots), 0, 0)
    ins = [(rows, (1,) + rows.shape[1:], place, False)]
    return call(pack_kernel, (IMG_DEV,), count, ins, [image_out(IMG_DEV, rows.shape[1:], BF16)])[0]


def transpose_kernel(s_ref, values, out):
    out[...] = values[...].T


def transposed(scalars, array):
    rows, outer = array.shape
    ins = [(array, (rows, 128), lambda i, s: (0, i), False)]
    return call(transpose_kernel, (outer // 128,), scalars, ins, [((outer, rows), array.dtype, (128, rows), lambda i, s: (i, 0))])[0]


def share_kernel(device_ref, facts, ids_out, own_out, load_out, histogram):
    devices, slots = facts.shape[0], facts.shape[1] - 1
    for b in range(NBINS):
        histogram[b] = 0

    def count(i, carry):
        for j in range(slots):
            b = facts[i, j]
            histogram[b] = histogram[b] + jnp.where(j < facts[i, slots], 1, 0)
        return carry

    lax.fori_loop(0, devices, count, 0)

    def place(i, carry):
        came, before = carry
        for k in range(IMG_DEV):
            moved = (i - 1) * slots + lax.rem(before - IMG_DEV + k + slots, slots)
            ids_out[i * IMG_DEV + k] = jnp.where(k >= IMG_DEV - came, moved, i * slots + k)

        @pl.when(i == device_ref[0])
        def _():
            own_out[0] = came

        return came + facts[i, slots] - IMG_DEV, facts[i, slots]

    lax.fori_loop(0, devices, place, (0, 0))
    for k in range(IMG_DEV):
        slot = ids_out[device_ref[0] * IMG_DEV + k]
        owner, j = lax.div(slot, slots), lax.rem(slot, slots)
        load_out[k] = histogram[facts[owner, j]]
        load_out[IMG_DEV + k] = jnp.where(j < facts[owner, slots], 1, 0)


def share(device, facts):
    smem = pl.BlockSpec(memory_space=pltpu.SMEM)
    return pl.pallas_call(
        share_kernel,
        grid_spec=pltpu.PrefetchScalarGridSpec(
            num_scalar_prefetch=1, grid=(), in_specs=[smem], out_specs=[smem] * 3,
            scratch_shapes=[pltpu.SMEM((NBINS,), jnp.int32)],
        ),
        out_shape=[jax.ShapeDtypeStruct((n,), jnp.int32) for n in (facts.shape[0] * IMG_DEV, 8, 2 * IMG_DEV)],
        cost_estimate=pl.CostEstimate(flops=1000, bytes_accessed=1000, transcendentals=0),
    )(device, facts)


def choose(s_ref, start, own, came):
    moved = pl.program_id(0) + start >= IMG_DEV - s_ref[0]
    return jnp.where(moved, came[0].astype(F32), own[0])


def rows_kernel(start, s_ref, own, came, rows_out, piece_out):
    rows = choose(s_ref, start, own, came)
    rows_out[0] = rows
    piece_out[0] = rows.astype(BF16)


def cot_kernel(start, s_ref, own, came, mods, rows_out, piece_out):
    modulation = columns_of(mods, own.shape[1])
    rows = choose(s_ref, start, own, came) * modulation[:, 6:7]
    rows_out[0] = rows
    piece_out[0] = (rows * modulation[:, 5:6]).astype(BF16)


def from_image(array, start):
    rest = array.shape[1:]
    return (array, (1,) + rest, lambda i, s: (i + start,) + (0,) * len(rest), False)


def middle_kernel(s_ref, keep, core, across, rows, mods, branch_out, middle_out, piece_out):
    branch = keep[0] + core[0].astype(F32) + across[0].astype(F32)
    branch_out[0] = branch
    middle = rows[0] + columns_of(mods, rows.shape[1])[:, 2:3] * branch
    middle_out[0] = middle
    piece_out[0] = middle.astype(BF16)


def result_kernel(s_ref, keep, core, across, middle, cot, mods, result_out, back_out, sums_out):
    branch = keep[0] + core[0].astype(F32) + across[0].astype(F32)
    result = middle[0] + columns_of(mods, middle.shape[1])[:, 5:6] * branch
    result_out[0] = result
    back_out[0] = result.astype(BF16)
    sums_out[0] = columns([jnp.sum(cot[0] * branch, axis=1, keepdims=True)])


def home_kernel(starts, s_ref, *refs):
    out = refs[-1]
    parts = len(starts)
    slot = pl.program_id(0)
    came, count = s_ref[0], s_ref[1]
    kept, away = refs[0][0], refs[parts][0].astype(F32)
    for part in range(1, parts):
        kept = jnp.where(slot >= starts[part], refs[part][0], kept)
        place = slot - count + IMG_DEV
        away = jnp.where(place >= starts[part], refs[parts + part][0].astype(F32), away)
    chosen = jnp.where(slot < IMG_DEV - came, kept, away)
    out[0] = jnp.where(slot < count, chosen, 0.0)


def home(scalars, slots, here, back):
    starts, start = [], 0
    for part in here:
        starts.append(start)
        start += part.shape[0]
    block = (1,) + here[0].shape[1:]
    ins = []
    for part, first in zip(here, starts):
        end = part.shape[0] - 1
        ins.append((part, block, lambda i, s, f=first, e=end: (jnp.clip(i - f, 0, e), 0, 0), False))
    for part, first in zip(back, starts):
        end = part.shape[0] - 1
        ins.append(
            (part, block, lambda i, s, f=first, e=end: (jnp.clip(i - s[1] + IMG_DEV - f, 0, e), 0, 0), False)
        )
    outs = [image_out(slots, block[1:], F32)]
    return call(functools.partial(home_kernel, starts), (slots,), scalars, ins, outs)[0]


def local(
    latents,
    condition,
    cotangent,
    noise_bins,
    image_counts,
    ada_weight,
    ada_bias,
    qkv_weight,
    norm_gains,
    proj_weight,
    gate_up_weight,
    down_weight,
):
    slots = latents.shape[0]
    devices = lax.axis_size("dp")
    device = lax.axis_index("dp").astype(jnp.int32)
    part = lax.axis_index("mp")
    me = part.astype(jnp.int32)[None]
    width = latents.shape[2]
    features = qkv_weight.shape[0]
    units = down_weight.shape[0]
    rows_in = latents.transpose(0, 2, 1)
    cot_in = cotangent.transpose(0, 2, 1)
    cos, sin = rope_tables()
    gains = norm_gains.astype(F32).T
    order = Order()

    own_count = image_counts[0]
    silu = jax.nn.silu(condition)
    facts = jnp.concatenate([noise_bins, image_counts]).astype(F32)
    facts = jnp.pad(facts, (0, width - slots - 1))[None]
    message = jnp.concatenate([silu, facts]).astype(BF16)[None]
    latest = (own_count - IMG_DEV + jnp.arange(IMG_DEV)) % slots
    silu_came = shifted(jnp.take(silu, latest, axis=0).astype(BF16), "dp", 1)
    message = gather_small(message, "dp", 0)
    facts = message[:, slots, : slots + 1].astype(jnp.int32)
    rows_last = order(last_slots, image_counts, rows_in)
    share_ids, own_facts, loads = order(lambda f: share(device[None], f), facts)
    came_here = own_facts[:1]
    home_facts = jnp.concatenate([came_here, image_counts])
    rows_last, _ = lax.optimization_barrier((rows_last, own_facts))
    rows_came = shifted(rows_last, "dp", 1)
    came = types.SimpleNamespace()

    silu_near = jnp.concatenate([silu[:IMG_DEV].astype(BF16), silu_came])
    silu_near = gather_small(silu_near, "mp", 1)
    modulation = einsum("bd,dkf->bkf", silu_near, ada_weight) + ada_bias.astype(F32)
    spread_mods = jnp.concatenate([modulation[:, 0:2], modulation[:, 3:5]], axis=1)
    spread_mods = gather_small(spread_mods, "mp", 2)

    parts = PARTS
    count = len(parts)
    state = [types.SimpleNamespace() for _ in parts]
    wqkv = qkv_weight.transpose(1, 2, 0).reshape(3 * width, features)
    weights = types.SimpleNamespace()

    def prepare():
        up = order(lambda w: w.reshape(features, 2 * units), gate_up_weight)
        weights.up = up
        weights.proj_t, weights.qkv_t, weights.down_t = (
            order(lambda w: transposed(me, w), array) for array in (proj_weight, wqkv, down_weight)
        )
        cot_last = order(last_slots, image_counts, cot_in)
        cot_ready, _ = lax.optimization_barrier((cot_last, weights.down_t))
        came.cot = shifted(cot_ready, "dp", 1)

    def prepare_up():
        weights.up_t = order(lambda w: transposed(me, w), weights.up)

    def choose_rows(p):
        start, images = parts[p]
        st = state[p]
        rest = rows_in.shape[1:]
        st.rows, piece = order(
            lambda own, came: call(
                functools.partial(rows_kernel, start), (images,), came_here,
                [from_image(own, start), from_image(came, start)],
                [image_out(images, rest, F32), image_out(images, rest, BF16)],
            ),
            rows_in, rows_came,
        )
        st.pieces_one = spread(piece)

    moved = (jnp.arange(IMG_DEV) >= IMG_DEV - came_here[0])[:, None, None]
    spread_mods = jnp.where(moved, spread_mods[IMG_DEV:], spread_mods[:IMG_DEV])
    spread_mods = jnp.pad(spread_mods, ((0, 0), (0, 4), (0, 0)))
    modulation = jnp.where(moved, modulation[IMG_DEV:], modulation[:IMG_DEV])
    load, live = loads[:IMG_DEV].astype(F32), loads[IMG_DEV:].astype(F32)
    scaling = live * (IMG_DEV * devices) / (NBINS * (load + 1.0 - live))
    scaling = jnp.broadcast_to(scaling[:, None, None], (IMG_DEV, 2, width))
    mods_all = jnp.concatenate([modulation, scaling], axis=1)
    mods_all = jnp.pad(mods_all, ((0, 0), (0, 0), (0, -width % 128)))
    for p, (start, images) in enumerate(parts):
        state[p].mods_full = spread_mods[start : start + images]
        state[p].mods = mods_all[start : start + images]

    def attention(p):
        st = state[p]
        images = parts[p][1]
        st.near, st.far, st.keep, st.over, st.attn, st.raw, st.heads, st.inverse_one = order(
            lambda *a: call(
                attention_kernel, (images,), me,
                [by_image(x) for x in a[:5]] + [entire(x) for x in a[5:]],
                [
                    image_out(images, (width, P_SIZE), BF16),
                    image_out(images, (width, P_SIZE), BF16),
                    image_out(images, (width, P_SIZE), F32),
                    image_out(images, (width, P_SIZE), F32),
                    flat_out(images, features),
                    image_out(images, (3 * width, P_SIZE), F32),
                    flat_out(images, width),
                    image_out(images, (1, P_SIZE), F32),
                ],
                scratch=[pltpu.VMEM((features, P_SIZE), BF16), pltpu.VMEM((width, P_SIZE), F32)],
                us=4.5 * images,
                vmem=58,
            ),
            *st.pieces_one, st.mods_full, wqkv, weights.proj_t, gains, cos, sin,
        )
        st.far_core = exchange(st.far, "mp", 1)
        st.core = exchange(st.near, "mp", 1)

    def choose_cot(p):
        start, images = parts[p]
        st = state[p]
        rest = rows_in.shape[1:]
        st.cot, piece = order(
            lambda own, came, mods: call(
                functools.partial(cot_kernel, start), (images,), came_here,
                [from_image(own, start), from_image(came, start), by_image(mods)],
                [image_out(images, rest, F32), image_out(images, rest, BF16)],
            ),
            cot_in, came.cot, st.mods,
        )
        st.pieces_grad_two = spread(piece)

    def relay_one(p):
        st = state[p]
        out = order(lambda *a: relay(me, *a), st.far, st.far_core, st.over)
        st.across = exchange(out, "mp", 2)

    def middle(p):
        st = state[p]
        images = parts[p][1]
        rest = (width, P_SIZE)
        st.branch_one, st.middle, piece = order(
            lambda keep, core, *a: call(
                middle_kernel, (images,), me,
                [by_image(keep), by_image(core)] + [by_image(x) for x in a],
                [image_out(images, rest, F32), image_out(images, rest, F32), image_out(images, rest, BF16)],
            ),
            st.keep, st.core, st.across, st.rows, st.mods,
        )
        st.pieces_two = spread(piece)

    def mlp(p):
        st = state[p]
        images = parts[p][1]
        (
            st.near_a, st.far_a, st.keep_a, st.over_a,
            st.near_b, st.far_b, st.keep_b, st.over_b,
            st.mlp, st.hidden, st.grad_rows_two, st.grad_two, st.inverse_two,
        ) = order(
            lambda *a: call(
                mlp_kernel, (images,), me,
                [by_image(x) for x in a[:9]] + [entire(x) for x in a[9:]],
                [
                    image_out(images, (width, P_SIZE), BF16),
                    image_out(images, (width, P_SIZE), BF16),
                    image_out(images, (width, P_SIZE), F32),
                    image_out(images, (width, P_SIZE), F32),
                    image_out(images, (width, P_SIZE), BF16),
                    image_out(images, (width + 16, P_SIZE), BF16),
                    image_out(images, (width, P_SIZE), F32),
                    image_out(images, (width, P_SIZE), F32),
                    flat_out(images, features),
                    flat_out(images, units),
                    flat_out(images, 2 * units),
                    flat_out(images, features),
                    image_out(images, (1, P_SIZE), F32),
                ],
                scratch=[pltpu.VMEM((features, P_SIZE), BF16), pltpu.VMEM((features, P_SIZE), F32)],
                us=6.0 * images,
                vmem=58,
            ),
            *st.pieces_two, *st.pieces_grad_two, st.mods_full,
            weights.up_t, weights.up, weights.down_t, down_weight,
        )
        st.far_core_b = exchange(st.far_b, "mp", 1)
        st.core_b = exchange(st.near_b, "mp", 1)

    def relay_three(p):
        st = state[p]
        out = order(lambda *a: relay(me, *a), st.far_b, st.far_core_b, st.over_b)
        st.across_b = exchange(out, "mp", 2)

    def middle_back(p):
        st = state[p]
        images = parts[p][1]
        st.grad_middle, piece, st.sums_two = order(
            lambda *a: call(
                middle_back_kernel, (images,), me, [by_image(x) for x in a],
                [
                    image_out(images, (width, P_SIZE), F32),
                    image_out(images, (width, P_SIZE), BF16),
                    image_out(images, (width, 128), F32),
                ],
            ),
            st.far_b, st.far_core_b, st.keep_b, st.core_b, st.across_b, st.cot, st.middle,
            st.branch_one, st.inverse_two, st.mods,
        )
        st.pieces_grad_one = spread(piece)

    def result_core(p):
        st = state[p]
        far, near, _ = lax.optimization_barrier((st.far_a, st.near_a, order.last))
        st.far_core_a = exchange(far, "mp", 1)
        st.core_a = exchange(near, "mp", 1)

    def relay_two(p):
        st = state[p]
        out = order(lambda *a: relay(me, *a), st.far_a, st.far_core_a, st.over_a)
        st.across_a = exchange(out, "mp", 2)

    def result(p):
        st = state[p]
        images = parts[p][1]
        st.result, back, st.sums_three = order(
            lambda keep, core, *a: call(
                result_kernel, (images,), me,
                [by_image(keep), by_image(core)] + [by_image(x) for x in a],
                [
                    image_out(images, (width, P_SIZE), F32),
                    image_out(images, (width, P_SIZE), BF16),
                    image_out(images, (width, 128), F32),
                ],
            ),
            st.keep_a, st.core_a, st.across_a, st.middle, st.cot, st.mods,
        )
        st.result_out = back

    def attention_back(p):
        st = state[p]
        images = parts[p][1]
        st.near_c, st.far_c, st.keep_c, st.over_c, st.grad_rows_one, st.grad_one, st.gain_sums = order(
            lambda *a: call(
                attention_back_kernel, (images,), me,
                [by_image(x) for x in a[:11]] + [entire(x) for x in a[11:]],
                [
                    image_out(images, (width, P_SIZE), BF16),
                    image_out(images, (width + 16, P_SIZE), BF16),
                    image_out(images, (width, P_SIZE), F32),
                    image_out(images, (width, P_SIZE), F32),
                    flat_out(images, 3 * width),
                    flat_out(images, features),
                    ((2, HEAD), F32, (2, HEAD), lambda i, s: (0, 0)),
                ],
                scratch=[
                    pltpu.VMEM((features, P_SIZE), BF16),
                    pltpu.VMEM((width, P_SIZE), F32),
                    pltpu.VMEM((3 * width, P_SIZE), F32),
                    pltpu.VMEM((features, 8), F32),
                    pltpu.VMEM((2, HEAD, P_SIZE), F32),
                ],
                us=4.5 * images,
                vmem=58,
            ),
            *st.pieces_grad_one, *st.pieces_one, st.inverse_one, st.mods_full, st.raw,
            proj_weight, weights.qkv_t, gains, cos, sin,
        )
        st.far_core_c = exchange(st.far_c, "mp", 1)
        st.core_c = exchange(st.near_c, "mp", 1)

    def relay_four(p):
        st = state[p]
        out = order(lambda *a: relay(me, *a), st.far_c, st.far_core_c, st.over_c)
        st.across_c = exchange(out, "mp", 2)

    def last(p):
        st = state[p]
        images = parts[p][1]
        st.grad_latent, back, st.sums_one = order(
            lambda *a: call(
                last_kernel, (images,), me, [by_image(x) for x in a],
                [
                    image_out(images, (width, P_SIZE), F32),
                    image_out(images, (width, P_SIZE), BF16),
                    image_out(images, (width, 128), F32),
                ],
            ),
            st.far_c, st.far_core_c, st.keep_c, st.core_c, st.across_c, st.grad_middle, st.rows,
            st.inverse_one, st.mods,
        )
        st.latent_out = back

    def each(field):
        return [field(st) for st in state]

    attn1 = Reduction(order)
    attn2 = Reduction(order, True)
    up1 = Reduction(order)
    up2 = Reduction(order, True)
    down = Reduction(order, False)

    def attention_weights():
        indices = jnp.concatenate([attn1.first(), attn2.first()])
        out1, own1, out2, own2 = order(
            lambda *a: attention_weight_halves(indices, *(a[i * count : (i + 1) * count] for i in range(4))),
            *each(lambda s: s.grad_rows_one), *each(lambda s: s.heads),
            *each(lambda s: s.attn), *each(lambda s: s.grad_one),
        )
        attn1.begin(out1, own1)
        attn2.begin(out2, own2)

    def begin(reduction):
        if reduction is down:
            lefts, rights, first, rows = each(lambda s: s.hidden), each(lambda s: s.grad_two), 0, units
        else:
            lefts, rights, rows = each(lambda s: s.mlp), each(lambda s: s.grad_rows_two), features // 2
            first = 0 if reduction is up1 else rows
        index = reduction.first()
        reduction.begin(
            *order(lambda *a: weight_halves(index, a[:count], a[count:], first, rows), *lefts, *rights)
        )

    def halve(reduction, level):
        reduction.halve(level)

    def join(reduction):
        for level in range(3, len(reduction.bits)):
            reduction.halve(level)
        reduction.join()
        for level in range(0, len(reduction.levels) - 2):
            reduction.double(level)

    def double(reduction, step):
        reduction.double(max(0, len(reduction.levels) - 2) + step)

    def unfolded(reduction, groups):
        index = reduction.first()
        return order(lambda a, b: unfold(index, [(a, b, g) for g in groups]), reduction.own, reduction.received)

    def finish_attention():
        done.qkv = order(
            lambda *a: unfold_pair(jnp.concatenate([attn1.first(), attn2.first()]), a),
            attn1.own, attn1.received, attn2.own, attn2.received,
        )

    def finish_down():
        done.down = unfolded(down, (0,))[0]

    def finish_up():
        indices = jnp.concatenate([up1.first(), up2.first()])
        done.up = order(
            lambda *a: paired(indices, a, 2, features // 8), up1.own, up1.received, up2.own, up2.received
        )

    done = types.SimpleNamespace()

    def send_back(p):
        st = state[p]
        result_out, latent_out, _ = lax.optimization_barrier((st.result_out, st.latent_out, order.last))
        st.result_back = shifted(result_out, "dp", -1)
        st.latent_back = shifted(latent_out, "dp", -1)

    def modulation_back():
        columns_one, columns_two, columns_three = (
            jnp.concatenate(each(field))
            for field in (lambda s: s.sums_one, lambda s: s.sums_two, lambda s: s.sums_three)
        )
        grad_mod = jnp.stack(
            [
                columns_one[..., 0],
                columns_one[..., 1],
                columns_two[..., 0],
                columns_two[..., 1],
                columns_two[..., 2],
                columns_three[..., 0],
            ]
        ).astype(BF16)
        gain_sums = sum(each(lambda s: s.gain_sums)).reshape(1, -1)
        high = gain_sums.astype(BF16)
        gain_row = jnp.concatenate([high, (gain_sums - high.astype(F32)).astype(BF16)], axis=1)
        sent = jnp.concatenate([grad_mod.reshape(6 * IMG_DEV, width), gain_row])[None]
        done.message = sent
        done.bits = bits_of("dp")
        modulation_send()

    def modulation_send():
        done.other = exchange(done.message, "dp", done.bits[0])

    def modulation_step():
        later = has_bit("dp", done.bits.pop(0))
        done.message = order(lambda a, b: in_order(a, b, later, 0, jnp.concatenate), done.message, done.other)
        if done.bits:
            modulation_send()

    def ada_back():
        while done.bits:
            modulation_step()
        sent = done.message
        mod_share = sent[:, : 6 * IMG_DEV].reshape(devices, 6, IMG_DEV, width).transpose(1, 0, 2, 3)
        mod_share = mod_share.reshape(6, devices * IMG_DEV, width)
        gain_sums = jnp.sum(sent[:, 6 * IMG_DEV].astype(F32), axis=0).reshape(2, 2, HEAD)
        done.gains = sum_small(gain_sums[0] + gain_sums[1], "mp")
        silu_all = gather_small(message[:, :slots], "mp", 2).reshape(devices * slots, -1)
        silu_share = jnp.take(silu_all, share_ids, axis=0)
        done.ada = order(lambda a, b: einsum("kbf,bd->kfd", a, b), mod_share, silu_share)
        done.bias = jnp.sum(mod_share.astype(F32), axis=1)

        slot = jnp.arange(slots)
        stays = slot < IMG_DEV - came_here[0]
        away_place = jnp.clip(slot - own_count + IMG_DEV, 0, IMG_DEV - 1)
        share_place = jnp.where(stays, device * IMG_DEV + slot, (device + 1) * IMG_DEV + away_place)
        share_place = jnp.clip(share_place, 0, devices * IMG_DEV - 1)
        live_here = (slot < own_count).astype(BF16)
        mod_slots = jnp.take(mod_share, share_place, axis=1) * live_here[None, :, None]
        grad_silu = sum_small(einsum("kbf,dkf->bd", mod_slots, ada_weight), "mp")
        grad_silu = lax.dynamic_slice_in_dim(grad_silu, part * width, width, 1)
        sigmoid_cond = jax.nn.sigmoid(condition)
        done.cond = grad_silu * sigmoid_cond * (1.0 + condition * (1.0 - sigmoid_cond))

    def home_result():
        done.output = order(
            lambda *a: home(home_facts, slots, a[:count], a[count:]), *each(lambda s: s.result), *each(lambda s: s.result_back)
        )

    def home_latent():
        done.latent = order(
            lambda *a: home(home_facts, slots, a[:count], a[count:]), *each(lambda s: s.grad_latent), *each(lambda s: s.latent_back)
        )

    prepare()
    choose_rows(0)
    prepare_up()
    choose_cot(0)
    attention(0)
    relay_one(0)
    middle(0)
    mlp(0)
    begin(down)
    relay_three(0)
    begin(up2)
    begin(up1)
    middle_back(0)
    halve(down, 1)
    result_core(0)
    halve(up2, 1)
    relay_two(0)
    halve(up1, 1)
    attention_back(0)
    halve(up2, 2)
    halve(up1, 2)
    attention_weights()
    halve(down, 2)
    relay_four(0)
    result(0)
    join(up1)
    join(up2)
    halve(attn1, 1)
    halve(attn2, 1)
    last(0)
    join(down)
    modulation_back()
    halve(attn2, 2)
    double(up1, 0)
    modulation_step()
    send_back(0)
    double(up2, 0)
    halve(attn1, 2)
    double(down, 0)
    join(attn2)
    double(up1, 1)
    modulation_step()
    home_result()
    home_latent()
    join(attn1)
    double(up2, 1)
    double(down, 1)
    double(attn2, 0)
    modulation_step()
    ada_back()
    double(attn1, 0)
    finish_up()
    finish_down()
    double(attn1, 1)
    double(attn2, 1)
    finish_attention()
    return (
        done.output.transpose(0, 2, 1),
        done.latent.transpose(0, 2, 1),
        done.cond,
        done.ada.transpose(2, 0, 1),
        done.bias,
        done.qkv[0].transpose(2, 0, 1),
        done.gains,
        done.qkv[1],
        done.up,
        done.down,
    )


def solution(mesh):
    return jax.shard_map(
        local,
        mesh=mesh,
        in_specs=(
            P("dp", None, "mp"),
            P("dp", "mp"),
            P("dp", None, "mp"),
            P("dp"),
            P("dp"),
            P(None, None, "mp"),
            P(None, "mp"),
            P(None, None, "mp"),
            P(),
            P("mp", None),
            P(None, None, "mp"),
            P("mp", None),
        ),
        out_specs=(
            P("dp", None, "mp"),
            P("dp", None, "mp"),
            P("dp", "mp"),
            P(None, None, "mp"),
            P(None, "mp"),
            P(None, None, "mp"),
            P(),
            P("mp", None),
            P(None, None, "mp"),
            P("mp", None),
        ),
        check_vma=False,
    )
```

time: 634 us -> 460 us (0.73)
  Pallas kernels: 0 us -> 159 us
  waiting for transfers between devices: 246 us -> 116 us
  other arithmetic: 107 us -> 25.8 us
  local copies, waits for them, and re-layouts: 119 us -> 39.7 us
  matrix products: 64.9 us -> 11.3 us
  starting transfers between devices: 86.6 us -> 99.9 us
    pallas_call x0 -> x39, Pallas kernels: none -> 159 us  [the longest x38 157 us: call(): pl.pallas_call(kernel, grid_spec=pltpu.PrefetchScalarGridSpec(num_scalar_...]
    ppermute x67 -> x70, waiting for transfers between devices: 233 us -> 114 us  [exchange(): return lax.ppermute(value, axis, pairs)]
    dot_general x22 -> x3, matrix products: 64.9 us -> 11.3 us  [einsum(): return jnp.einsum(spec, *operands, preferred_element_type=F32)]
    convert_element_type x26 -> x1, local copies, waits for them, and re-layouts: 33.5 us -> 0.63 us  [modulation_back(): grad_mod = jnp.stack([columns_one[..., 0], columns_one[..., 1], columns_t...]
    transpose x4 -> x2, local copies, waits for them, and re-layouts: 24.3 us -> 0.76 us  [the longest x1 0.71 us: local(): gains = norm_gains.astype(F32).T]
    convert_element_type x19 -> x9, other arithmetic: 26.3 us -> 5.23 us  [the longest x5 4.06 us: join(): (a + b.astype(F32)).astype(BF16)]
    ppermute x67 -> x70, starting transfers between devices: 67.3 us -> 86.1 us  [exchange(): return lax.ppermute(value, axis, pairs)]
    add x19 -> x2, other arithmetic: 15.4 us -> 0.1 us  [the longest x1 0.08 us: ada_back(): done.gains = sum_small(gain_sums[0] + gain_sums[1], 'mp')]
  transfers between devices with their start and end apart: 71 -> 75, of which waited for: 40 -> 26; matrix products, arithmetic and copies ran while one was open for 28% -> 11% of each run, Pallas kernels for 0% -> 23%
where the time goes in v2:
time: 460 us; the launch traced here: 455 us
  Pallas kernels  159 us (35%)
  waiting for transfers between devices  116 us (25%)
  starting transfers between devices  99.9 us (22%)
  local copies, waits for them, and re-layouts  39.7 us (9%)
  other arithmetic  25.8 us (6%)
  matrix products  11.3 us (2%)
    pallas_call x38, Pallas kernels, call(): pl.pallas_call(kernel, grid_spec=pltpu.PrefetchScalarGridSpec(num_scalar_...  157 us
    ppermute x70, waiting for transfers between devices, exchange(): return lax.ppermute(value, axis, pairs)  114 us
    ppermute x70, starting transfers between devices, exchange(): return lax.ppermute(value, axis, pairs)  86.1 us
    unnamed x170, local copies, waits for them, and re-layouts  30.2 us
    ppermute x5, starting transfers between devices, shifted(): return lax.ppermute(value, axis, pairs)  13.8 us
    dot_general x3, matrix products, einsum(): return jnp.einsum(spec, *operands, preferred_element_type=F32)  11.3 us
    select_n x22, other arithmetic, in_order(): jnp.where(later, join([other, mine], axis=axis), join([mine, other], axis...  10 us
  transfers between devices with their start and end apart: 75, of which 26 were waited for; matrix products, arithmetic and copies ran while one was open for 11% of the time, Pallas kernels for 23%

profile of v2, /device:TPU:0, one launch (start us, length us, event | category | flops | bytes accessed | tf_op | source)
XLA Modules:
  0.0 454.5 jit_solution(504336117457712724)
XLA Ops:
  2.8 4.9 %collective-permute-start.5 = (bf16[4,288]{1,0:T(4,128)(2,1)S(1)}, bf16[4,288]{1,0:T(4,128)(2,1)S(1)}, u32[]{:S(2)}, u32[]{:S(2)}) collective-permute-start(bf16[4,288]{1,0:T(4,128)(2,1)S(1)} %select_convert_fusion), channel_id=1, source_target_pairs={{0,4},{4,8},{8,12},{12,16},{16,20},{20,24},{24,28},{1,5},{5,9},{9,... | collective-permute-start | bytes 6920 | tf_op jit(solution)/shard_map/ppermute | solution.py:33
  29.0 4.6 %copy.76 = bf16[144,8,2,768]{3,1,2,0:T(8,128)(2,1)} copy(bf16[144,8,2,768]{3,2,1,0:T(2,128)(2,1)} %bitcast.79) | data formatting | bytes 7077888
  48.6 10.1 %collective-permute-done.9.p2.r2 = bf16[4,288,256]{2,1,0:T(8,128)(2,1)S(1)} collective-permute-done((bf16[4,288,256]{2,1,0:T(8,128)(2,1)S(1)}, bf16[4,288,256]{2,1,0:T(8,128)(2,1)S(1)}, u32[]{:S(2)}, u32[]{:S(2)}) %collective-permute-start.9) | collective-permute-done | bytes 589856 | tf_op jit(solution)/shard_map/ppermute | solution.py:27
  60.9 7.0 %shard_map.220.wup_t = bf16[1536,1152]{1,0:T(8,128)(2,1)S(1)} custom-call(s32[1]{0:T(128)} %bitcast.5.s_ref.me_ref, bf16[1152,1536]{1,0:T(8,128)(2,1)} %bitcast.76), custom_call_target="tpu_custom_call" | custom-call | flops 300000000 | bytes 1000 | tf_op jit(solution)/shard_map/pallas_call | solution.py:81
  73.2 19.3 %shard_map.222 = (bf16[4,288,256]{2,1,0:T(8,128)(2,1)}, bf16[4,288,256]{2,1,0:T(8,128)(2,1)}, f32[4,288,256]{2,1,0:T(8,128)}, f32[4,288,256]{2,1,0:T(8,128)}, bf...) custom-call(s32[1]{0:T(128)} %bitcast.5.s_ref.me_ref, ...), custom_call_target="tpu_custom_call" | custom-call | flops 1800000000 | bytes 1000 | tf_op jit(solution)/shard_map/pallas_call | solution.py:81
  99.4 14.1 %collective-permute-done.15.across = bf16[4,288,256]{2,1,0:T(8,128)(2,1)S(1)} collective-permute-done((bf16[4,288,256]{2,1,0:T(8,128)(2,1)S(1)}, bf16[4,288,256]{2,1,0:T(8,128)(2,1)S(1)}, u32[]{:S(2)}, u32[]{:S(2)}) %collective-permute-start.15) | collective-permute-done | bytes 589856 | tf_op jit(solution)/shard_map/ppermute | solution.py:27
  119.9 6.2 %collective-permute-done.20.g2 = bf16[4,288,256]{2,1,0:T(8,128)(2,1)S(1)} collective-permute-done((bf16[4,288,256]{2,1,0:T(8,128)(2,1)S(1)}, bf16[4,288,256]{2,1,0:T(8,128)(2,1)S(1)}, u32[]{:S(2)}, u32[]{:S(2)}) %collective-permute-start.20) | collective-permute-done | bytes 589856 | tf_op jit(solution)/shard_map/ppermute | solution.py:27
  126.7 11.3 %collective-permute-done.17.p2 = bf16[4,288,256]{2,1,0:T(8,128)(2,1)S(1)} collective-permute-done((bf16[4,288,256]{2,1,0:T(8,128)(2,1)S(1)}, bf16[4,288,256]{2,1,0:T(8,128)(2,1)S(1)}, u32[]{:S(2)}, u32[]{:S(2)}) %collective-permute-start.17) | collective-permute-done | bytes 589856 | tf_op jit(solution)/shard_map/ppermute | solution.py:27
  140.8 24.7 %shard_map.225 = (bf16[4,288,256]{2,1,0:T(8,128)(2,1)}, bf16[4,288,256]{2,1,0:T(8,128)(2,1)}, f32[4,288,256]{2,1,0:T(8,128)}, f32[4,288,256]{2,1,0:T(8,128)}, bf...) custom-call(s32[1]{0:T(128)} %bitcast.5.s_ref.me_ref, ...), custom_call_target="tpu_custom_call" | custom-call | flops 2400000000 | bytes 1000 | tf_op jit(solution)/shard_map/pallas_call | solution.py:81
  181.2 5.2 %shard_map.228 = (bf16[1,288,1536]{2,1,0:T(8,128)(2,1)}, f32[1,288,1536]{2,1,0:T(8,128)S(1)}) custom-call(s32[1]{0:T(128)} %bitcast.7.s_ref, bf16[1152,1024]{1,0:T(8,128)(2,1)S(1)} %copy-done.4, bf16[1536,1024]{1,0:T(8,128)(2,1)} %get-tuple-element.360.refs_1_), custom_call_target="tpu_custom_call" | custom-call | flops 300000000 | bytes 1000 | tf_op jit(solution)/shard_map/pallas_call | solution.py:81
  187.5 5.4 %shard_map.229 = (bf16[1,288,1536]{2,1,0:T(8,128)(2,1)}, f32[1,288,1536]{2,1,0:T(8,128)S(1)}) custom-call(s32[1]{0:T(128)} %bitcast.6.s_ref, bf16[1152,1024]{1,0:T(8,128)(2,1)S(1)} %copy-done.4, bf16[1536,1024]{1,0:T(8,128)(2,1)} %get-tuple-element.360.refs_1_), custom_call_target="tpu_custom_call" | custom-call | flops 300000000 | bytes 1000 | tf_op jit(solution)/shard_map/pallas_call | solution.py:81
  194.1 4.7 %shard_map.230 = (f32[4,288,256]{2,1,0:T(8,128)S(1)}, bf16[4,288,256]{2,1,0:T(8,128)(2,1)}, f32[4,288,128]{2,1,0:T(8,128)S(1)}) custom-call(s32[1]{0:T(128)} %bitcast.5.s_ref.me_ref, bf16[4,304,256]{2,1,0:T(8,128)(2,1)S(1)} %copy-done.19, bf16[4,304,256]{2,1,0:T(8,128)(2,1)} %collective-permute-done.22.far_core, f32[4,288,256]{2,1,0:T(8,128)S(1)} %copy-done.31, ...), custom_call_target="tpu_custom_call" | custom-call | flops 300000000 | bytes 1000 | tf_op jit(solution)/shard_map/pallas_call | solution.py:81
  204.3 10.5 %collective-permute-done.30.p2 = bf16[4,288,256]{2,1,0:T(8,128)(2,1)} collective-permute-done((bf16[4,288,256]{2,1,0:T(8,128)(2,1)}, bf16[4,288,256]{2,1,0:T(8,128)(2,1)}, u32[]{:S(2)}, u32[]{:S(2)}) %collective-permute-start.30) | collective-permute-done | bytes 589856 | tf_op jit(solution)/shard_map/ppermute | solution.py:27
  236.7 18.5 %shard_map.235 = (bf16[4,288,256]{2,1,0:T(8,128)(2,1)}, bf16[4,304,256]{2,1,0:T(8,128)(2,1)}, f32[4,288,256]{2,1,0:T(8,128)}, f32[4,288,256]{2,1,0:T(8,128)}, bf...) custom-call(s32[1]{0:T(128)} %bitcast.5.s_ref.me_ref, ...), custom_call_target="tpu_custom_call" | custom-call | flops 1800000000 | bytes 1000 | tf_op jit(solution)/shard_map/pallas_call | solution.py:81
  263.6 8.2 %shard_map.238 = (bf16[2,144,1152]{2,1,0:T(8,128)(2,1)S(1)}, f32[2,144,1152]{2,1,0:T(8,128)S(1)}, bf16[2,144,1152]{2,1,0:T(8,128)(2,1)}, f32[2,144,1152]{2,1,0:T(8,128)S(1)}) custom-call(s32[2]{0:T(128)S(1)} %pad_add_fusion.1.s_ref, bf16[864,1024]{1,0:T(8,128)(2,1)} %get-tuple-element.423.refs_0_, bf16[288,1024]{1,0:T(8,128)(2,1)S(1)} %copy-done.41, ...), custom_call_target="tpu_custom_call" | custom-call | flops 300000000 | bytes 1000 | tf_op jit(solution)/shard_map/pallas_call | solution.py:81
  283.6 5.9 %collective-permute-done.39 = bf16[1,72,1536]{2,1,0:T(8,128)(2,1)S(1)} collective-permute-done((bf16[1,72,1536]{2,1,0:T(8,128)(2,1)S(1)}, bf16[1,72,1536]{2,1,0:T(8,128)(2,1)S(1)}, u32[]{:S(2)}, u32[]{:S(2)}) %collective-permute-start.39) | collective-permute-done | bytes 221216 | tf_op jit(solution)/shard_map/ppermute | solution.py:27
  296.8 16.1 %collective-permute-done.41.got_a.got_b = bf16[2,144,1152]{2,1,0:T(8,128)(2,1)S(1)} collective-permute-done((bf16[2,144,1152]{2,1,0:T(8,128)(2,1)}, bf16[2,144,1152]{2,1,0:T(8,128)(2,1)S(1)}, u32[]{:S(2)}, u32[]{:S(2)}) %collective-permute-start.41) | collective-permute-done | bytes 663584 | tf_op jit(solution)/shard_map/ppermute | solution.py:27
  346.0 10.3 %collective-permute-done.52 = bf16[1,144,1536]{2,1,0:T(8,128)(2,1)S(1)} collective-permute-done((bf16[1,144,1536]{2,1,0:T(8,128)(2,1)S(1)}, bf16[1,144,1536]{2,1,0:T(8,128)(2,1)S(1)}, u32[]{:S(2)}, u32[]{:S(2)}) %collective-permute-start.52) | collective-permute-done | bytes 442400 | tf_op jit(solution)/shard_map/ppermute | solution.py:27
  359.3 10.2 %collective-permute-start.58 = (bf16[1,192,1152]{2,1,0:T(8,128)(2,1)S(1)}, bf16[1,192,1152]{2,1,0:T(8,128)(2,1)S(1)}, u32[]{:S(2)}, u32[]{:S(2)}) collective-permute-start(bf16[1,192,1152]{2,1,0:T(8,128)(2,1)S(1)} %maximum_select_fusion.7), channel_id=1, source_target_pairs={{0,8},{4,12},{8,0},{12,4},{16,24},{20,28},{24,16},{28,20},{1,9},{5... | collective-permute-start | bytes 1327112 | tf_op jit(solution)/shard_map/ppermute | solution.py:27
  373.2 5.7 %collective-permute-start.60 = (bf16[4,25,288]{2,1,0:T(8,128)(2,1)S(1)}, bf16[4,25,288]{2,1,0:T(8,128)(2,1)S(1)}, u32[]{:S(2)}, u32[]{:S(2)}) collective-permute-start(bf16[4,25,288]{2,1,0:T(8,128)(2,1)S(1)} %maximum_select_fusion.14), channel_id=1, source_target_pairs={{0,16},{4,20},{8,24},{12,28},{16,0},{20,4},{24,8},{28,12},{1,17},{... | collective-permute-start | bytes 172808 | tf_op jit(solution)/shard_map/ppermute | solution.py:27
  382.6 10.8 %collective-permute-start.66 = (bf16[1,288,1536]{2,1,0:T(8,128)(2,1)S(1)}, bf16[1,288,1536]{2,1,0:T(8,128)(2,1)S(1)}, u32[]{:S(2)}, u32[]{:S(2)}) collective-permute-start(bf16[1,288,1536]{2,1,0:T(8,128)(2,1)S(1)} %maximum_select_fusion.refs_0_), channel_id=1, source_target_pairs={{0,4},{4,0},{8,12},{12,8},{16,20},{20,16},{24,28},{28,24},{1,5},{5... | collective-permute-start | bytes 2654216 | tf_op jit(solution)/shard_map/ppermute | solution.py:27
  402.6 4.5 fusion.1
  420.9 7.1 %shard_map.249 = f32[1152,2,768]{2,1,0:T(2,128)} custom-call(s32[2]{0:T(128)S(1)} %pad_add_fusion.1.s_ref, bf16[1,288,1536]{2,1,0:T(8,128)(2,1)S(1)} %maximum_select_fusion.refs_0_, bf16[1,288,1536]{2,1,0:T(8,128)(2,1)S(1)} %collective-permute-done.66.refs_1_, bf16[1,288,1536]{2,1,0:T(8,128)(2,1)S(1)} %maximum_select_fusion.1.refs_2_, ...), custom_call_target="tpu_custom_call" | custom-call | flops 300000000 | bytes 1000 | tf_op jit(solution)/shard_map/pallas_call | solution.py:81
  449.3 4.7 %shard_map.251 = (f32[3,288,1152]{2,1,0:T(8,128)}, f32[288,1152]{1,0:T(8,128)}) custom-call(s32[2]{0:T(128)S(1)} %pad_add_fusion.1.s_ref, bf16[2,144,1152]{2,1,0:T(8,128)(2,1)S(1)} %maximum_select_fusion.3.mine1, bf16[2,144,1152]{2,1,0:T(8,128)(2,1)S(1)} %collective-permute-done.71.other1, bf16[2,144,1152]{2,1,0:T(8,128)(2,1)S(1)} %maximum_select_fusion.4.mine2, ...), custom_call_target="tpu_custom_call" | custom-call | flops 300000000 | bytes 1000 | tf_op jit(solution)/shard_map/pallas_call | solution.py:81
  (426 shorter events, 221.1 us)
Async XLA Ops:
  44.2 25.6 %collective-permute-start.4 = (bf16[4,288,256]{2,1,0:T(8,128)(2,1)S(1)}, bf16[4,288,256]{2,1,0:T(8,128)(2,1)S(1)}, u32[]{:S(2)}, u32[]{:S(2)}) collective-permute-start(bf16[4,288,256]{2,1,0:T(8,128)(2,1)S(1)} %shard_map.218), channel_id=1, source_target_pairs={{0,4},{4,8},{8,12},{12,16},{16,20},{20,24},{24,28},{1,5},{5,9},{9,... | collective-permute-start | bytes 1769480 | tf_op jit(solution)/shard_map/ppermute | solution.py:33
  98.9 27.3 %collective-permute-start.20 = (bf16[4,288,256]{2,1,0:T(8,128)(2,1)S(1)}, bf16[4,288,256]{2,1,0:T(8,128)(2,1)S(1)}, u32[]{:S(2)}, u32[]{:S(2)}) collective-permute-start(bf16[4,288,256]{2,1,0:T(8,128)(2,1)S(1)} %get-tuple-element.326.g0), channel_id=1, source_target_pairs={{0,2},{1,3},{2,0},{3,1},{4,6},{5,7},{6,4},{7,5},{8,10},{9,11},{10,... | collective-permute-start | bytes 1769480 | tf_op jit(solution)/shard_map/ppermute | solution.py:27
  179.2 24.5 %collective-permute-start.63 = (bf16[8,8,288]{2,1,0:T(8,128)(2,1)S(1)}, bf16[8,8,288]{2,1,0:T(8,128)(2,1)S(1)}, u32[]{:S(2)}, u32[]{:S(2)}) collective-permute-start(bf16[8,8,288]{2,1,0:T(8,128)(2,1)S(1)} %get-tuple-element.537), channel_id=1, source_target_pairs={{0,1},{1,0},{2,3},{3,2},{4,5},{5,4},{6,7},{7,6},{8,9},{9,8},{10,11... | collective-permute-start | bytes 110600 | tf_op jit(solution)/shard_map/ppermute | solution.py:27
  186.4 29.1 %collective-permute-start.26 = (bf16[1,288,1536]{2,1,0:T(8,128)(2,1)}, bf16[1,288,1536]{2,1,0:T(8,128)(2,1)S(1)}, u32[]{:S(2)}, u32[]{:S(2)}) collective-permute-start(bf16[1,288,1536]{2,1,0:T(8,128)(2,1)} %get-tuple-element.357), channel_id=1, source_target_pairs={{0,8},{4,12},{8,0},{12,4},{16,24},{20,28},{24,16},{28,20},{1,9},{5... | collective-permute-start | bytes 2654216 | tf_op jit(solution)/shard_map/ppermute | solution.py:27
  200.8 29.6 %collective-permute-start.28 = (bf16[1,288,1536]{2,1,0:T(8,128)(2,1)}, bf16[1,288,1536]{2,1,0:T(8,128)(2,1)}, u32[]{:S(2)}, u32[]{:S(2)}) collective-permute-start(bf16[1,288,1536]{2,1,0:T(8,128)(2,1)} %get-tuple-element.361), channel_id=1, source_target_pairs={{0,4},{4,0},{8,12},{12,8},{16,20},{20,16},{24,28},{28,24},{1,5},{5... | collective-permute-start | bytes 2654216 | tf_op jit(solution)/shard_map/ppermute | solution.py:27
  203.0 31.2 %collective-permute-start.29 = (bf16[4,288,256]{2,1,0:T(8,128)(2,1)}, bf16[4,288,256]{2,1,0:T(8,128)(2,1)}, u32[]{:S(2)}, u32[]{:S(2)}) collective-permute-start(bf16[4,288,256]{2,1,0:T(8,128)(2,1)} %get-tuple-element.392.p0), channel_id=1, source_target_pairs={{0,1},{1,0},{2,3},{3,2},{4,5},{5,4},{6,7},{7,6},{8,9},{9,8},{10,11... | collective-permute-start | bytes 1769480 | tf_op jit(solution)/shard_map/ppermute | solution.py:27
  220.4 34.8 %collective-permute-start.32 = (bf16[1,144,1536]{2,1,0:T(8,128)(2,1)}, bf16[1,144,1536]{2,1,0:T(8,128)(2,1)}, u32[]{:S(2)}, u32[]{:S(2)}) collective-permute-start(bf16[1,144,1536]{2,1,0:T(8,128)(2,1)} %get-tuple-element.382), channel_id=1, source_target_pairs={{0,4},{4,0},{8,12},{12,8},{16,20},{20,16},{24,28},{28,24},{1,5},{5... | collective-permute-start | bytes 1327112 | tf_op jit(solution)/shard_map/ppermute | solution.py:27
  224.6 47.3 %collective-permute-start.34 = (bf16[1,192,1152]{2,1,0:T(8,128)(2,1)}, bf16[1,192,1152]{2,1,0:T(8,128)(2,1)}, u32[]{:S(2)}, u32[]{:S(2)}) collective-permute-start(bf16[1,192,1152]{2,1,0:T(8,128)(2,1)} %copy-done.57), channel_id=1, source_target_pairs={{0,8},{4,12},{8,0},{12,4},{16,24},{20,28},{24,16},{28,20},{1,9},{5... | collective-permute-start | bytes 1327112 | tf_op jit(solution)/shard_map/ppermute | solution.py:27
  230.4 47.3 %collective-permute-start.36 = (bf16[4,288,256]{2,1,0:T(8,128)(2,1)}, bf16[4,288,256]{2,1,0:T(8,128)(2,1)}, u32[]{:S(2)}, u32[]{:S(2)}) collective-permute-start(bf16[4,288,256]{2,1,0:T(8,128)(2,1)} %get-tuple-element.438), channel_id=1, source_target_pairs={{0,1},{1,0},{2,3},{3,2},{4,5},{5,4},{6,7},{7,6},{8,9},{9,8},{10,11... | collective-permute-start | bytes 1769480 | tf_op jit(solution)/shard_map/ppermute | solution.py:27
  234.2 43.6 %collective-permute-start.37 = (bf16[4,288,256]{2,1,0:T(8,128)(2,1)}, bf16[4,288,256]{2,1,0:T(8,128)(2,1)}, u32[]{:S(2)}, u32[]{:S(2)}) collective-permute-start(bf16[4,288,256]{2,1,0:T(8,128)(2,1)} %shard_map.233), channel_id=1, source_target_pairs={{0,2},{1,3},{2,0},{3,1},{4,6},{5,7},{6,4},{7,5},{8,10},{9,11},{10,... | collective-permute-start | bytes 1769480 | tf_op jit(solution)/shard_map/ppermute | solution.py:27
  275.4 47.9 %collective-permute-start.44 = (bf16[1,96,1152]{2,1,0:T(8,128)(2,1)S(1)}, bf16[1,96,1152]{2,1,0:T(8,128)(2,1)}, u32[]{:S(2)}, u32[]{:S(2)}) collective-permute-start(bf16[1,96,1152]{2,1,0:T(8,128)(2,1)S(1)} %get-tuple-element.433), channel_id=1, source_target_pairs={{0,16},{4,20},{8,24},{12,28},{16,0},{20,4},{24,8},{28,12},{1,17},{... | collective-permute-start | bytes 663560 | tf_op jit(solution)/shard_map/ppermute | solution.py:27
  277.7 37.4 %collective-permute-start.42 = (bf16[4,288,256]{2,1,0:T(8,128)(2,1)}, bf16[4,288,256]{2,1,0:T(8,128)(2,1)S(1)}, u32[]{:S(2)}, u32[]{:S(2)}) collective-permute-start(bf16[4,288,256]{2,1,0:T(8,128)(2,1)} %get-tuple-element.408), channel_id=1, source_target_pairs={{0,1},{1,0},{2,3},{3,2},{4,5},{5,4},{6,7},{7,6},{8,9},{9,8},{10,11... | collective-permute-start | bytes 1769480 | tf_op jit(solution)/shard_map/ppermute | solution.py:27
  281.2 31.6 %collective-permute-start.41 = (bf16[2,144,1152]{2,1,0:T(8,128)(2,1)}, bf16[2,144,1152]{2,1,0:T(8,128)(2,1)S(1)}, u32[]{:S(2)}, u32[]{:S(2)}) collective-permute-start(bf16[2,144,1152]{2,1,0:T(8,128)(2,1)} %get-tuple-element.429), channel_id=1, source_target_pairs={{0,8},{4,12},{8,0},{12,4},{16,24},{20,28},{24,16},{28,20},{1,9},{5... | collective-permute-start | bytes 1990664 | tf_op jit(solution)/shard_map/ppermute | solution.py:27
  289.5 27.4 %collective-permute-start.43 = (bf16[4,304,256]{2,1,0:T(8,128)(2,1)S(1)}, bf16[4,304,256]{2,1,0:T(8,128)(2,1)S(1)}, u32[]{:S(2)}, u32[]{:S(2)}) collective-permute-start(bf16[4,304,256]{2,1,0:T(8,128)(2,1)S(1)} %shard_map.240), channel_id=1, source_target_pairs={{0,2},{1,3},{2,0},{3,1},{4,6},{5,7},{6,4},{7,5},{8,10},{9,11},{10,... | collective-permute-start | bytes 1867784 | tf_op jit(solution)/shard_map/ppermute | solution.py:27
  295.1 38.0 %collective-permute-start.48 = (bf16[1,72,1536]{2,1,0:T(8,128)(2,1)}, bf16[1,72,1536]{2,1,0:T(8,128)(2,1)}, u32[]{:S(2)}, u32[]{:S(2)}) collective-permute-start(bf16[1,72,1536]{2,1,0:T(8,128)(2,1)} %add_convert_fusion.1), channel_id=1, source_target_pairs={{0,16},{4,20},{8,24},{12,28},{16,0},{20,4},{24,8},{28,12},{1,17},{... | collective-permute-start | bytes 663560 | tf_op jit(solution)/shard_map/ppermute | solution.py:27
  336.2 46.4 %collective-permute-start.56 = (bf16[1,72,1152]{2,1,0:T(8,128)(2,1)S(1)}, bf16[1,72,1152]{2,1,0:T(8,128)(2,1)S(1)}, u32[]{:S(2)}, u32[]{:S(2)}) collective-permute-start(bf16[1,72,1152]{2,1,0:T(8,128)(2,1)S(1)} %get-tuple-element.486), channel_id=1, source_target_pairs={{0,16},{4,20},{8,24},{12,28},{16,0},{20,4},{24,8},{28,12},{1,17},{... | collective-permute-start | bytes 497672 | tf_op jit(solution)/shard_map/ppermute | solution.py:27
  344.6 28.5 %collective-permute-start.55 = (bf16[4,288,256]{2,1,0:T(8,128)(2,1)S(1)}, bf16[4,288,256]{2,1,0:T(8,128)(2,1)S(1)}, u32[]{:S(2)}, u32[]{:S(2)}) collective-permute-start(bf16[4,288,256]{2,1,0:T(8,128)(2,1)S(1)} %copy-done.56), channel_id=1, source_target_pairs={{4,0},{8,4},{12,8},{16,12},{20,16},{24,20},{28,24},{5,1},{9,5},{13... | collective-permute-start | bytes 1769480 | tf_op jit(solution)/shard_map/ppermute | solution.py:33
  356.3 37.9 %collective-permute-start.57 = (bf16[1,144,1536]{2,1,0:T(8,128)(2,1)S(1)}, bf16[1,144,1536]{2,1,0:T(8,128)(2,1)S(1)}, u32[]{:S(2)}, u32[]{:S(2)}) collective-permute-start(bf16[1,144,1536]{2,1,0:T(8,128)(2,1)S(1)} %maximum_select_fusion.6), channel_id=1, source_target_pairs={{0,4},{4,0},{8,12},{12,8},{16,20},{20,16},{24,28},{28,24},{1,5},{5... | collective-permute-start | bytes 1327112 | tf_op jit(solution)/shard_map/ppermute | solution.py:27
  357.3 40.8 %collective-permute-start.59 = (bf16[1,72,1152]{2,1,0:T(8,128)(2,1)S(1)}, bf16[1,72,1152]{2,1,0:T(8,128)(2,1)S(1)}, u32[]{:S(2)}, u32[]{:S(2)}) collective-permute-start(bf16[1,72,1152]{2,1,0:T(8,128)(2,1)S(1)} %add_convert_fusion.4), channel_id=1, source_target_pairs={{0,16},{4,20},{8,24},{12,28},{16,0},{20,4},{24,8},{28,12},{1,17},{... | collective-permute-start | bytes 497672 | tf_op jit(solution)/shard_map/ppermute | solution.py:27
  359.3 38.6 %collective-permute-start.58 = (bf16[1,192,1152]{2,1,0:T(8,128)(2,1)S(1)}, bf16[1,192,1152]{2,1,0:T(8,128)(2,1)S(1)}, u32[]{:S(2)}, u32[]{:S(2)}) collective-permute-start(bf16[1,192,1152]{2,1,0:T(8,128)(2,1)S(1)} %maximum_select_fusion.7), channel_id=1, source_target_pairs={{0,8},{4,12},{8,0},{12,4},{16,24},{20,28},{24,16},{28,20},{1,9},{5... | collective-permute-start | bytes 1327112 | tf_op jit(solution)/shard_map/ppermute | solution.py:27
  373.2 25.9 %collective-permute-start.60 = (bf16[4,25,288]{2,1,0:T(8,128)(2,1)S(1)}, bf16[4,25,288]{2,1,0:T(8,128)(2,1)S(1)}, u32[]{:S(2)}, u32[]{:S(2)}) collective-permute-start(bf16[4,25,288]{2,1,0:T(8,128)(2,1)S(1)} %maximum_select_fusion.14), channel_id=1, source_target_pairs={{0,16},{4,20},{8,24},{12,28},{16,0},{20,4},{24,8},{28,12},{1,17},{... | collective-permute-start | bytes 172808 | tf_op jit(solution)/shard_map/ppermute | solution.py:27
  382.6 34.3 %collective-permute-start.66 = (bf16[1,288,1536]{2,1,0:T(8,128)(2,1)S(1)}, bf16[1,288,1536]{2,1,0:T(8,128)(2,1)S(1)}, u32[]{:S(2)}, u32[]{:S(2)}) collective-permute-start(bf16[1,288,1536]{2,1,0:T(8,128)(2,1)S(1)} %maximum_select_fusion.refs_0_), channel_id=1, source_target_pairs={{0,4},{4,0},{8,12},{12,8},{16,20},{20,16},{24,28},{28,24},{1,5},{5... | collective-permute-start | bytes 2654216 | tf_op jit(solution)/shard_map/ppermute | solution.py:27
  398.1 31.7 %collective-permute-start.68 = (bf16[1,384,1152]{2,1,0:T(8,128)(2,1)S(1)}, bf16[1,384,1152]{2,1,0:T(8,128)(2,1)}, u32[]{:S(2)}, u32[]{:S(2)}) collective-permute-start(bf16[1,384,1152]{2,1,0:T(8,128)(2,1)S(1)} %maximum_select_fusion.2.refs_0_), channel_id=1, source_target_pairs={{0,4},{4,0},{8,12},{12,8},{16,20},{20,16},{24,28},{28,24},{1,5},{5... | collective-permute-start | bytes 2654216 | tf_op jit(solution)/shard_map/ppermute | solution.py:27
  399.1 38.1 %collective-permute-start.70 = (bf16[2,72,1152]{2,1,0:T(8,128)(2,1)}, bf16[2,72,1152]{2,1,0:T(8,128)(2,1)}, u32[]{:S(2)}, u32[]{:S(2)}) collective-permute-start(bf16[2,72,1152]{2,1,0:T(8,128)(2,1)} %maximum_select_fusion.8), channel_id=1, source_target_pairs={{0,4},{4,0},{8,12},{12,8},{16,20},{20,16},{24,28},{28,24},{1,5},{5... | collective-permute-start | bytes 995336 | tf_op jit(solution)/shard_map/ppermute | solution.py:27
  (133 other events, 1375.3 us)

commit v3 on v2

--- a/solution.py
+++ b/solution.py
@@ -73,7 +73,7 @@
     return [piece, core, over, both]
 
 
-def call(kernel, grid, scalars, ins, outs, scratch=(), vmem=48, us=3.0):
+def call(kernel, grid, scalars, ins, outs, scratch=(), vmem=24, us=3.0):
     in_specs = [
         pl.BlockSpec(block, index, pipeline_mode=pl.Buffered(1)) if whole else pl.BlockSpec(block, index)
         for _, block, index, whole in ins
@@ -897,8 +897,9 @@
             ),
             *st.pieces_one, st.mods_full, wqkv, weights.proj_t, gains, cos, sin,
         )
-        st.far_core = exchange(st.far, "mp", 1)
-        st.core = exchange(st.near, "mp", 1)
+        far, near, _ = lax.optimization_barrier((st.far, st.near, st.pieces_grad_two[2]))
+        st.far_core = exchange(far, "mp", 1)
+        st.core = exchange(near, "mp", 1)
 
     def choose_cot(p):
         start, images = parts[p]
@@ -1076,11 +1077,11 @@
     def each(field):
         return [field(st) for st in state]
 
-    attn1 = Reduction(order)
-    attn2 = Reduction(order, True)
-    up1 = Reduction(order)
-    up2 = Reduction(order, True)
-    down = Reduction(order, False)
+    attn1 = Reduction(order, True)
+    attn2 = Reduction(order, False)
+    up1 = Reduction(order, False)
+    up2 = Reduction(order, False)
+    down = Reduction(order, True)
 
     def attention_weights():
         indices = jnp.concatenate([attn1.first(), attn2.first()])
@@ -1137,11 +1138,13 @@
 
     done = types.SimpleNamespace()
 
-    def send_back(p):
-        st = state[p]
-        result_out, latent_out, _ = lax.optimization_barrier((st.result_out, st.latent_out, order.last))
-        st.result_back = shifted(result_out, "dp", -1)
-        st.latent_back = shifted(latent_out, "dp", -1)
+    def send_result(p):
+        out, _ = lax.optimization_barrier((state[p].result_out, order.last))
+        state[p].result_back = shifted(out, "dp", -1)
+
+    def send_latent(p):
+        out, _ = lax.optimization_barrier((state[p].latent_out, order.last))
+        state[p].latent_back = shifted(out, "dp", -1)
 
     def modulation_back():
         columns_one, columns_two, columns_three = (
@@ -1212,59 +1215,60 @@
 
     prepare()
     choose_rows(0)
-    prepare_up()
     choose_cot(0)
     attention(0)
     relay_one(0)
+    prepare_up()
     middle(0)
     mlp(0)
+    relay_three(0)
+    begin(up1)
     begin(down)
-    relay_three(0)
     begin(up2)
-    begin(up1)
     middle_back(0)
+    halve(up1, 1)
+    result_core(0)
     halve(down, 1)
-    result_core(0)
+    relay_two(0)
     halve(up2, 1)
-    relay_two(0)
-    halve(up1, 1)
+    halve(up1, 2)
     attention_back(0)
+    join(up1)
+    halve(down, 2)
+    attention_weights()
     halve(up2, 2)
-    halve(up1, 2)
-    attention_weights()
-    halve(down, 2)
     relay_four(0)
+    double(up1, 0)
     result(0)
-    join(up1)
-    join(up2)
+    send_result(0)
+    join(down)
     halve(attn1, 1)
     halve(attn2, 1)
     last(0)
-    join(down)
+    send_latent(0)
+    join(up2)
+    double(up1, 1)
     modulation_back()
-    halve(attn2, 2)
-    double(up1, 0)
-    modulation_step()
-    send_back(0)
-    double(up2, 0)
+    home_result()
     halve(attn1, 2)
     double(down, 0)
+    halve(attn2, 2)
+    home_latent()
+    double(up2, 0)
+    join(attn1)
+    modulation_step()
     join(attn2)
-    double(up1, 1)
+    double(down, 1)
+    double(up2, 1)
     modulation_step()
-    home_result()
-    home_latent()
-    join(attn1)
-    double(up2, 1)
-    double(down, 1)
+    double(attn1, 0)
     double(attn2, 0)
+    finish_down()
+    finish_up()
+    double(attn1, 1)
+    double(attn2, 1)
     modulation_step()
     ada_back()
-    double(attn1, 0)
-    finish_up()
-    finish_down()
-    double(attn1, 1)
-    double(attn2, 1)
     finish_attention()
     return (
         done.output.transpose(0, 2, 1),

time: 460 us -> 434 us (0.943)
  Pallas kernels: 159 us -> 141 us
  waiting for transfers between devices: 116 us -> 133 us
  starting transfers between devices: 99.9 us -> 88.8 us
  other arithmetic: 25.8 us -> 16.7 us
    ppermute x5, waiting for transfers between devices: 1.94 us -> 27.1 us  [shifted(): return lax.ppermute(value, axis, pairs)]
    pallas_call x38, Pallas kernels: 157 us -> 139 us  [call(): pl.pallas_call(kernel, grid_spec=pltpu.PrefetchScalarGridSpec(num_scalar_...]
    ppermute x70, starting transfers between devices: 86.1 us -> 74.1 us  [exchange(): return lax.ppermute(value, axis, pairs)]
    ppermute x70, waiting for transfers between devices: 114 us -> 106 us  [exchange(): return lax.ppermute(value, axis, pairs)]
    unnamed x170 -> x162, local copies, waits for them, and re-layouts: 30.2 us -> 29.9 us
  transfers between devices with their start and end apart: 75 -> 75, of which waited for: 26 -> 21; matrix products, arithmetic and copies ran while one was open for 11% -> 8% of each run, Pallas kernels for 23% -> 25%
where the time goes in v3:
time: 434 us; the launch traced here: 429 us
  Pallas kernels  141 us (32%)
  waiting for transfers between devices  133 us (31%)
  starting transfers between devices  88.8 us (20%)
  local copies, waits for them, and re-layouts  36.3 us (8%)
  other arithmetic  16.7 us (4%)
  matrix products  10.7 us (2%)
    pallas_call x38, Pallas kernels, call(): pl.pallas_call(kernel, grid_spec=pltpu.PrefetchScalarGridSpec(num_scalar_...  139 us
    ppermute x70, waiting for transfers between devices, exchange(): return lax.ppermute(value, axis, pairs)  106 us
    ppermute x70, starting transfers between devices, exchange(): return lax.ppermute(value, axis, pairs)  74.1 us
    unnamed x162, local copies, waits for them, and re-layouts  29.9 us
    ppermute x5, waiting for transfers between devices, shifted(): return lax.ppermute(value, axis, pairs)  27.1 us
    ppermute x5, starting transfers between devices, shifted(): return lax.ppermute(value, axis, pairs)  14.7 us
    dot_general x3, matrix products, einsum(): return jnp.einsum(spec, *operands, preferred_element_type=F32)  10.7 us
  transfers between devices with their start and end apart: 75, of which 21 were waited for; matrix products, arithmetic and copies ran while one was open for 8% of the time, Pallas kernels for 25%

profile of v3, /device:TPU:0, one launch (start us, length us, event | category | flops | bytes accessed | tf_op | source)
XLA Modules:
  0.0 429.0 jit_solution(2941724886804565981)
XLA Ops:
  2.8 4.9 %collective-permute-start.5 = (bf16[4,288]{1,0:T(4,128)(2,1)S(1)}, bf16[4,288]{1,0:T(4,128)(2,1)S(1)}, u32[]{:S(2)}, u32[]{:S(2)}) collective-permute-start(bf16[4,288]{1,0:T(4,128)(2,1)S(1)} %select_convert_fusion), channel_id=1, source_target_pairs={{0,4},{4,8},{8,12},{12,16},{16,20},{20,24},{24,28},{1,5},{5,9},{9,... | collective-permute-start | bytes 6920 | tf_op jit(solution)/shard_map/ppermute | solution.py:33
  38.7 4.2 collective-permute-start.4
  45.9 13.6 %collective-permute-done.9.p2.r2 = bf16[4,288,256]{2,1,0:T(8,128)(2,1)S(1)} collective-permute-done((bf16[4,288,256]{2,1,0:T(8,128)(2,1)S(1)}, bf16[4,288,256]{2,1,0:T(8,128)(2,1)S(1)}, u32[]{:S(2)}, u32[]{:S(2)}) %collective-permute-start.9) | collective-permute-done | bytes 589856 | tf_op jit(solution)/shard_map/ppermute | solution.py:27
  67.8 19.3 %shard_map.221 = (bf16[4,288,256]{2,1,0:T(8,128)(2,1)}, bf16[4,288,256]{2,1,0:T(8,128)(2,1)}, f32[4,288,256]{2,1,0:T(8,128)}, f32[4,288,256]{2,1,0:T(8,128)}, bf...) custom-call(s32[1]{0:T(128)} %bitcast.4.s_ref.me_ref, ...), custom_call_target="tpu_custom_call" | custom-call | flops 1800000000 | bytes 1000 | tf_op jit(solution)/shard_map/pallas_call | solution.py:81
  96.8 10.6 %collective-permute-done.16.across = bf16[4,288,256]{2,1,0:T(8,128)(2,1)S(1)} collective-permute-done((bf16[4,288,256]{2,1,0:T(8,128)(2,1)S(1)}, bf16[4,288,256]{2,1,0:T(8,128)(2,1)S(1)}, u32[]{:S(2)}, u32[]{:S(2)}) %collective-permute-start.16) | collective-permute-done | bytes 589856 | tf_op jit(solution)/shard_map/ppermute | solution.py:27
  111.6 13.5 %collective-permute-done.18.p2 = bf16[4,288,256]{2,1,0:T(8,128)(2,1)S(1)} collective-permute-done((bf16[4,288,256]{2,1,0:T(8,128)(2,1)S(1)}, bf16[4,288,256]{2,1,0:T(8,128)(2,1)S(1)}, u32[]{:S(2)}, u32[]{:S(2)}) %collective-permute-start.18) | collective-permute-done | bytes 589856 | tf_op jit(solution)/shard_map/ppermute | solution.py:27
  128.0 24.7 %shard_map.225 = (bf16[4,288,256]{2,1,0:T(8,128)(2,1)}, bf16[4,288,256]{2,1,0:T(8,128)(2,1)}, f32[4,288,256]{2,1,0:T(8,128)}, f32[4,288,256]{2,1,0:T(8,128)}, bf...) custom-call(s32[1]{0:T(128)} %bitcast.4.s_ref.me_ref, ...), custom_call_target="tpu_custom_call" | custom-call | flops 2400000000 | bytes 1000 | tf_op jit(solution)/shard_map/pallas_call | solution.py:81
  176.9 3.8 shard_map.230
  188.4 8.5 %collective-permute-done.70 = bf16[8,8,576]{2,1,0:T(8,128)(2,1)S(1)} collective-permute-done((bf16[8,8,576]{2,1,0:T(8,128)(2,1)S(1)}, bf16[8,8,576]{2,1,0:T(8,128)(2,1)S(1)}, u32[]{:S(2)}, u32[]{:S(2)}) %collective-permute-start.70) | collective-permute-done | bytes 73760 | tf_op jit(solution)/shard_map/ppermute | solution.py:27
  204.4 3.5 shard_map.233
  218.5 18.5 %shard_map.236 = (bf16[4,288,256]{2,1,0:T(8,128)(2,1)}, bf16[4,304,256]{2,1,0:T(8,128)(2,1)}, f32[4,288,256]{2,1,0:T(8,128)}, f32[4,288,256]{2,1,0:T(8,128)}, bf...) custom-call(s32[1]{0:T(128)} %bitcast.4.s_ref.me_ref, ...), custom_call_target="tpu_custom_call" | custom-call | flops 1800000000 | bytes 1000 | tf_op jit(solution)/shard_map/pallas_call | solution.py:81
  244.9 4.9 %shard_map.238 = (bf16[2,144,1152]{2,1,0:T(8,128)(2,1)S(1)}, f32[2,144,1152]{2,1,0:T(8,128)S(1)}, bf16[2,144,1152]{2,1,0:T(8,128)(2,1)S(1)}, f32[2,144,1152]{2,1,0:T(8,128)S(1)}) custom-call(s32[2]{0:T(128)S(1)} %pad_add_fusion.1.s_ref, bf16[864,1024]{1,0:T(8,128)(2,1)S(1)} %copy-done.35, bf16[288,1024]{1,0:T(8,128)(2,1)S(1)} %copy-done.53, ...), custom_call_target="tpu_custom_call" | custom-call | flops 300000000 | bytes 1000 | tf_op jit(solution)/shard_map/pallas_call | solution.py:81
  264.8 14.8 %collective-permute-done.41.got_a.got_b = bf16[2,144,1152]{2,1,0:T(8,128)(2,1)S(1)} collective-permute-done((bf16[2,144,1152]{2,1,0:T(8,128)(2,1)S(1)}, bf16[2,144,1152]{2,1,0:T(8,128)(2,1)S(1)}, u32[]{:S(2)}, u32[]{:S(2)}) %collective-permute-start.41) | collective-permute-done | bytes 663584 | tf_op jit(solution)/shard_map/ppermute | solution.py:27
  294.1 5.3 %collective-permute-done.46 = bf16[1,144,1536]{2,1,0:T(8,128)(2,1)S(1)} collective-permute-done((bf16[1,144,1536]{2,1,0:T(8,128)(2,1)S(1)}, bf16[1,144,1536]{2,1,0:T(8,128)(2,1)S(1)}, u32[]{:S(2)}, u32[]{:S(2)}) %collective-permute-start.46) | collective-permute-done | bytes 442400 | tf_op jit(solution)/shard_map/ppermute | solution.py:27
  299.7 4.9 %collective-permute-done.47.refs_1_ = bf16[4,288,256]{2,1,0:T(8,128)(2,1)S(1)} collective-permute-done((bf16[4,288,256]{2,1,0:T(8,128)(2,1)S(1)}, bf16[4,288,256]{2,1,0:T(8,128)(2,1)S(1)}, u32[]{:S(2)}, u32[]{:S(2)}) %collective-permute-start.47) | collective-permute-done | bytes 589856 | tf_op jit(solution)/shard_map/ppermute | solution.py:33
  304.6 13.6 %collective-permute-start.62 = (bf16[1,288,1536]{2,1,0:T(8,128)(2,1)S(1)}, bf16[1,288,1536]{2,1,0:T(8,128)(2,1)}, u32[]{:S(2)}, u32[]{:S(2)}) collective-permute-start(bf16[1,288,1536]{2,1,0:T(8,128)(2,1)S(1)} %maximum_select_fusion.refs_0_), channel_id=1, source_target_pairs={{0,4},{4,0},{8,12},{12,8},{16,20},{20,16},{24,28},{28,24},{1,5},{5... | collective-permute-start | bytes 2654216 | tf_op jit(solution)/shard_map/ppermute | solution.py:27
  318.3 3.7 shard_map.245
  329.3 22.2 %collective-permute-done.51.refs_1_ = bf16[4,288,256]{2,1,0:T(8,128)(2,1)} collective-permute-done((bf16[4,288,256]{2,1,0:T(8,128)(2,1)}, bf16[4,288,256]{2,1,0:T(8,128)(2,1)}, u32[]{:S(2)}, u32[]{:S(2)}) %collective-permute-start.51) | collective-permute-done | bytes 589856 | tf_op jit(solution)/shard_map/ppermute | solution.py:33
  351.6 5.4 %shard_map.248 = f32[8,288,256]{2,1,0:T(8,128)} custom-call(s32[2]{0:T(128)S(1)} %pad_add_fusion.s_ref, f32[4,288,256]{2,1,0:T(8,128)S(1)} %copy-done.49, bf16[4,288,256]{2,1,0:T(8,128)(2,1)} %collective-permute-done.51.refs_1_), custom_call_target="tpu_custom_call" | custom-call | flops 300000000 | bytes 1000 | tf_op jit(solution)/shard_map/pallas_call | solution.py:81
  365.0 10.7 %collective-permute-done.57 = bf16[1,144,1536]{2,1,0:T(8,128)(2,1)S(1)} collective-permute-done((bf16[1,144,1536]{2,1,0:T(8,128)(2,1)S(1)}, bf16[1,144,1536]{2,1,0:T(8,128)(2,1)S(1)}, u32[]{:S(2)}, u32[]{:S(2)}) %collective-permute-start.57) | collective-permute-done | bytes 442400 | tf_op jit(solution)/shard_map/ppermute | solution.py:27
  382.9 13.8 %collective-permute-done.61.refs_1_ = bf16[1,384,1152]{2,1,0:T(8,128)(2,1)S(1)} collective-permute-done((bf16[1,384,1152]{2,1,0:T(8,128)(2,1)S(1)}, bf16[1,384,1152]{2,1,0:T(8,128)(2,1)S(1)}, u32[]{:S(2)}, u32[]{:S(2)}) %collective-permute-start.61) | collective-permute-done | bytes 884768 | tf_op jit(solution)/shard_map/ppermute | solution.py:27
  401.1 7.1 %shard_map.250 = f32[1152,2,768]{2,1,0:T(2,128)} custom-call(s32[2]{0:T(128)S(1)} %pad_add_fusion.2.s_ref, bf16[1,288,1536]{2,1,0:T(8,128)(2,1)S(1)} %maximum_select_fusion.refs_0_, bf16[1,288,1536]{2,1,0:T(8,128)(2,1)} %collective-permute-done.62.refs_1_, bf16[1,288,1536]{2,1,0:T(8,128)(2,1)S(1)} %maximum_select_fusion.2.refs_2_, ...), custom_call_target="tpu_custom_call" | custom-call | flops 300000000 | bytes 1000 | tf_op jit(solution)/shard_map/pallas_call | solution.py:81
  414.3 4.5 %fusion.1 = f32[6,288,1152]{2,1,0:T(8,128)} fusion(bf16[6,32,288]{2,0,1:T(8,128)(2,1)S(1)} %bitcast.86, bf16[32,1152]{1,0:T(8,128)(2,1)S(1)} %broadcast_select_fusion), kind=kOutput, calls=%fused_computation.30 | convolution fusion | flops 127401984 | bytes 8146944 | tf_op jit(solution)/shard_map/kbf,bd->kfd/dot_general | solution.py:635
  424.0 4.7 %shard_map.251 = (f32[3,288,1152]{2,1,0:T(8,128)}, f32[288,1152]{1,0:T(8,128)}) custom-call(s32[2]{0:T(128)S(1)} %pad_add_fusion.1.s_ref, bf16[2,144,1152]{2,1,0:T(8,128)(2,1)S(1)} %maximum_select_fusion.3.mine1, bf16[2,144,1152]{2,1,0:T(8,128)(2,1)S(1)} %collective-permute-done.71.other1, bf16[2,144,1152]{2,1,0:T(8,128)(2,1)S(1)} %maximum_select_fusion.4.mine2, ...), custom_call_target="tpu_custom_call" | custom-call | flops 300000000 | bytes 1000 | tf_op jit(solution)/shard_map/pallas_call | solution.py:81
  (419 shorter events, 185.4 us)
Async XLA Ops:
  63.9 23.3 %collective-permute-start.13 = (bf16[4,288,256]{2,1,0:T(8,128)(2,1)}, bf16[4,288,256]{2,1,0:T(8,128)(2,1)}, u32[]{:S(2)}, u32[]{:S(2)}) collective-permute-start(bf16[4,288,256]{2,1,0:T(8,128)(2,1)} %get-tuple-element.330.g0), channel_id=1, source_target_pairs={{0,2},{1,3},{2,0},{3,1},{4,6},{5,7},{6,4},{7,5},{8,10},{9,11},{10,... | collective-permute-start | bytes 1769480 | tf_op jit(solution)/shard_map/ppermute | solution.py:27
  153.6 29.2 %collective-permute-start.69 = (bf16[8,8,288]{2,1,0:T(8,128)(2,1)S(1)}, bf16[8,8,288]{2,1,0:T(8,128)(2,1)S(1)}, u32[]{:S(2)}, u32[]{:S(2)}) collective-permute-start(bf16[8,8,288]{2,1,0:T(8,128)(2,1)S(1)} %get-tuple-element.541), channel_id=1, source_target_pairs={{0,1},{1,0},{2,3},{3,2},{4,5},{5,4},{6,7},{7,6},{8,9},{9,8},{10,11... | collective-permute-start | bytes 110600 | tf_op jit(solution)/shard_map/ppermute | solution.py:27
  169.1 29.4 %collective-permute-start.26 = (bf16[1,384,1152]{2,1,0:T(8,128)(2,1)S(1)}, bf16[1,384,1152]{2,1,0:T(8,128)(2,1)S(1)}, u32[]{:S(2)}, u32[]{:S(2)}) collective-permute-start(bf16[1,384,1152]{2,1,0:T(8,128)(2,1)S(1)} %get-tuple-element.361), channel_id=1, source_target_pairs={{0,8},{4,12},{8,0},{12,4},{16,24},{20,28},{24,16},{28,20},{1,9},{5... | collective-permute-start | bytes 2654216 | tf_op jit(solution)/shard_map/ppermute | solution.py:27
  175.8 32.1 %collective-permute-start.28 = (bf16[1,288,1536]{2,1,0:T(8,128)(2,1)}, bf16[1,288,1536]{2,1,0:T(8,128)(2,1)}, u32[]{:S(2)}, u32[]{:S(2)}) collective-permute-start(bf16[1,288,1536]{2,1,0:T(8,128)(2,1)} %get-tuple-element.365), channel_id=1, source_target_pairs={{0,4},{4,0},{8,12},{12,8},{16,20},{20,16},{24,28},{28,24},{1,5},{5... | collective-permute-start | bytes 2654216 | tf_op jit(solution)/shard_map/ppermute | solution.py:27
  212.9 24.0 %collective-permute-start.33 = (bf16[1,72,1536]{2,1,0:T(8,128)(2,1)S(1)}, bf16[1,72,1536]{2,1,0:T(8,128)(2,1)S(1)}, u32[]{:S(2)}, u32[]{:S(2)}) collective-permute-start(bf16[1,72,1536]{2,1,0:T(8,128)(2,1)S(1)} %get-tuple-element.398), channel_id=1, source_target_pairs={{0,16},{4,20},{8,24},{12,28},{16,0},{20,4},{24,8},{28,12},{1,17},{... | collective-permute-start | bytes 663560 | tf_op jit(solution)/shard_map/ppermute | solution.py:27
  216.7 40.0 %collective-permute-start.38 = (bf16[4,288,256]{2,1,0:T(8,128)(2,1)}, bf16[4,288,256]{2,1,0:T(8,128)(2,1)}, u32[]{:S(2)}, u32[]{:S(2)}) collective-permute-start(bf16[4,288,256]{2,1,0:T(8,128)(2,1)} %get-tuple-element.446), channel_id=1, source_target_pairs={{0,1},{1,0},{2,3},{3,2},{4,5},{5,4},{6,7},{7,6},{8,9},{9,8},{10,11... | collective-permute-start | bytes 1769480 | tf_op jit(solution)/shard_map/ppermute | solution.py:27
  216.7 33.2 %collective-permute-start.35 = (bf16[1,144,1536]{2,1,0:T(8,128)(2,1)}, bf16[1,144,1536]{2,1,0:T(8,128)(2,1)}, u32[]{:S(2)}, u32[]{:S(2)}) collective-permute-start(bf16[1,144,1536]{2,1,0:T(8,128)(2,1)} %get-tuple-element.394), channel_id=1, source_target_pairs={{0,8},{4,12},{8,0},{12,4},{16,24},{20,28},{24,16},{28,20},{1,9},{5... | collective-permute-start | bytes 1327112 | tf_op jit(solution)/shard_map/ppermute | solution.py:27
  217.0 40.8 %collective-permute-start.39 = (bf16[4,288,256]{2,1,0:T(8,128)(2,1)}, bf16[4,288,256]{2,1,0:T(8,128)(2,1)}, u32[]{:S(2)}, u32[]{:S(2)}) collective-permute-start(bf16[4,288,256]{2,1,0:T(8,128)(2,1)} %shard_map.233), channel_id=1, source_target_pairs={{0,2},{1,3},{2,0},{3,1},{4,6},{5,7},{6,4},{7,5},{8,10},{9,11},{10,... | collective-permute-start | bytes 1769480 | tf_op jit(solution)/shard_map/ppermute | solution.py:27
  253.2 33.3 %collective-permute-start.43 = (bf16[4,288,256]{2,1,0:T(8,128)(2,1)S(1)}, bf16[4,288,256]{2,1,0:T(8,128)(2,1)S(1)}, u32[]{:S(2)}, u32[]{:S(2)}) collective-permute-start(bf16[4,288,256]{2,1,0:T(8,128)(2,1)S(1)} %copy-done.75), channel_id=1, source_target_pairs={{0,1},{1,0},{2,3},{3,2},{4,5},{5,4},{6,7},{7,6},{8,9},{9,8},{10,11... | collective-permute-start | bytes 1769480 | tf_op jit(solution)/shard_map/ppermute | solution.py:27
  253.9 25.7 %collective-permute-start.41 = (bf16[2,144,1152]{2,1,0:T(8,128)(2,1)S(1)}, bf16[2,144,1152]{2,1,0:T(8,128)(2,1)S(1)}, u32[]{:S(2)}, u32[]{:S(2)}) collective-permute-start(bf16[2,144,1152]{2,1,0:T(8,128)(2,1)S(1)} %get-tuple-element.433), channel_id=1, source_target_pairs={{0,8},{4,12},{8,0},{12,4},{16,24},{20,28},{24,16},{28,20},{1,9},{5... | collective-permute-start | bytes 1990664 | tf_op jit(solution)/shard_map/ppermute | solution.py:27
  256.7 25.0 %collective-permute-start.42 = (bf16[2,144,1152]{2,1,0:T(8,128)(2,1)S(1)}, bf16[2,144,1152]{2,1,0:T(8,128)(2,1)S(1)}, u32[]{:S(2)}, u32[]{:S(2)}) collective-permute-start(bf16[2,144,1152]{2,1,0:T(8,128)(2,1)S(1)} %get-tuple-element.435), channel_id=1, source_target_pairs={{0,4},{4,0},{8,12},{12,8},{16,20},{20,16},{24,28},{28,24},{1,5},{5... | collective-permute-start | bytes 1990664 | tf_op jit(solution)/shard_map/ppermute | solution.py:27
  257.8 35.0 %collective-permute-start.45 = (bf16[1,72,1536]{2,1,0:T(8,128)(2,1)S(1)}, bf16[1,72,1536]{2,1,0:T(8,128)(2,1)S(1)}, u32[]{:S(2)}, u32[]{:S(2)}) collective-permute-start(bf16[1,72,1536]{2,1,0:T(8,128)(2,1)S(1)} %get-tuple-element.439), channel_id=1, source_target_pairs={{0,16},{4,20},{8,24},{12,28},{16,0},{20,4},{24,8},{28,12},{1,17},{... | collective-permute-start | bytes 663560 | tf_op jit(solution)/shard_map/ppermute | solution.py:27
  263.9 23.9 %collective-permute-start.44 = (bf16[4,304,256]{2,1,0:T(8,128)(2,1)S(1)}, bf16[4,304,256]{2,1,0:T(8,128)(2,1)S(1)}, u32[]{:S(2)}, u32[]{:S(2)}) collective-permute-start(bf16[4,304,256]{2,1,0:T(8,128)(2,1)S(1)} %shard_map.240), channel_id=1, source_target_pairs={{0,2},{1,3},{2,0},{3,1},{4,6},{5,7},{6,4},{7,5},{8,10},{9,11},{10,... | collective-permute-start | bytes 1867784 | tf_op jit(solution)/shard_map/ppermute | solution.py:27
  279.6 44.2 %collective-permute-start.49 = (bf16[1,96,1152]{2,1,0:T(8,128)(2,1)S(1)}, bf16[1,96,1152]{2,1,0:T(8,128)(2,1)S(1)}, u32[]{:S(2)}, u32[]{:S(2)}) collective-permute-start(bf16[1,96,1152]{2,1,0:T(8,128)(2,1)S(1)} %add_convert_fusion.1), channel_id=1, source_target_pairs={{0,16},{4,20},{8,24},{12,28},{16,0},{20,4},{24,8},{28,12},{1,17},{... | collective-permute-start | bytes 663560 | tf_op jit(solution)/shard_map/ppermute | solution.py:27
  287.8 34.6 %collective-permute-start.48 = (bf16[2,72,1152]{2,1,0:T(8,128)(2,1)S(1)}, bf16[2,72,1152]{2,1,0:T(8,128)(2,1)S(1)}, u32[]{:S(2)}, u32[]{:S(2)}) collective-permute-start(bf16[2,72,1152]{2,1,0:T(8,128)(2,1)S(1)} %get-tuple-element.460), channel_id=1, source_target_pairs={{0,4},{4,0},{8,12},{12,8},{16,20},{20,16},{24,28},{28,24},{1,5},{5... | collective-permute-start | bytes 995336 | tf_op jit(solution)/shard_map/ppermute | solution.py:27
  292.8 33.4 %collective-permute-start.50 = (bf16[2,72,1152]{2,1,0:T(8,128)(2,1)}, bf16[2,72,1152]{2,1,0:T(8,128)(2,1)S(1)}, u32[]{:S(2)}, u32[]{:S(2)}) collective-permute-start(bf16[2,72,1152]{2,1,0:T(8,128)(2,1)} %get-tuple-element.464), channel_id=1, source_target_pairs={{0,8},{4,12},{8,0},{12,4},{16,24},{20,28},{24,16},{28,20},{1,9},{5... | collective-permute-start | bytes 995336 | tf_op jit(solution)/shard_map/ppermute | solution.py:27
  299.4 57.5 %collective-permute-start.52 = (bf16[1,72,1536]{2,1,0:T(8,128)(2,1)}, bf16[1,72,1536]{2,1,0:T(8,128)(2,1)}, u32[]{:S(2)}, u32[]{:S(2)}) collective-permute-start(bf16[1,72,1536]{2,1,0:T(8,128)(2,1)} %add_convert_fusion), channel_id=1, source_target_pairs={{0,16},{4,20},{8,24},{12,28},{16,0},{20,4},{24,8},{28,12},{1,17},{... | collective-permute-start | bytes 663560 | tf_op jit(solution)/shard_map/ppermute | solution.py:27
  304.6 96.5 %collective-permute-start.62 = (bf16[1,288,1536]{2,1,0:T(8,128)(2,1)S(1)}, bf16[1,288,1536]{2,1,0:T(8,128)(2,1)}, u32[]{:S(2)}, u32[]{:S(2)}) collective-permute-start(bf16[1,288,1536]{2,1,0:T(8,128)(2,1)S(1)} %maximum_select_fusion.refs_0_), channel_id=1, source_target_pairs={{0,4},{4,0},{8,12},{12,8},{16,20},{20,16},{24,28},{28,24},{1,5},{5... | collective-permute-start | bytes 2654216 | tf_op jit(solution)/shard_map/ppermute | solution.py:27
  323.8 34.6 %collective-permute-start.53 = (bf16[1,72,1152]{2,1,0:T(8,128)(2,1)}, bf16[1,72,1152]{2,1,0:T(8,128)(2,1)}, u32[]{:S(2)}, u32[]{:S(2)}) collective-permute-start(bf16[1,72,1152]{2,1,0:T(8,128)(2,1)} %get-tuple-element.487), channel_id=1, source_target_pairs={{0,16},{4,20},{8,24},{12,28},{16,0},{20,4},{24,8},{28,12},{1,17},{... | collective-permute-start | bytes 497672 | tf_op jit(solution)/shard_map/ppermute | solution.py:27
  323.8 27.8 %collective-permute-start.51 = (bf16[4,288,256]{2,1,0:T(8,128)(2,1)}, bf16[4,288,256]{2,1,0:T(8,128)(2,1)}, u32[]{:S(2)}, u32[]{:S(2)}) collective-permute-start(bf16[4,288,256]{2,1,0:T(8,128)(2,1)} %get-tuple-element.495), channel_id=1, source_target_pairs={{4,0},{8,4},{12,8},{16,12},{20,16},{24,20},{28,24},{5,1},{9,5},{13... | collective-permute-start | bytes 1769480 | tf_op jit(solution)/shard_map/ppermute | solution.py:33
  326.2 38.4 %collective-permute-start.56 = (bf16[1,192,1152]{2,1,0:T(8,128)(2,1)}, bf16[1,192,1152]{2,1,0:T(8,128)(2,1)S(1)}, u32[]{:S(2)}, u32[]{:S(2)}) collective-permute-start(bf16[1,192,1152]{2,1,0:T(8,128)(2,1)} %maximum_select_fusion.6), channel_id=1, source_target_pairs={{0,4},{4,0},{8,12},{12,8},{16,20},{20,16},{24,28},{28,24},{1,5},{5... | collective-permute-start | bytes 1327112 | tf_op jit(solution)/shard_map/ppermute | solution.py:27
  376.7 24.4 %collective-permute-start.63 = (bf16[1,288,1536]{2,1,0:T(8,128)(2,1)S(1)}, bf16[1,288,1536]{2,1,0:T(8,128)(2,1)S(1)}, u32[]{:S(2)}, u32[]{:S(2)}) collective-permute-start(bf16[1,288,1536]{2,1,0:T(8,128)(2,1)S(1)} %maximum_select_fusion.2.refs_2_), channel_id=1, source_target_pairs={{0,4},{4,0},{8,12},{12,8},{16,20},{20,16},{24,28},{28,24},{1,5},{5... | collective-permute-start | bytes 2654216 | tf_op jit(solution)/shard_map/ppermute | solution.py:27
  379.1 29.1 %collective-permute-start.64 = (bf16[2,72,1152]{2,1,0:T(8,128)(2,1)S(1)}, bf16[2,72,1152]{2,1,0:T(8,128)(2,1)S(1)}, u32[]{:S(2)}, u32[]{:S(2)}) collective-permute-start(bf16[2,72,1152]{2,1,0:T(8,128)(2,1)S(1)} %maximum_select_fusion.8), channel_id=1, source_target_pairs={{0,4},{4,0},{8,12},{12,8},{16,20},{20,16},{24,28},{28,24},{1,5},{5... | collective-permute-start | bytes 995336 | tf_op jit(solution)/shard_map/ppermute | solution.py:27
  379.3 29.0 %collective-permute-start.65 = (bf16[2,72,1152]{2,1,0:T(8,128)(2,1)S(1)}, bf16[2,72,1152]{2,1,0:T(8,128)(2,1)S(1)}, u32[]{:S(2)}, u32[]{:S(2)}) collective-permute-start(bf16[2,72,1152]{2,1,0:T(8,128)(2,1)S(1)} %maximum_select_fusion.9), channel_id=1, source_target_pairs={{0,8},{4,12},{8,0},{12,4},{16,24},{20,28},{24,16},{28,20},{1,9},{5... | collective-permute-start | bytes 995336 | tf_op jit(solution)/shard_map/ppermute | solution.py:27
  (129 other events, 1303.3 us)

commit v4 on v3

--- a/solution.py
+++ b/solution.py
@@ -893,7 +893,7 @@
                 ],
                 scratch=[pltpu.VMEM((features, P_SIZE), BF16), pltpu.VMEM((width, P_SIZE), F32)],
                 us=4.5 * images,
-                vmem=58,
+                vmem=48,
             ),
             *st.pieces_one, st.mods_full, wqkv, weights.proj_t, gains, cos, sin,
         )
@@ -962,7 +962,7 @@
                 ],
                 scratch=[pltpu.VMEM((features, P_SIZE), BF16), pltpu.VMEM((features, P_SIZE), F32)],
                 us=6.0 * images,
-                vmem=58,
+                vmem=48,
             ),
             *st.pieces_two, *st.pieces_grad_two, st.mods_full,
             weights.up_t, weights.up, weights.down_t, down_weight,
@@ -1044,7 +1044,7 @@
                     pltpu.VMEM((2, HEAD, P_SIZE), F32),
                 ],
                 us=4.5 * images,
-                vmem=58,
+                vmem=48,
             ),
             *st.pieces_grad_one, *st.pieces_one, st.inverse_one, st.mods_full, st.raw,
             proj_weight, weights.qkv_t, gains, cos, sin,

time: 434 us -> 425 us (0.979)
  local copies, waits for them, and re-layouts: 36.3 us -> 31.5 us
    unnamed x162 -> x174, local copies, waits for them, and re-layouts: 29.9 us -> 27 us
  transfers between devices with their start and end apart: 75 -> 75, of which waited for: 21 -> 22; matrix products, arithmetic and copies ran while one was open for 8% -> 8% of each run, Pallas kernels for 25% -> 25%
where the time goes in v4:
time: 425 us; the launch traced here: 421 us
  Pallas kernels  138 us (32%)
  waiting for transfers between devices  132 us (31%)
  starting transfers between devices  89.4 us (21%)
  local copies, waits for them, and re-layouts  31.5 us (7%)
  other arithmetic  16.8 us (4%)
  matrix products  10.7 us (3%)
    pallas_call x38, Pallas kernels, call(): pl.pallas_call(kernel, grid_spec=pltpu.PrefetchScalarGridSpec(num_scalar_...  136 us
    ppermute x70, waiting for transfers between devices, exchange(): return lax.ppermute(value, axis, pairs)  105 us
    ppermute x70, starting transfers between devices, exchange(): return lax.ppermute(value, axis, pairs)  74.2 us
    unnamed x174, local copies, waits for them, and re-layouts  27 us
    ppermute x5, waiting for transfers between devices, shifted(): return lax.ppermute(value, axis, pairs)  26.3 us
    ppermute x5, starting transfers between devices, shifted(): return lax.ppermute(value, axis, pairs)  15.2 us
    dot_general x3, matrix products, einsum(): return jnp.einsum(spec, *operands, preferred_element_type=F32)  10.7 us
  transfers between devices with their start and end apart: 75, of which 22 were waited for; matrix products, arithmetic and copies ran while one was open for 8% of the time, Pallas kernels for 25%

profile of v4, /device:TPU:0, one launch (start us, length us, event | category | flops | bytes accessed | tf_op | source)
XLA Modules:
  0.0 421.3 jit_solution(2154139183460391585)
XLA Ops:
  2.8 4.9 %collective-permute-start.5 = (bf16[4,288]{1,0:T(4,128)(2,1)S(1)}, bf16[4,288]{1,0:T(4,128)(2,1)S(1)}, u32[]{:S(2)}, u32[]{:S(2)}) collective-permute-start(bf16[4,288]{1,0:T(4,128)(2,1)S(1)} %select_convert_fusion), channel_id=1, source_target_pairs={{0,4},{4,8},{8,12},{12,16},{16,20},{20,24},{24,28},{1,5},{5,9},{9,... | collective-permute-start | bytes 6920 | tf_op jit(solution)/shard_map/ppermute | solution.py:33
  37.6 4.2 collective-permute-start.4
  44.8 13.6 %collective-permute-done.9.p2.r2 = bf16[4,288,256]{2,1,0:T(8,128)(2,1)S(1)} collective-permute-done((bf16[4,288,256]{2,1,0:T(8,128)(2,1)S(1)}, bf16[4,288,256]{2,1,0:T(8,128)(2,1)S(1)}, u32[]{:S(2)}, u32[]{:S(2)}) %collective-permute-start.9) | collective-permute-done | bytes 589856 | tf_op jit(solution)/shard_map/ppermute | solution.py:27
  63.6 18.7 %shard_map.221 = (bf16[4,288,256]{2,1,0:T(8,128)(2,1)S(1)}, bf16[4,288,256]{2,1,0:T(8,128)(2,1)S(1)}, f32[4,288,256]{2,1,0:T(8,128)}, f32[4,288,256]{2,1,0:T(8,1...) custom-call(s32[1]{0:T(128)} %bitcast.4.s_ref.me_ref, ...), custom_call_target="tpu_custom_call" | custom-call | flops 1800000000 | bytes 1000 | tf_op jit(solution)/shard_map/pallas_call | solution.py:81
  90.6 10.6 %collective-permute-done.16.across = bf16[4,288,256]{2,1,0:T(8,128)(2,1)S(1)} collective-permute-done((bf16[4,288,256]{2,1,0:T(8,128)(2,1)S(1)}, bf16[4,288,256]{2,1,0:T(8,128)(2,1)S(1)}, u32[]{:S(2)}, u32[]{:S(2)}) %collective-permute-start.16) | collective-permute-done | bytes 589856 | tf_op jit(solution)/shard_map/ppermute | solution.py:27
  105.5 13.5 %collective-permute-done.18.p2 = bf16[4,288,256]{2,1,0:T(8,128)(2,1)S(1)} collective-permute-done((bf16[4,288,256]{2,1,0:T(8,128)(2,1)S(1)}, bf16[4,288,256]{2,1,0:T(8,128)(2,1)S(1)}, u32[]{:S(2)}, u32[]{:S(2)}) %collective-permute-start.18) | collective-permute-done | bytes 589856 | tf_op jit(solution)/shard_map/ppermute | solution.py:27
  121.0 24.0 %shard_map.225 = (bf16[4,288,256]{2,1,0:T(8,128)(2,1)}, bf16[4,288,256]{2,1,0:T(8,128)(2,1)}, f32[4,288,256]{2,1,0:T(8,128)}, f32[4,288,256]{2,1,0:T(8,128)}, bf...) custom-call(s32[1]{0:T(128)} %bitcast.4.s_ref.me_ref, ...), custom_call_target="tpu_custom_call" | custom-call | flops 2400000000 | bytes 1000 | tf_op jit(solution)/shard_map/pallas_call | solution.py:81
  169.3 3.8 shard_map.230
  175.9 3.7 collective-permute-done.25.got_a.got_b
  181.4 7.9 %collective-permute-done.70 = bf16[8,8,576]{2,1,0:T(8,128)(2,1)S(1)} collective-permute-done((bf16[8,8,576]{2,1,0:T(8,128)(2,1)S(1)}, bf16[8,8,576]{2,1,0:T(8,128)(2,1)S(1)}, u32[]{:S(2)}, u32[]{:S(2)}) %collective-permute-start.70) | collective-permute-done | bytes 73760 | tf_op jit(solution)/shard_map/ppermute | solution.py:27
  210.4 18.1 %shard_map.236 = (bf16[4,288,256]{2,1,0:T(8,128)(2,1)S(1)}, bf16[4,304,256]{2,1,0:T(8,128)(2,1)}, f32[4,288,256]{2,1,0:T(8,128)}, f32[4,288,256]{2,1,0:T(8,128)}...) custom-call(s32[1]{0:T(128)} %bitcast.4.s_ref.me_ref, ...), custom_call_target="tpu_custom_call" | custom-call | flops 1800000000 | bytes 1000 | tf_op jit(solution)/shard_map/pallas_call | solution.py:81
  237.2 4.9 %shard_map.238 = (bf16[2,144,1152]{2,1,0:T(8,128)(2,1)S(1)}, f32[2,144,1152]{2,1,0:T(8,128)S(1)}, bf16[2,144,1152]{2,1,0:T(8,128)(2,1)S(1)}, f32[2,144,1152]{2,1,0:T(8,128)S(1)}) custom-call(s32[2]{0:T(128)S(1)} %pad_add_fusion.1.s_ref, bf16[864,1024]{1,0:T(8,128)(2,1)S(1)} %copy-done.35, bf16[288,1024]{1,0:T(8,128)(2,1)S(1)} %copy-done.60, ...), custom_call_target="tpu_custom_call" | custom-call | flops 300000000 | bytes 1000 | tf_op jit(solution)/shard_map/pallas_call | solution.py:81
  256.7 15.9 %collective-permute-done.41.got_a.got_b = bf16[2,144,1152]{2,1,0:T(8,128)(2,1)S(1)} collective-permute-done((bf16[2,144,1152]{2,1,0:T(8,128)(2,1)S(1)}, bf16[2,144,1152]{2,1,0:T(8,128)(2,1)S(1)}, u32[]{:S(2)}, u32[]{:S(2)}) %collective-permute-start.41) | collective-permute-done | bytes 663584 | tf_op jit(solution)/shard_map/ppermute | solution.py:27
  286.4 4.7 %collective-permute-done.46 = bf16[1,144,1536]{2,1,0:T(8,128)(2,1)S(1)} collective-permute-done((bf16[1,144,1536]{2,1,0:T(8,128)(2,1)S(1)}, bf16[1,144,1536]{2,1,0:T(8,128)(2,1)S(1)}, u32[]{:S(2)}, u32[]{:S(2)}) %collective-permute-start.46) | collective-permute-done | bytes 442400 | tf_op jit(solution)/shard_map/ppermute | solution.py:27
  291.8 4.1 collective-permute-done.47.refs_1_
  295.9 14.1 %collective-permute-start.62 = (bf16[1,288,1536]{2,1,0:T(8,128)(2,1)S(1)}, bf16[1,288,1536]{2,1,0:T(8,128)(2,1)}, u32[]{:S(2)}, u32[]{:S(2)}) collective-permute-start(bf16[1,288,1536]{2,1,0:T(8,128)(2,1)S(1)} %maximum_select_fusion.refs_0_), channel_id=1, source_target_pairs={{0,4},{4,0},{8,12},{12,8},{16,20},{20,16},{24,28},{28,24},{1,5},{5... | collective-permute-start | bytes 2654216 | tf_op jit(solution)/shard_map/ppermute | solution.py:27
  310.0 3.7 shard_map.245
  321.1 22.2 %collective-permute-done.51.refs_1_ = bf16[4,288,256]{2,1,0:T(8,128)(2,1)} collective-permute-done((bf16[4,288,256]{2,1,0:T(8,128)(2,1)}, bf16[4,288,256]{2,1,0:T(8,128)(2,1)}, u32[]{:S(2)}, u32[]{:S(2)}) %collective-permute-start.51) | collective-permute-done | bytes 589856 | tf_op jit(solution)/shard_map/ppermute | solution.py:33
  343.3 5.4 %shard_map.248 = f32[8,288,256]{2,1,0:T(8,128)} custom-call(s32[2]{0:T(128)S(1)} %pad_add_fusion.s_ref, f32[4,288,256]{2,1,0:T(8,128)S(1)} %copy-done.51, bf16[4,288,256]{2,1,0:T(8,128)(2,1)} %collective-permute-done.51.refs_1_), custom_call_target="tpu_custom_call" | custom-call | flops 300000000 | bytes 1000 | tf_op jit(solution)/shard_map/pallas_call | solution.py:81
  356.7 10.6 %collective-permute-done.57 = bf16[1,144,1536]{2,1,0:T(8,128)(2,1)S(1)} collective-permute-done((bf16[1,144,1536]{2,1,0:T(8,128)(2,1)S(1)}, bf16[1,144,1536]{2,1,0:T(8,128)(2,1)S(1)}, u32[]{:S(2)}, u32[]{:S(2)}) %collective-permute-start.57) | collective-permute-done | bytes 442400 | tf_op jit(solution)/shard_map/ppermute | solution.py:27
  374.6 14.2 %collective-permute-done.61.refs_1_ = bf16[1,384,1152]{2,1,0:T(8,128)(2,1)S(1)} collective-permute-done((bf16[1,384,1152]{2,1,0:T(8,128)(2,1)S(1)}, bf16[1,384,1152]{2,1,0:T(8,128)(2,1)S(1)}, u32[]{:S(2)}, u32[]{:S(2)}) %collective-permute-start.61) | collective-permute-done | bytes 884768 | tf_op jit(solution)/shard_map/ppermute | solution.py:27
  392.8 7.1 %shard_map.250 = f32[1152,2,768]{2,1,0:T(2,128)} custom-call(s32[2]{0:T(128)S(1)} %copy-done.70, bf16[1,288,1536]{2,1,0:T(8,128)(2,1)S(1)} %maximum_select_fusion.refs_0_, bf16[1,288,1536]{2,1,0:T(8,128)(2,1)} %collective-permute-done.62.refs_1_, bf16[1,288,1536]{2,1,0:T(8,128)(2,1)S(1)} %maximum_select_fusion.2.refs_2_, ...), custom_call_target="tpu_custom_call" | custom-call | flops 300000000 | bytes 1000 | tf_op jit(solution)/shard_map/pallas_call | solution.py:81
  406.5 4.5 %fusion.1 = f32[6,288,1152]{2,1,0:T(8,128)} fusion(bf16[6,32,288]{2,0,1:T(8,128)(2,1)S(1)} %bitcast.88, bf16[32,1152]{1,0:T(8,128)(2,1)S(1)} %broadcast_select_fusion), kind=kOutput, calls=%fused_computation.30 | convolution fusion | flops 127401984 | bytes 8146944 | tf_op jit(solution)/shard_map/kbf,bd->kfd/dot_general | solution.py:635
  416.3 4.7 %shard_map.251 = (f32[3,288,1152]{2,1,0:T(8,128)}, f32[288,1152]{1,0:T(8,128)}) custom-call(s32[2]{0:T(128)S(1)} %pad_add_fusion.1.s_ref, bf16[2,144,1152]{2,1,0:T(8,128)(2,1)S(1)} %maximum_select_fusion.3.mine1, bf16[2,144,1152]{2,1,0:T(8,128)(2,1)S(1)} %collective-permute-done.71.other1, bf16[2,144,1152]{2,1,0:T(8,128)(2,1)S(1)} %maximum_select_fusion.4.mine2, ...), custom_call_target="tpu_custom_call" | custom-call | flops 300000000 | bytes 1000 | tf_op jit(solution)/shard_map/pallas_call | solution.py:81
  (431 shorter events, 179.3 us)
Async XLA Ops:
  147.2 28.0 %collective-permute-start.69 = (bf16[8,8,288]{2,1,0:T(8,128)(2,1)S(1)}, bf16[8,8,288]{2,1,0:T(8,128)(2,1)S(1)}, u32[]{:S(2)}, u32[]{:S(2)}) collective-permute-start(bf16[8,8,288]{2,1,0:T(8,128)(2,1)S(1)} %get-tuple-element.541), channel_id=1, source_target_pairs={{0,1},{1,0},{2,3},{3,2},{4,5},{5,4},{6,7},{7,6},{8,9},{9,8},{10,11... | collective-permute-start | bytes 110600 | tf_op jit(solution)/shard_map/ppermute | solution.py:27
  157.1 22.6 %collective-permute-start.25 = (bf16[1,288,1536]{2,1,0:T(8,128)(2,1)S(1)}, bf16[1,288,1536]{2,1,0:T(8,128)(2,1)S(1)}, u32[]{:S(2)}, u32[]{:S(2)}) collective-permute-start(bf16[1,288,1536]{2,1,0:T(8,128)(2,1)S(1)} %get-tuple-element.357), channel_id=1, source_target_pairs={{0,4},{4,0},{8,12},{12,8},{16,20},{20,16},{24,28},{28,24},{1,5},{5... | collective-permute-start | bytes 2654216 | tf_op jit(solution)/shard_map/ppermute | solution.py:27
  161.5 29.4 %collective-permute-start.26 = (bf16[1,384,1152]{2,1,0:T(8,128)(2,1)S(1)}, bf16[1,384,1152]{2,1,0:T(8,128)(2,1)S(1)}, u32[]{:S(2)}, u32[]{:S(2)}) collective-permute-start(bf16[1,384,1152]{2,1,0:T(8,128)(2,1)S(1)} %get-tuple-element.361), channel_id=1, source_target_pairs={{0,8},{4,12},{8,0},{12,4},{16,24},{20,28},{24,16},{28,20},{1,9},{5... | collective-permute-start | bytes 2654216 | tf_op jit(solution)/shard_map/ppermute | solution.py:27
  168.7 31.7 %collective-permute-start.28 = (bf16[1,288,1536]{2,1,0:T(8,128)(2,1)}, bf16[1,288,1536]{2,1,0:T(8,128)(2,1)}, u32[]{:S(2)}, u32[]{:S(2)}) collective-permute-start(bf16[1,288,1536]{2,1,0:T(8,128)(2,1)} %get-tuple-element.365), channel_id=1, source_target_pairs={{0,4},{4,0},{8,12},{12,8},{16,20},{20,16},{24,28},{28,24},{1,5},{5... | collective-permute-start | bytes 2654216 | tf_op jit(solution)/shard_map/ppermute | solution.py:27
  205.6 23.7 %collective-permute-start.33 = (bf16[1,72,1536]{2,1,0:T(8,128)(2,1)S(1)}, bf16[1,72,1536]{2,1,0:T(8,128)(2,1)S(1)}, u32[]{:S(2)}, u32[]{:S(2)}) collective-permute-start(bf16[1,72,1536]{2,1,0:T(8,128)(2,1)S(1)} %get-tuple-element.398), channel_id=1, source_target_pairs={{0,16},{4,20},{8,24},{12,28},{16,0},{20,4},{24,8},{28,12},{1,17},{... | collective-permute-start | bytes 663560 | tf_op jit(solution)/shard_map/ppermute | solution.py:27
  208.5 39.8 %collective-permute-start.38 = (bf16[4,288,256]{2,1,0:T(8,128)(2,1)}, bf16[4,288,256]{2,1,0:T(8,128)(2,1)}, u32[]{:S(2)}, u32[]{:S(2)}) collective-permute-start(bf16[4,288,256]{2,1,0:T(8,128)(2,1)} %get-tuple-element.446), channel_id=1, source_target_pairs={{0,1},{1,0},{2,3},{3,2},{4,5},{5,4},{6,7},{7,6},{8,9},{9,8},{10,11... | collective-permute-start | bytes 1769480 | tf_op jit(solution)/shard_map/ppermute | solution.py:27
  208.5 33.6 %collective-permute-start.35 = (bf16[1,144,1536]{2,1,0:T(8,128)(2,1)}, bf16[1,144,1536]{2,1,0:T(8,128)(2,1)}, u32[]{:S(2)}, u32[]{:S(2)}) collective-permute-start(bf16[1,144,1536]{2,1,0:T(8,128)(2,1)} %get-tuple-element.394), channel_id=1, source_target_pairs={{0,8},{4,12},{8,0},{12,4},{16,24},{20,28},{24,16},{28,20},{1,9},{5... | collective-permute-start | bytes 1327112 | tf_op jit(solution)/shard_map/ppermute | solution.py:27
  208.8 41.3 %collective-permute-start.39 = (bf16[4,288,256]{2,1,0:T(8,128)(2,1)}, bf16[4,288,256]{2,1,0:T(8,128)(2,1)}, u32[]{:S(2)}, u32[]{:S(2)}) collective-permute-start(bf16[4,288,256]{2,1,0:T(8,128)(2,1)} %shard_map.233), channel_id=1, source_target_pairs={{0,2},{1,3},{2,0},{3,1},{4,6},{5,7},{6,4},{7,5},{8,10},{9,11},{10,... | collective-permute-start | bytes 1769480 | tf_op jit(solution)/shard_map/ppermute | solution.py:27
  245.5 31.9 %collective-permute-start.43 = (bf16[4,288,256]{2,1,0:T(8,128)(2,1)S(1)}, bf16[4,288,256]{2,1,0:T(8,128)(2,1)S(1)}, u32[]{:S(2)}, u32[]{:S(2)}) collective-permute-start(bf16[4,288,256]{2,1,0:T(8,128)(2,1)S(1)} %copy-done.72), channel_id=1, source_target_pairs={{0,1},{1,0},{2,3},{3,2},{4,5},{5,4},{6,7},{7,6},{8,9},{9,8},{10,11... | collective-permute-start | bytes 1769480 | tf_op jit(solution)/shard_map/ppermute | solution.py:27
  246.2 26.3 %collective-permute-start.41 = (bf16[2,144,1152]{2,1,0:T(8,128)(2,1)S(1)}, bf16[2,144,1152]{2,1,0:T(8,128)(2,1)S(1)}, u32[]{:S(2)}, u32[]{:S(2)}) collective-permute-start(bf16[2,144,1152]{2,1,0:T(8,128)(2,1)S(1)} %get-tuple-element.433), channel_id=1, source_target_pairs={{0,8},{4,12},{8,0},{12,4},{16,24},{20,28},{24,16},{28,20},{1,9},{5... | collective-permute-start | bytes 1990664 | tf_op jit(solution)/shard_map/ppermute | solution.py:27
  248.3 25.0 %collective-permute-start.42 = (bf16[2,144,1152]{2,1,0:T(8,128)(2,1)S(1)}, bf16[2,144,1152]{2,1,0:T(8,128)(2,1)S(1)}, u32[]{:S(2)}, u32[]{:S(2)}) collective-permute-start(bf16[2,144,1152]{2,1,0:T(8,128)(2,1)S(1)} %get-tuple-element.435), channel_id=1, source_target_pairs={{0,4},{4,0},{8,12},{12,8},{16,20},{20,16},{24,28},{28,24},{1,5},{5... | collective-permute-start | bytes 1990664 | tf_op jit(solution)/shard_map/ppermute | solution.py:27
  250.1 34.0 %collective-permute-start.45 = (bf16[1,72,1536]{2,1,0:T(8,128)(2,1)S(1)}, bf16[1,72,1536]{2,1,0:T(8,128)(2,1)S(1)}, u32[]{:S(2)}, u32[]{:S(2)}) collective-permute-start(bf16[1,72,1536]{2,1,0:T(8,128)(2,1)S(1)} %get-tuple-element.439), channel_id=1, source_target_pairs={{0,16},{4,20},{8,24},{12,28},{16,0},{20,4},{24,8},{28,12},{1,17},{... | collective-permute-start | bytes 663560 | tf_op jit(solution)/shard_map/ppermute | solution.py:27
  255.8 22.9 %collective-permute-start.44 = (bf16[4,304,256]{2,1,0:T(8,128)(2,1)S(1)}, bf16[4,304,256]{2,1,0:T(8,128)(2,1)S(1)}, u32[]{:S(2)}, u32[]{:S(2)}) collective-permute-start(bf16[4,304,256]{2,1,0:T(8,128)(2,1)S(1)} %shard_map.240), channel_id=1, source_target_pairs={{0,2},{1,3},{2,0},{3,1},{4,6},{5,7},{6,4},{7,5},{8,10},{9,11},{10,... | collective-permute-start | bytes 1867784 | tf_op jit(solution)/shard_map/ppermute | solution.py:27
  272.6 43.0 %collective-permute-start.49 = (bf16[1,96,1152]{2,1,0:T(8,128)(2,1)S(1)}, bf16[1,96,1152]{2,1,0:T(8,128)(2,1)S(1)}, u32[]{:S(2)}, u32[]{:S(2)}) collective-permute-start(bf16[1,96,1152]{2,1,0:T(8,128)(2,1)S(1)} %add_convert_fusion.1), channel_id=1, source_target_pairs={{0,16},{4,20},{8,24},{12,28},{16,0},{20,4},{24,8},{28,12},{1,17},{... | collective-permute-start | bytes 663560 | tf_op jit(solution)/shard_map/ppermute | solution.py:27
  278.7 35.4 %collective-permute-start.48 = (bf16[2,72,1152]{2,1,0:T(8,128)(2,1)S(1)}, bf16[2,72,1152]{2,1,0:T(8,128)(2,1)S(1)}, u32[]{:S(2)}, u32[]{:S(2)}) collective-permute-start(bf16[2,72,1152]{2,1,0:T(8,128)(2,1)S(1)} %get-tuple-element.460), channel_id=1, source_target_pairs={{0,4},{4,0},{8,12},{12,8},{16,20},{20,16},{24,28},{28,24},{1,5},{5... | collective-permute-start | bytes 995336 | tf_op jit(solution)/shard_map/ppermute | solution.py:27
  284.1 33.8 %collective-permute-start.50 = (bf16[2,72,1152]{2,1,0:T(8,128)(2,1)}, bf16[2,72,1152]{2,1,0:T(8,128)(2,1)S(1)}, u32[]{:S(2)}, u32[]{:S(2)}) collective-permute-start(bf16[2,72,1152]{2,1,0:T(8,128)(2,1)} %get-tuple-element.464), channel_id=1, source_target_pairs={{0,8},{4,12},{8,0},{12,4},{16,24},{20,28},{24,16},{28,20},{1,9},{5... | collective-permute-start | bytes 995336 | tf_op jit(solution)/shard_map/ppermute | solution.py:27
  291.1 57.5 %collective-permute-start.52 = (bf16[1,72,1536]{2,1,0:T(8,128)(2,1)}, bf16[1,72,1536]{2,1,0:T(8,128)(2,1)}, u32[]{:S(2)}, u32[]{:S(2)}) collective-permute-start(bf16[1,72,1536]{2,1,0:T(8,128)(2,1)} %add_convert_fusion), channel_id=1, source_target_pairs={{0,16},{4,20},{8,24},{12,28},{16,0},{20,4},{24,8},{28,12},{1,17},{... | collective-permute-start | bytes 663560 | tf_op jit(solution)/shard_map/ppermute | solution.py:27
  295.9 96.9 %collective-permute-start.62 = (bf16[1,288,1536]{2,1,0:T(8,128)(2,1)S(1)}, bf16[1,288,1536]{2,1,0:T(8,128)(2,1)}, u32[]{:S(2)}, u32[]{:S(2)}) collective-permute-start(bf16[1,288,1536]{2,1,0:T(8,128)(2,1)S(1)} %maximum_select_fusion.refs_0_), channel_id=1, source_target_pairs={{0,4},{4,0},{8,12},{12,8},{16,20},{20,16},{24,28},{28,24},{1,5},{5... | collective-permute-start | bytes 2654216 | tf_op jit(solution)/shard_map/ppermute | solution.py:27
  315.5 34.6 %collective-permute-start.53 = (bf16[1,72,1152]{2,1,0:T(8,128)(2,1)}, bf16[1,72,1152]{2,1,0:T(8,128)(2,1)}, u32[]{:S(2)}, u32[]{:S(2)}) collective-permute-start(bf16[1,72,1152]{2,1,0:T(8,128)(2,1)} %get-tuple-element.487), channel_id=1, source_target_pairs={{0,16},{4,20},{8,24},{12,28},{16,0},{20,4},{24,8},{28,12},{1,17},{... | collective-permute-start | bytes 497672 | tf_op jit(solution)/shard_map/ppermute | solution.py:27
  315.5 27.7 %collective-permute-start.51 = (bf16[4,288,256]{2,1,0:T(8,128)(2,1)}, bf16[4,288,256]{2,1,0:T(8,128)(2,1)}, u32[]{:S(2)}, u32[]{:S(2)}) collective-permute-start(bf16[4,288,256]{2,1,0:T(8,128)(2,1)} %get-tuple-element.495), channel_id=1, source_target_pairs={{4,0},{8,4},{12,8},{16,12},{20,16},{24,20},{28,24},{5,1},{9,5},{13... | collective-permute-start | bytes 1769480 | tf_op jit(solution)/shard_map/ppermute | solution.py:33
  317.9 38.4 %collective-permute-start.56 = (bf16[1,192,1152]{2,1,0:T(8,128)(2,1)}, bf16[1,192,1152]{2,1,0:T(8,128)(2,1)S(1)}, u32[]{:S(2)}, u32[]{:S(2)}) collective-permute-start(bf16[1,192,1152]{2,1,0:T(8,128)(2,1)} %maximum_select_fusion.6), channel_id=1, source_target_pairs={{0,4},{4,0},{8,12},{12,8},{16,20},{20,16},{24,28},{28,24},{1,5},{5... | collective-permute-start | bytes 1327112 | tf_op jit(solution)/shard_map/ppermute | solution.py:27
  368.3 24.5 %collective-permute-start.63 = (bf16[1,288,1536]{2,1,0:T(8,128)(2,1)S(1)}, bf16[1,288,1536]{2,1,0:T(8,128)(2,1)S(1)}, u32[]{:S(2)}, u32[]{:S(2)}) collective-permute-start(bf16[1,288,1536]{2,1,0:T(8,128)(2,1)S(1)} %maximum_select_fusion.2.refs_2_), channel_id=1, source_target_pairs={{0,4},{4,0},{8,12},{12,8},{16,20},{20,16},{24,28},{28,24},{1,5},{5... | collective-permute-start | bytes 2654216 | tf_op jit(solution)/shard_map/ppermute | solution.py:27
  370.9 29.1 %collective-permute-start.64 = (bf16[2,72,1152]{2,1,0:T(8,128)(2,1)S(1)}, bf16[2,72,1152]{2,1,0:T(8,128)(2,1)S(1)}, u32[]{:S(2)}, u32[]{:S(2)}) collective-permute-start(bf16[2,72,1152]{2,1,0:T(8,128)(2,1)S(1)} %maximum_select_fusion.8), channel_id=1, source_target_pairs={{0,4},{4,0},{8,12},{12,8},{16,20},{20,16},{24,28},{28,24},{1,5},{5... | collective-permute-start | bytes 995336 | tf_op jit(solution)/shard_map/ppermute | solution.py:27
  371.0 29.0 %collective-permute-start.65 = (bf16[2,72,1152]{2,1,0:T(8,128)(2,1)S(1)}, bf16[2,72,1152]{2,1,0:T(8,128)(2,1)S(1)}, u32[]{:S(2)}, u32[]{:S(2)}) collective-permute-start(bf16[2,72,1152]{2,1,0:T(8,128)(2,1)S(1)} %maximum_select_fusion.9), channel_id=1, source_target_pairs={{0,8},{4,12},{8,0},{12,4},{16,24},{20,28},{24,16},{28,20},{1,9},{5... | collective-permute-start | bytes 995336 | tf_op jit(solution)/shard_map/ppermute | solution.py:27
  (135 other events, 1466.2 us)

commit v5 on v4

--- a/solution.py
+++ b/solution.py
@@ -1253,11 +1253,11 @@
     halve(attn1, 2)
     double(down, 0)
     halve(attn2, 2)
-    home_latent()
     double(up2, 0)
     join(attn1)
     modulation_step()
     join(attn2)
+    home_latent()
     double(down, 1)
     double(up2, 1)
     modulation_step()

time: 425 us -> 416 us (0.979)
  starting transfers between devices: 89.4 us -> 83 us
  waiting for transfers between devices: 132 us -> 127 us
    ppermute x5, waiting for transfers between devices: 26.3 us -> 11 us  [shifted(): return lax.ppermute(value, axis, pairs)]
    ppermute x70, waiting for transfers between devices: 105 us -> 116 us  [exchange(): return lax.ppermute(value, axis, pairs)]
    ppermute x70, starting transfers between devices: 74.2 us -> 67.9 us  [exchange(): return lax.ppermute(value, axis, pairs)]
    unnamed x174 -> x182, local copies, waits for them, and re-layouts: 27 us -> 28.3 us
  transfers between devices with their start and end apart: 75 -> 75, of which waited for: 22 -> 24; matrix products, arithmetic and copies ran while one was open for 8% -> 8% of each run, Pallas kernels for 25% -> 26%
where the time goes in v5:
time: 416 us; the launch traced here: 412 us
  Pallas kernels  137 us (33%)
  waiting for transfers between devices  127 us (31%)
  starting transfers between devices  83 us (20%)
  local copies, waits for them, and re-layouts  32.8 us (8%)
  other arithmetic  17.5 us (4%)
  matrix products  10.7 us (3%)
    pallas_call x38, Pallas kernels, call(): pl.pallas_call(kernel, grid_spec=pltpu.PrefetchScalarGridSpec(num_scalar_...  135 us
    ppermute x70, waiting for transfers between devices, exchange(): return lax.ppermute(value, axis, pairs)  116 us
    ppermute x70, starting transfers between devices, exchange(): return lax.ppermute(value, axis, pairs)  67.9 us
    unnamed x182, local copies, waits for them, and re-layouts  28.3 us
    ppermute x5, starting transfers between devices, shifted(): return lax.ppermute(value, axis, pairs)  15 us
    ppermute x5, waiting for transfers between devices, shifted(): return lax.ppermute(value, axis, pairs)  11 us
    dot_general x3, matrix products, einsum(): return jnp.einsum(spec, *operands, preferred_element_type=F32)  10.7 us
  transfers between devices with their start and end apart: 75, of which 24 were waited for; matrix products, arithmetic and copies ran while one was open for 8% of the time, Pallas kernels for 26%

profile of v5, /device:TPU:0, one launch (start us, length us, event | category | flops | bytes accessed | tf_op | source)
XLA Modules:
  0.0 411.6 jit_solution(1380243915358348498)
XLA Ops:
  2.8 4.9 %collective-permute-start.5 = (bf16[4,288]{1,0:T(4,128)(2,1)S(1)}, bf16[4,288]{1,0:T(4,128)(2,1)S(1)}, u32[]{:S(2)}, u32[]{:S(2)}) collective-permute-start(bf16[4,288]{1,0:T(4,128)(2,1)S(1)} %select_convert_fusion), channel_id=1, source_target_pairs={{0,4},{4,8},{8,12},{12,16},{16,20},{20,24},{24,28},{1,5},{5,9},{9,... | collective-permute-start | bytes 6920 | tf_op jit(solution)/shard_map/ppermute | solution.py:33
  37.6 4.2 %collective-permute-start.4 = (bf16[4,288,256]{2,1,0:T(8,128)(2,1)S(1)}, bf16[4,288,256]{2,1,0:T(8,128)(2,1)S(1)}, u32[]{:S(2)}, u32[]{:S(2)}) collective-permute-start(bf16[4,288,256]{2,1,0:T(8,128)(2,1)S(1)} %shard_map.218), channel_id=1, source_target_pairs={{0,4},{4,8},{8,12},{12,16},{16,20},{20,24},{24,28},{1,5},{5,9},{9,... | collective-permute-start | bytes 1769480 | tf_op jit(solution)/shard_map/ppermute | solution.py:33
  44.8 13.6 %collective-permute-done.9.p2.r2 = bf16[4,288,256]{2,1,0:T(8,128)(2,1)S(1)} collective-permute-done((bf16[4,288,256]{2,1,0:T(8,128)(2,1)S(1)}, bf16[4,288,256]{2,1,0:T(8,128)(2,1)S(1)}, u32[]{:S(2)}, u32[]{:S(2)}) %collective-permute-start.9) | collective-permute-done | bytes 589856 | tf_op jit(solution)/shard_map/ppermute | solution.py:27
  63.6 18.7 %shard_map.221 = (bf16[4,288,256]{2,1,0:T(8,128)(2,1)S(1)}, bf16[4,288,256]{2,1,0:T(8,128)(2,1)S(1)}, f32[4,288,256]{2,1,0:T(8,128)}, f32[4,288,256]{2,1,0:T(8,1...) custom-call(s32[1]{0:T(128)} %bitcast.4.s_ref.me_ref, ...), custom_call_target="tpu_custom_call" | custom-call | flops 1800000000 | bytes 1000 | tf_op jit(solution)/shard_map/pallas_call | solution.py:81
  90.6 10.6 %collective-permute-done.16.across = bf16[4,288,256]{2,1,0:T(8,128)(2,1)S(1)} collective-permute-done((bf16[4,288,256]{2,1,0:T(8,128)(2,1)S(1)}, bf16[4,288,256]{2,1,0:T(8,128)(2,1)S(1)}, u32[]{:S(2)}, u32[]{:S(2)}) %collective-permute-start.16) | collective-permute-done | bytes 589856 | tf_op jit(solution)/shard_map/ppermute | solution.py:27
  105.5 13.5 %collective-permute-done.18.p2 = bf16[4,288,256]{2,1,0:T(8,128)(2,1)S(1)} collective-permute-done((bf16[4,288,256]{2,1,0:T(8,128)(2,1)S(1)}, bf16[4,288,256]{2,1,0:T(8,128)(2,1)S(1)}, u32[]{:S(2)}, u32[]{:S(2)}) %collective-permute-start.18) | collective-permute-done | bytes 589856 | tf_op jit(solution)/shard_map/ppermute | solution.py:27
  121.0 23.9 %shard_map.225 = (bf16[4,288,256]{2,1,0:T(8,128)(2,1)}, bf16[4,288,256]{2,1,0:T(8,128)(2,1)}, f32[4,288,256]{2,1,0:T(8,128)}, f32[4,288,256]{2,1,0:T(8,128)}, bf...) custom-call(s32[1]{0:T(128)} %bitcast.4.s_ref.me_ref, ...), custom_call_target="tpu_custom_call" | custom-call | flops 2400000000 | bytes 1000 | tf_op jit(solution)/shard_map/pallas_call | solution.py:81
  169.3 3.8 shard_map.230
  181.5 7.9 %collective-permute-done.70 = bf16[8,8,576]{2,1,0:T(8,128)(2,1)S(1)} collective-permute-done((bf16[8,8,576]{2,1,0:T(8,128)(2,1)S(1)}, bf16[8,8,576]{2,1,0:T(8,128)(2,1)S(1)}, u32[]{:S(2)}, u32[]{:S(2)}) %collective-permute-start.70) | collective-permute-done | bytes 73760 | tf_op jit(solution)/shard_map/ppermute | solution.py:27
  210.9 18.1 %shard_map.236 = (bf16[4,288,256]{2,1,0:T(8,128)(2,1)S(1)}, bf16[4,304,256]{2,1,0:T(8,128)(2,1)}, f32[4,288,256]{2,1,0:T(8,128)}, f32[4,288,256]{2,1,0:T(8,128)}...) custom-call(s32[1]{0:T(128)} %bitcast.4.s_ref.me_ref, ...), custom_call_target="tpu_custom_call" | custom-call | flops 1800000000 | bytes 1000 | tf_op jit(solution)/shard_map/pallas_call | solution.py:81
  237.8 4.9 %shard_map.238 = (bf16[2,144,1152]{2,1,0:T(8,128)(2,1)S(1)}, f32[2,144,1152]{2,1,0:T(8,128)S(1)}, bf16[2,144,1152]{2,1,0:T(8,128)(2,1)S(1)}, f32[2,144,1152]{2,1,0:T(8,128)S(1)}) custom-call(s32[2]{0:T(128)S(1)} %pad_add_fusion.1.s_ref, bf16[864,1024]{1,0:T(8,128)(2,1)S(1)} %copy-done.35, bf16[288,1024]{1,0:T(8,128)(2,1)S(1)} %copy-done.62, ...), custom_call_target="tpu_custom_call" | custom-call | flops 300000000 | bytes 1000 | tf_op jit(solution)/shard_map/pallas_call | solution.py:81
  252.1 3.8 shard_map.241
  257.9 15.2 %collective-permute-done.41.got_a.got_b = bf16[2,144,1152]{2,1,0:T(8,128)(2,1)S(1)} collective-permute-done((bf16[2,144,1152]{2,1,0:T(8,128)(2,1)S(1)}, bf16[2,144,1152]{2,1,0:T(8,128)(2,1)S(1)}, u32[]{:S(2)}, u32[]{:S(2)}) %collective-permute-start.41) | collective-permute-done | bytes 663584 | tf_op jit(solution)/shard_map/ppermute | solution.py:27
  287.6 5.5 %collective-permute-done.46 = bf16[1,144,1536]{2,1,0:T(8,128)(2,1)S(1)} collective-permute-done((bf16[1,144,1536]{2,1,0:T(8,128)(2,1)S(1)}, bf16[1,144,1536]{2,1,0:T(8,128)(2,1)S(1)}, u32[]{:S(2)}, u32[]{:S(2)}) %collective-permute-start.46) | collective-permute-done | bytes 442400 | tf_op jit(solution)/shard_map/ppermute | solution.py:27
  294.3 3.9 collective-permute-done.47.refs_1_
  298.2 13.8 %collective-permute-start.62 = (bf16[1,288,1536]{2,1,0:T(8,128)(2,1)S(1)}, bf16[1,288,1536]{2,1,0:T(8,128)(2,1)S(1)}, u32[]{:S(2)}, u32[]{:S(2)}) collective-permute-start(bf16[1,288,1536]{2,1,0:T(8,128)(2,1)S(1)} %maximum_select_fusion.refs_0_), channel_id=1, source_target_pairs={{0,4},{4,0},{8,12},{12,8},{16,20},{20,16},{24,28},{28,24},{1,5},{5... | collective-permute-start | bytes 2654216 | tf_op jit(solution)/shard_map/ppermute | solution.py:27
  313.3 5.4 %shard_map.245 = f32[8,288,256]{2,1,0:T(8,128)} custom-call(s32[2]{0:T(128)S(1)} %pad_add_fusion.s_ref, f32[4,288,256]{2,1,0:T(8,128)S(1)} %copy-done.53, bf16[4,288,256]{2,1,0:T(8,128)(2,1)} %collective-permute-done.47.refs_1_), custom_call_target="tpu_custom_call" | custom-call | flops 300000000 | bytes 1000 | tf_op jit(solution)/shard_map/pallas_call | solution.py:81
  331.7 10.4 %collective-permute-done.53 = bf16[1,25,288]{2,1,0:T(8,128)(2,1)S(1)} collective-permute-done((bf16[1,25,288]{2,1,0:T(8,128)(2,1)S(1)}, bf16[1,25,288]{2,1,0:T(8,128)(2,1)S(1)}, u32[]{:S(2)}, u32[]{:S(2)}) %collective-permute-start.53) | collective-permute-done | bytes 14432 | tf_op jit(solution)/shard_map/ppermute | solution.py:27
  344.3 7.1 %collective-permute-done.55.refs_1_ = bf16[4,288,256]{2,1,0:T(8,128)(2,1)S(1)} collective-permute-done((bf16[4,288,256]{2,1,0:T(8,128)(2,1)S(1)}, bf16[4,288,256]{2,1,0:T(8,128)(2,1)S(1)}, u32[]{:S(2)}, u32[]{:S(2)}) %collective-permute-start.55) | collective-permute-done | bytes 589856 | tf_op jit(solution)/shard_map/ppermute | solution.py:33
  361.0 4.2 %collective-permute-done.59 = bf16[1,72,1152]{2,1,0:T(8,128)(2,1)S(1)} collective-permute-done((bf16[1,72,1152]{2,1,0:T(8,128)(2,1)S(1)}, bf16[1,72,1152]{2,1,0:T(8,128)(2,1)S(1)}, u32[]{:S(2)}, u32[]{:S(2)}) %collective-permute-start.59) | collective-permute-done | bytes 165920 | tf_op jit(solution)/shard_map/ppermute | solution.py:27
  365.7 18.9 %collective-permute-done.61.refs_1_ = bf16[1,384,1152]{2,1,0:T(8,128)(2,1)S(1)} collective-permute-done((bf16[1,384,1152]{2,1,0:T(8,128)(2,1)S(1)}, bf16[1,384,1152]{2,1,0:T(8,128)(2,1)S(1)}, u32[]{:S(2)}, u32[]{:S(2)}) %collective-permute-start.61) | collective-permute-done | bytes 884768 | tf_op jit(solution)/shard_map/ppermute | solution.py:27
  386.5 5.4 %shard_map.250 = f32[1152,2,768]{2,1,0:T(2,128)} custom-call(s32[2]{0:T(128)S(1)} %copy-done.72, bf16[1,288,1536]{2,1,0:T(8,128)(2,1)S(1)} %maximum_select_fusion.refs_0_, bf16[1,288,1536]{2,1,0:T(8,128)(2,1)S(1)} %collective-permute-done.62.refs_1_, bf16[1,288,1536]{2,1,0:T(8,128)(2,1)S(1)} %maximum_select_fusion.2.refs_2_, ...), custom_call_target="tpu_custom_call" | custom-call | flops 300000000 | bytes 1000 | tf_op jit(solution)/shard_map/pallas_call | solution.py:81
  397.0 4.5 %fusion.1 = f32[6,288,1152]{2,1,0:T(8,128)} fusion(bf16[6,32,288]{2,0,1:T(8,128)(2,1)S(1)} %bitcast.88, bf16[32,1152]{1,0:T(8,128)(2,1)S(1)} %broadcast_select_fusion), kind=kOutput, calls=%fused_computation.30 | convolution fusion | flops 127401984 | bytes 8146944 | tf_op jit(solution)/shard_map/kbf,bd->kfd/dot_general | solution.py:635
  406.7 4.7 %shard_map.251 = (f32[3,288,1152]{2,1,0:T(8,128)}, f32[288,1152]{1,0:T(8,128)}) custom-call(s32[2]{0:T(128)S(1)} %pad_add_fusion.1.s_ref, bf16[2,144,1152]{2,1,0:T(8,128)(2,1)S(1)} %maximum_select_fusion.3.mine1, bf16[2,144,1152]{2,1,0:T(8,128)(2,1)S(1)} %collective-permute-done.71.other1, bf16[2,144,1152]{2,1,0:T(8,128)(2,1)S(1)} %maximum_select_fusion.4.mine2, ...), custom_call_target="tpu_custom_call" | custom-call | flops 300000000 | bytes 1000 | tf_op jit(solution)/shard_map/pallas_call | solution.py:81
  (439 shorter events, 181.6 us)
Async XLA Ops:
  147.1 28.1 %collective-permute-start.69 = (bf16[8,8,288]{2,1,0:T(8,128)(2,1)S(1)}, bf16[8,8,288]{2,1,0:T(8,128)(2,1)S(1)}, u32[]{:S(2)}, u32[]{:S(2)}) collective-permute-start(bf16[8,8,288]{2,1,0:T(8,128)(2,1)S(1)} %get-tuple-element.541), channel_id=1, source_target_pairs={{0,1},{1,0},{2,3},{3,2},{4,5},{5,4},{6,7},{7,6},{8,9},{9,8},{10,11... | collective-permute-start | bytes 110600 | tf_op jit(solution)/shard_map/ppermute | solution.py:27
  157.1 22.6 %collective-permute-start.25 = (bf16[1,288,1536]{2,1,0:T(8,128)(2,1)S(1)}, bf16[1,288,1536]{2,1,0:T(8,128)(2,1)S(1)}, u32[]{:S(2)}, u32[]{:S(2)}) collective-permute-start(bf16[1,288,1536]{2,1,0:T(8,128)(2,1)S(1)} %get-tuple-element.357), channel_id=1, source_target_pairs={{0,4},{4,0},{8,12},{12,8},{16,20},{20,16},{24,28},{28,24},{1,5},{5... | collective-permute-start | bytes 2654216 | tf_op jit(solution)/shard_map/ppermute | solution.py:27
  161.5 30.0 %collective-permute-start.26 = (bf16[1,384,1152]{2,1,0:T(8,128)(2,1)S(1)}, bf16[1,384,1152]{2,1,0:T(8,128)(2,1)S(1)}, u32[]{:S(2)}, u32[]{:S(2)}) collective-permute-start(bf16[1,384,1152]{2,1,0:T(8,128)(2,1)S(1)} %get-tuple-element.361), channel_id=1, source_target_pairs={{0,8},{4,12},{8,0},{12,4},{16,24},{20,28},{24,16},{28,20},{1,9},{5... | collective-permute-start | bytes 2654216 | tf_op jit(solution)/shard_map/ppermute | solution.py:27
  168.7 32.2 %collective-permute-start.28 = (bf16[1,288,1536]{2,1,0:T(8,128)(2,1)}, bf16[1,288,1536]{2,1,0:T(8,128)(2,1)}, u32[]{:S(2)}, u32[]{:S(2)}) collective-permute-start(bf16[1,288,1536]{2,1,0:T(8,128)(2,1)} %get-tuple-element.365), channel_id=1, source_target_pairs={{0,4},{4,0},{8,12},{12,8},{16,20},{20,16},{24,28},{28,24},{1,5},{5... | collective-permute-start | bytes 2654216 | tf_op jit(solution)/shard_map/ppermute | solution.py:27
  206.2 23.7 %collective-permute-start.33 = (bf16[1,72,1536]{2,1,0:T(8,128)(2,1)S(1)}, bf16[1,72,1536]{2,1,0:T(8,128)(2,1)S(1)}, u32[]{:S(2)}, u32[]{:S(2)}) collective-permute-start(bf16[1,72,1536]{2,1,0:T(8,128)(2,1)S(1)} %get-tuple-element.398), channel_id=1, source_target_pairs={{0,16},{4,20},{8,24},{12,28},{16,0},{20,4},{24,8},{28,12},{1,17},{... | collective-permute-start | bytes 663560 | tf_op jit(solution)/shard_map/ppermute | solution.py:27
  209.1 39.8 %collective-permute-start.38 = (bf16[4,288,256]{2,1,0:T(8,128)(2,1)}, bf16[4,288,256]{2,1,0:T(8,128)(2,1)}, u32[]{:S(2)}, u32[]{:S(2)}) collective-permute-start(bf16[4,288,256]{2,1,0:T(8,128)(2,1)} %get-tuple-element.446), channel_id=1, source_target_pairs={{0,1},{1,0},{2,3},{3,2},{4,5},{5,4},{6,7},{7,6},{8,9},{9,8},{10,11... | collective-permute-start | bytes 1769480 | tf_op jit(solution)/shard_map/ppermute | solution.py:27
  209.1 33.6 %collective-permute-start.35 = (bf16[1,144,1536]{2,1,0:T(8,128)(2,1)}, bf16[1,144,1536]{2,1,0:T(8,128)(2,1)}, u32[]{:S(2)}, u32[]{:S(2)}) collective-permute-start(bf16[1,144,1536]{2,1,0:T(8,128)(2,1)} %get-tuple-element.394), channel_id=1, source_target_pairs={{0,8},{4,12},{8,0},{12,4},{16,24},{20,28},{24,16},{28,20},{1,9},{5... | collective-permute-start | bytes 1327112 | tf_op jit(solution)/shard_map/ppermute | solution.py:27
  209.4 41.3 %collective-permute-start.39 = (bf16[4,288,256]{2,1,0:T(8,128)(2,1)}, bf16[4,288,256]{2,1,0:T(8,128)(2,1)}, u32[]{:S(2)}, u32[]{:S(2)}) collective-permute-start(bf16[4,288,256]{2,1,0:T(8,128)(2,1)} %shard_map.233), channel_id=1, source_target_pairs={{0,2},{1,3},{2,0},{3,1},{4,6},{5,7},{6,4},{7,5},{8,10},{9,11},{10,... | collective-permute-start | bytes 1769480 | tf_op jit(solution)/shard_map/ppermute | solution.py:27
  246.0 33.3 %collective-permute-start.43 = (bf16[4,288,256]{2,1,0:T(8,128)(2,1)S(1)}, bf16[4,288,256]{2,1,0:T(8,128)(2,1)S(1)}, u32[]{:S(2)}, u32[]{:S(2)}) collective-permute-start(bf16[4,288,256]{2,1,0:T(8,128)(2,1)S(1)} %copy-done.74), channel_id=1, source_target_pairs={{0,1},{1,0},{2,3},{3,2},{4,5},{5,4},{6,7},{7,6},{8,9},{9,8},{10,11... | collective-permute-start | bytes 1769480 | tf_op jit(solution)/shard_map/ppermute | solution.py:27
  246.8 26.3 %collective-permute-start.41 = (bf16[2,144,1152]{2,1,0:T(8,128)(2,1)S(1)}, bf16[2,144,1152]{2,1,0:T(8,128)(2,1)S(1)}, u32[]{:S(2)}, u32[]{:S(2)}) collective-permute-start(bf16[2,144,1152]{2,1,0:T(8,128)(2,1)S(1)} %get-tuple-element.433), channel_id=1, source_target_pairs={{0,8},{4,12},{8,0},{12,4},{16,24},{20,28},{24,16},{28,20},{1,9},{5... | collective-permute-start | bytes 1990664 | tf_op jit(solution)/shard_map/ppermute | solution.py:27
  248.9 26.4 %collective-permute-start.42 = (bf16[2,144,1152]{2,1,0:T(8,128)(2,1)S(1)}, bf16[2,144,1152]{2,1,0:T(8,128)(2,1)S(1)}, u32[]{:S(2)}, u32[]{:S(2)}) collective-permute-start(bf16[2,144,1152]{2,1,0:T(8,128)(2,1)S(1)} %get-tuple-element.435), channel_id=1, source_target_pairs={{0,4},{4,0},{8,12},{12,8},{16,20},{20,16},{24,28},{28,24},{1,5},{5... | collective-permute-start | bytes 1990664 | tf_op jit(solution)/shard_map/ppermute | solution.py:27
  250.7 34.7 %collective-permute-start.45 = (bf16[1,72,1536]{2,1,0:T(8,128)(2,1)S(1)}, bf16[1,72,1536]{2,1,0:T(8,128)(2,1)S(1)}, u32[]{:S(2)}, u32[]{:S(2)}) collective-permute-start(bf16[1,72,1536]{2,1,0:T(8,128)(2,1)S(1)} %get-tuple-element.439), channel_id=1, source_target_pairs={{0,16},{4,20},{8,24},{12,28},{16,0},{20,4},{24,8},{28,12},{1,17},{... | collective-permute-start | bytes 663560 | tf_op jit(solution)/shard_map/ppermute | solution.py:27
  256.4 24.2 %collective-permute-start.44 = (bf16[4,304,256]{2,1,0:T(8,128)(2,1)S(1)}, bf16[4,304,256]{2,1,0:T(8,128)(2,1)S(1)}, u32[]{:S(2)}, u32[]{:S(2)}) collective-permute-start(bf16[4,304,256]{2,1,0:T(8,128)(2,1)S(1)} %shard_map.240), channel_id=1, source_target_pairs={{0,2},{1,3},{2,0},{3,1},{4,6},{5,7},{6,4},{7,5},{8,10},{9,11},{10,... | collective-permute-start | bytes 1867784 | tf_op jit(solution)/shard_map/ppermute | solution.py:27
  273.1 46.4 %collective-permute-start.49 = (bf16[1,96,1152]{2,1,0:T(8,128)(2,1)}, bf16[1,96,1152]{2,1,0:T(8,128)(2,1)}, u32[]{:S(2)}, u32[]{:S(2)}) collective-permute-start(bf16[1,96,1152]{2,1,0:T(8,128)(2,1)} %add_convert_fusion.1), channel_id=1, source_target_pairs={{0,16},{4,20},{8,24},{12,28},{16,0},{20,4},{24,8},{28,12},{1,17},{... | collective-permute-start | bytes 663560 | tf_op jit(solution)/shard_map/ppermute | solution.py:27
  280.6 38.0 %collective-permute-start.48 = (bf16[2,72,1152]{2,1,0:T(8,128)(2,1)}, bf16[2,72,1152]{2,1,0:T(8,128)(2,1)S(1)}, u32[]{:S(2)}, u32[]{:S(2)}) collective-permute-start(bf16[2,72,1152]{2,1,0:T(8,128)(2,1)} %get-tuple-element.460), channel_id=1, source_target_pairs={{0,4},{4,0},{8,12},{12,8},{16,20},{20,16},{24,28},{28,24},{1,5},{5... | collective-permute-start | bytes 995336 | tf_op jit(solution)/shard_map/ppermute | solution.py:27
  285.3 35.7 %collective-permute-start.50 = (bf16[2,72,1152]{2,1,0:T(8,128)(2,1)}, bf16[2,72,1152]{2,1,0:T(8,128)(2,1)S(1)}, u32[]{:S(2)}, u32[]{:S(2)}) collective-permute-start(bf16[2,72,1152]{2,1,0:T(8,128)(2,1)} %get-tuple-element.464), channel_id=1, source_target_pairs={{0,8},{4,12},{8,0},{12,4},{16,24},{20,28},{24,16},{28,20},{1,9},{5... | collective-permute-start | bytes 995336 | tf_op jit(solution)/shard_map/ppermute | solution.py:27
  293.1 30.0 %collective-permute-start.51 = (bf16[1,72,1536]{2,1,0:T(8,128)(2,1)}, bf16[1,72,1536]{2,1,0:T(8,128)(2,1)}, u32[]{:S(2)}, u32[]{:S(2)}) collective-permute-start(bf16[1,72,1536]{2,1,0:T(8,128)(2,1)} %add_convert_fusion), channel_id=1, source_target_pairs={{0,16},{4,20},{8,24},{12,28},{16,0},{20,4},{24,8},{28,12},{1,17},{... | collective-permute-start | bytes 663560 | tf_op jit(solution)/shard_map/ppermute | solution.py:27
  298.2 88.3 %collective-permute-start.62 = (bf16[1,288,1536]{2,1,0:T(8,128)(2,1)S(1)}, bf16[1,288,1536]{2,1,0:T(8,128)(2,1)S(1)}, u32[]{:S(2)}, u32[]{:S(2)}) collective-permute-start(bf16[1,288,1536]{2,1,0:T(8,128)(2,1)S(1)} %maximum_select_fusion.refs_0_), channel_id=1, source_target_pairs={{0,4},{4,0},{8,12},{12,8},{16,20},{20,16},{24,28},{28,24},{1,5},{5... | collective-permute-start | bytes 2654216 | tf_op jit(solution)/shard_map/ppermute | solution.py:27
  318.7 23.5 %collective-permute-start.53 = (bf16[1,25,288]{2,1,0:T(8,128)(2,1)S(1)}, bf16[1,25,288]{2,1,0:T(8,128)(2,1)S(1)}, u32[]{:S(2)}, u32[]{:S(2)}) collective-permute-start(bf16[1,25,288]{2,1,0:T(8,128)(2,1)S(1)} %maximum_bitcast_fusion), channel_id=1, source_target_pairs={{0,4},{4,0},{8,12},{12,8},{16,20},{20,16},{24,28},{28,24},{1,5},{5... | collective-permute-start | bytes 43208 | tf_op jit(solution)/shard_map/ppermute | solution.py:27
  321.1 34.0 %collective-permute-start.56 = (bf16[1,192,1152]{2,1,0:T(8,128)(2,1)S(1)}, bf16[1,192,1152]{2,1,0:T(8,128)(2,1)S(1)}, u32[]{:S(2)}, u32[]{:S(2)}) collective-permute-start(bf16[1,192,1152]{2,1,0:T(8,128)(2,1)S(1)} %maximum_select_fusion.6), channel_id=1, source_target_pairs={{0,4},{4,0},{8,12},{12,8},{16,20},{20,16},{24,28},{28,24},{1,5},{5... | collective-permute-start | bytes 1327112 | tf_op jit(solution)/shard_map/ppermute | solution.py:27
  358.8 25.8 %collective-permute-start.61 = (bf16[1,384,1152]{2,1,0:T(8,128)(2,1)S(1)}, bf16[1,384,1152]{2,1,0:T(8,128)(2,1)S(1)}, u32[]{:S(2)}, u32[]{:S(2)}) collective-permute-start(bf16[1,384,1152]{2,1,0:T(8,128)(2,1)S(1)} %maximum_select_fusion.1.refs_0_), channel_id=1, source_target_pairs={{0,8},{4,12},{8,0},{12,4},{16,24},{20,28},{24,16},{28,20},{1,9},{5... | collective-permute-start | bytes 2654216 | tf_op jit(solution)/shard_map/ppermute | solution.py:27
  360.9 25.6 %collective-permute-start.63 = (bf16[1,288,1536]{2,1,0:T(8,128)(2,1)S(1)}, bf16[1,288,1536]{2,1,0:T(8,128)(2,1)S(1)}, u32[]{:S(2)}, u32[]{:S(2)}) collective-permute-start(bf16[1,288,1536]{2,1,0:T(8,128)(2,1)S(1)} %maximum_select_fusion.2.refs_2_), channel_id=1, source_target_pairs={{0,4},{4,0},{8,12},{12,8},{16,20},{20,16},{24,28},{28,24},{1,5},{5... | collective-permute-start | bytes 2654216 | tf_op jit(solution)/shard_map/ppermute | solution.py:27
  365.3 26.7 %collective-permute-start.64 = (bf16[2,72,1152]{2,1,0:T(8,128)(2,1)S(1)}, bf16[2,72,1152]{2,1,0:T(8,128)(2,1)S(1)}, u32[]{:S(2)}, u32[]{:S(2)}) collective-permute-start(bf16[2,72,1152]{2,1,0:T(8,128)(2,1)S(1)} %maximum_select_fusion.8), channel_id=1, source_target_pairs={{0,4},{4,0},{8,12},{12,8},{16,20},{20,16},{24,28},{28,24},{1,5},{5... | collective-permute-start | bytes 995336 | tf_op jit(solution)/shard_map/ppermute | solution.py:27
  365.5 26.6 %collective-permute-start.65 = (bf16[2,72,1152]{2,1,0:T(8,128)(2,1)S(1)}, bf16[2,72,1152]{2,1,0:T(8,128)(2,1)S(1)}, u32[]{:S(2)}, u32[]{:S(2)}) collective-permute-start(bf16[2,72,1152]{2,1,0:T(8,128)(2,1)S(1)} %maximum_select_fusion.9), channel_id=1, source_target_pairs={{0,8},{4,12},{8,0},{12,4},{16,24},{20,28},{24,16},{28,20},{1,9},{5... | collective-permute-start | bytes 995336 | tf_op jit(solution)/shard_map/ppermute | solution.py:27
  (139 other events, 1490.6 us)

commit v6 on v5

--- a/solution.py
+++ b/solution.py
@@ -1133,7 +1133,7 @@
     def finish_up():
         indices = jnp.concatenate([up1.first(), up2.first()])
         done.up = order(
-            lambda *a: paired(indices, a, 2, features // 8), up1.own, up1.received, up2.own, up2.received
+            lambda *a: paired(indices, a, 2, features // 4), up1.own, up1.received, up2.own, up2.received
         )
 
     done = types.SimpleNamespace()

time: 416 us -> 416 us (level)
    ppermute x5, waiting for transfers between devices: 11 us -> 19.5 us  [shifted(): return lax.ppermute(value, axis, pairs)]
    ppermute x70, waiting for transfers between devices: 116 us -> 110 us  [exchange(): return lax.ppermute(value, axis, pairs)]
  transfers between devices with their start and end apart: 75 -> 75, of which waited for: 24 -> 27; matrix products, arithmetic and copies ran while one was open for 8% -> 8% of each run, Pallas kernels for 26% -> 25%
where the time goes in v6:
time: 416 us; the launch traced here: 413 us
  Pallas kernels  136 us (33%)
  waiting for transfers between devices  129 us (31%)
  starting transfers between devices  82.8 us (20%)
  local copies, waits for them, and re-layouts  32.8 us (8%)
  other arithmetic  17.5 us (4%)
  matrix products  10.7 us (3%)
    pallas_call x38, Pallas kernels, call(): pl.pallas_call(kernel, grid_spec=pltpu.PrefetchScalarGridSpec(num_scalar_...  134 us
    ppermute x70, waiting for transfers between devices, exchange(): return lax.ppermute(value, axis, pairs)  110 us
    ppermute x70, starting transfers between devices, exchange(): return lax.ppermute(value, axis, pairs)  68 us
    unnamed x182, local copies, waits for them, and re-layouts  28.3 us
    ppermute x5, waiting for transfers between devices, shifted(): return lax.ppermute(value, axis, pairs)  19.5 us
    ppermute x5, starting transfers between devices, shifted(): return lax.ppermute(value, axis, pairs)  14.7 us
    dot_general x3, matrix products, einsum(): return jnp.einsum(spec, *operands, preferred_element_type=F32)  10.7 us
  transfers between devices with their start and end apart: 75, of which 27 were waited for; matrix products, arithmetic and copies ran while one was open for 8% of the time, Pallas kernels for 25%

profile of v6, /device:TPU:0, one launch (start us, length us, event | category | flops | bytes accessed | tf_op | source)
XLA Modules:
  0.0 412.5 jit_solution(6567408475694865500)
XLA Ops:
  2.8 4.9 %collective-permute-start.5 = (bf16[4,288]{1,0:T(4,128)(2,1)S(1)}, bf16[4,288]{1,0:T(4,128)(2,1)S(1)}, u32[]{:S(2)}, u32[]{:S(2)}) collective-permute-start(bf16[4,288]{1,0:T(4,128)(2,1)S(1)} %select_convert_fusion), channel_id=1, source_target_pairs={{0,4},{4,8},{8,12},{12,16},{16,20},{20,24},{24,28},{1,5},{5,9},{9,... | collective-permute-start | bytes 6920 | tf_op jit(solution)/shard_map/ppermute | solution.py:33
  37.6 3.9 collective-permute-start.4
  44.5 13.6 %collective-permute-done.9.p2.r2 = bf16[4,288,256]{2,1,0:T(8,128)(2,1)S(1)} collective-permute-done((bf16[4,288,256]{2,1,0:T(8,128)(2,1)S(1)}, bf16[4,288,256]{2,1,0:T(8,128)(2,1)S(1)}, u32[]{:S(2)}, u32[]{:S(2)}) %collective-permute-start.9) | collective-permute-done | bytes 589856 | tf_op jit(solution)/shard_map/ppermute | solution.py:27
  63.3 18.7 %shard_map.221 = (bf16[4,288,256]{2,1,0:T(8,128)(2,1)S(1)}, bf16[4,288,256]{2,1,0:T(8,128)(2,1)S(1)}, f32[4,288,256]{2,1,0:T(8,128)}, f32[4,288,256]{2,1,0:T(8,1...) custom-call(s32[1]{0:T(128)} %bitcast.4.s_ref.me_ref, ...), custom_call_target="tpu_custom_call" | custom-call | flops 1800000000 | bytes 1000 | tf_op jit(solution)/shard_map/pallas_call | solution.py:81
  90.3 10.6 %collective-permute-done.16.across = bf16[4,288,256]{2,1,0:T(8,128)(2,1)S(1)} collective-permute-done((bf16[4,288,256]{2,1,0:T(8,128)(2,1)S(1)}, bf16[4,288,256]{2,1,0:T(8,128)(2,1)S(1)}, u32[]{:S(2)}, u32[]{:S(2)}) %collective-permute-start.16) | collective-permute-done | bytes 589856 | tf_op jit(solution)/shard_map/ppermute | solution.py:27
  105.2 13.5 %collective-permute-done.18.p2 = bf16[4,288,256]{2,1,0:T(8,128)(2,1)S(1)} collective-permute-done((bf16[4,288,256]{2,1,0:T(8,128)(2,1)S(1)}, bf16[4,288,256]{2,1,0:T(8,128)(2,1)S(1)}, u32[]{:S(2)}, u32[]{:S(2)}) %collective-permute-start.18) | collective-permute-done | bytes 589856 | tf_op jit(solution)/shard_map/ppermute | solution.py:27
  120.7 23.9 %shard_map.225 = (bf16[4,288,256]{2,1,0:T(8,128)(2,1)}, bf16[4,288,256]{2,1,0:T(8,128)(2,1)}, f32[4,288,256]{2,1,0:T(8,128)}, f32[4,288,256]{2,1,0:T(8,128)}, bf...) custom-call(s32[1]{0:T(128)} %bitcast.4.s_ref.me_ref, ...), custom_call_target="tpu_custom_call" | custom-call | flops 2400000000 | bytes 1000 | tf_op jit(solution)/shard_map/pallas_call | solution.py:81
  169.1 3.8 shard_map.230
  175.7 3.7 collective-permute-done.25.got_a.got_b
  181.2 7.9 %collective-permute-done.70 = bf16[8,8,576]{2,1,0:T(8,128)(2,1)S(1)} collective-permute-done((bf16[8,8,576]{2,1,0:T(8,128)(2,1)S(1)}, bf16[8,8,576]{2,1,0:T(8,128)(2,1)S(1)}, u32[]{:S(2)}, u32[]{:S(2)}) %collective-permute-start.70) | collective-permute-done | bytes 73760 | tf_op jit(solution)/shard_map/ppermute | solution.py:27
  210.7 18.1 %shard_map.236 = (bf16[4,288,256]{2,1,0:T(8,128)(2,1)S(1)}, bf16[4,304,256]{2,1,0:T(8,128)(2,1)}, f32[4,288,256]{2,1,0:T(8,128)}, f32[4,288,256]{2,1,0:T(8,128)}...) custom-call(s32[1]{0:T(128)} %bitcast.4.s_ref.me_ref, ...), custom_call_target="tpu_custom_call" | custom-call | flops 1800000000 | bytes 1000 | tf_op jit(solution)/shard_map/pallas_call | solution.py:81
  237.5 4.9 %shard_map.238 = (bf16[2,144,1152]{2,1,0:T(8,128)(2,1)S(1)}, f32[2,144,1152]{2,1,0:T(8,128)S(1)}, bf16[2,144,1152]{2,1,0:T(8,128)(2,1)S(1)}, f32[2,144,1152]{2,1,0:T(8,128)S(1)}) custom-call(s32[2]{0:T(128)S(1)} %pad_add_fusion.1.s_ref, bf16[864,1024]{1,0:T(8,128)(2,1)S(1)} %copy-done.35, bf16[288,1024]{1,0:T(8,128)(2,1)S(1)} %copy-done.62, ...), custom_call_target="tpu_custom_call" | custom-call | flops 300000000 | bytes 1000 | tf_op jit(solution)/shard_map/pallas_call | solution.py:81
  251.9 3.8 shard_map.241
  257.7 15.1 %collective-permute-done.41.got_a.got_b = bf16[2,144,1152]{2,1,0:T(8,128)(2,1)S(1)} collective-permute-done((bf16[2,144,1152]{2,1,0:T(8,128)(2,1)S(1)}, bf16[2,144,1152]{2,1,0:T(8,128)(2,1)S(1)}, u32[]{:S(2)}, u32[]{:S(2)}) %collective-permute-start.41) | collective-permute-done | bytes 663584 | tf_op jit(solution)/shard_map/ppermute | solution.py:27
  287.4 5.4 %collective-permute-done.46 = bf16[1,144,1536]{2,1,0:T(8,128)(2,1)S(1)} collective-permute-done((bf16[1,144,1536]{2,1,0:T(8,128)(2,1)S(1)}, bf16[1,144,1536]{2,1,0:T(8,128)(2,1)S(1)}, u32[]{:S(2)}, u32[]{:S(2)}) %collective-permute-start.46) | collective-permute-done | bytes 442400 | tf_op jit(solution)/shard_map/ppermute | solution.py:27
  294.0 3.9 collective-permute-done.47.refs_1_
  298.0 13.8 %collective-permute-start.62 = (bf16[1,288,1536]{2,1,0:T(8,128)(2,1)S(1)}, bf16[1,288,1536]{2,1,0:T(8,128)(2,1)S(1)}, u32[]{:S(2)}, u32[]{:S(2)}) collective-permute-start(bf16[1,288,1536]{2,1,0:T(8,128)(2,1)S(1)} %maximum_select_fusion.refs_0_), channel_id=1, source_target_pairs={{0,4},{4,0},{8,12},{12,8},{16,20},{20,16},{24,28},{28,24},{1,5},{5... | collective-permute-start | bytes 2654216 | tf_op jit(solution)/shard_map/ppermute | solution.py:27
  313.1 5.4 %shard_map.245 = f32[8,288,256]{2,1,0:T(8,128)} custom-call(s32[2]{0:T(128)S(1)} %pad_add_fusion.s_ref, f32[4,288,256]{2,1,0:T(8,128)S(1)} %copy-done.53, bf16[4,288,256]{2,1,0:T(8,128)(2,1)} %collective-permute-done.47.refs_1_), custom_call_target="tpu_custom_call" | custom-call | flops 300000000 | bytes 1000 | tf_op jit(solution)/shard_map/pallas_call | solution.py:81
  335.6 15.6 %collective-permute-done.55.refs_1_ = bf16[4,288,256]{2,1,0:T(8,128)(2,1)S(1)} collective-permute-done((bf16[4,288,256]{2,1,0:T(8,128)(2,1)S(1)}, bf16[4,288,256]{2,1,0:T(8,128)(2,1)S(1)}, u32[]{:S(2)}, u32[]{:S(2)}) %collective-permute-start.55) | collective-permute-done | bytes 589856 | tf_op jit(solution)/shard_map/ppermute | solution.py:33
  351.2 3.6 shard_map.248
  365.2 18.5 %collective-permute-done.61.refs_1_ = bf16[1,384,1152]{2,1,0:T(8,128)(2,1)S(1)} collective-permute-done((bf16[1,384,1152]{2,1,0:T(8,128)(2,1)S(1)}, bf16[1,384,1152]{2,1,0:T(8,128)(2,1)S(1)}, u32[]{:S(2)}, u32[]{:S(2)}) %collective-permute-start.61) | collective-permute-done | bytes 884768 | tf_op jit(solution)/shard_map/ppermute | solution.py:27
  385.7 4.4 %shard_map.250 = f32[1152,2,768]{2,1,0:T(2,128)} custom-call(s32[2]{0:T(128)S(1)} %copy-done.72, bf16[1,288,1536]{2,1,0:T(8,128)(2,1)S(1)} %maximum_select_fusion.refs_0_, bf16[1,288,1536]{2,1,0:T(8,128)(2,1)S(1)} %collective-permute-done.62.refs_1_, bf16[1,288,1536]{2,1,0:T(8,128)(2,1)S(1)} %maximum_select_fusion.2.refs_2_, ...), custom_call_target="tpu_custom_call" | custom-call | flops 300000000 | bytes 1000 | tf_op jit(solution)/shard_map/pallas_call | solution.py:81
  396.3 4.5 %fusion.1 = f32[6,288,1152]{2,1,0:T(8,128)} fusion(bf16[6,32,288]{2,0,1:T(8,128)(2,1)S(1)} %bitcast.88, bf16[32,1152]{1,0:T(8,128)(2,1)S(1)} %broadcast_select_fusion), kind=kOutput, calls=%fused_computation.30 | convolution fusion | flops 127401984 | bytes 8146944 | tf_op jit(solution)/shard_map/kbf,bd->kfd/dot_general | solution.py:635
  407.4 4.7 %shard_map.251 = (f32[3,288,1152]{2,1,0:T(8,128)}, f32[288,1152]{1,0:T(8,128)}) custom-call(s32[2]{0:T(128)S(1)} %pad_add_fusion.1.s_ref, bf16[2,144,1152]{2,1,0:T(8,128)(2,1)S(1)} %maximum_select_fusion.3.mine1, bf16[2,144,1152]{2,1,0:T(8,128)(2,1)S(1)} %collective-permute-done.71.other1, bf16[2,144,1152]{2,1,0:T(8,128)(2,1)S(1)} %maximum_select_fusion.4.mine2, ...), custom_call_target="tpu_custom_call" | custom-call | flops 300000000 | bytes 1000 | tf_op jit(solution)/shard_map/pallas_call | solution.py:81
  (439 shorter events, 182.9 us)
Async XLA Ops:
  146.8 28.2 %collective-permute-start.69 = (bf16[8,8,288]{2,1,0:T(8,128)(2,1)S(1)}, bf16[8,8,288]{2,1,0:T(8,128)(2,1)S(1)}, u32[]{:S(2)}, u32[]{:S(2)}) collective-permute-start(bf16[8,8,288]{2,1,0:T(8,128)(2,1)S(1)} %get-tuple-element.541), channel_id=1, source_target_pairs={{0,1},{1,0},{2,3},{3,2},{4,5},{5,4},{6,7},{7,6},{8,9},{9,8},{10,11... | collective-permute-start | bytes 110600 | tf_op jit(solution)/shard_map/ppermute | solution.py:27
  161.3 29.9 %collective-permute-start.26 = (bf16[1,384,1152]{2,1,0:T(8,128)(2,1)S(1)}, bf16[1,384,1152]{2,1,0:T(8,128)(2,1)S(1)}, u32[]{:S(2)}, u32[]{:S(2)}) collective-permute-start(bf16[1,384,1152]{2,1,0:T(8,128)(2,1)S(1)} %get-tuple-element.361), channel_id=1, source_target_pairs={{0,8},{4,12},{8,0},{12,4},{16,24},{20,28},{24,16},{28,20},{1,9},{5... | collective-permute-start | bytes 2654216 | tf_op jit(solution)/shard_map/ppermute | solution.py:27
  168.5 32.2 %collective-permute-start.28 = (bf16[1,288,1536]{2,1,0:T(8,128)(2,1)}, bf16[1,288,1536]{2,1,0:T(8,128)(2,1)}, u32[]{:S(2)}, u32[]{:S(2)}) collective-permute-start(bf16[1,288,1536]{2,1,0:T(8,128)(2,1)} %get-tuple-element.365), channel_id=1, source_target_pairs={{0,4},{4,0},{8,12},{12,8},{16,20},{20,16},{24,28},{28,24},{1,5},{5... | collective-permute-start | bytes 2654216 | tf_op jit(solution)/shard_map/ppermute | solution.py:27
  205.9 23.7 %collective-permute-start.33 = (bf16[1,72,1536]{2,1,0:T(8,128)(2,1)S(1)}, bf16[1,72,1536]{2,1,0:T(8,128)(2,1)S(1)}, u32[]{:S(2)}, u32[]{:S(2)}) collective-permute-start(bf16[1,72,1536]{2,1,0:T(8,128)(2,1)S(1)} %get-tuple-element.398), channel_id=1, source_target_pairs={{0,16},{4,20},{8,24},{12,28},{16,0},{20,4},{24,8},{28,12},{1,17},{... | collective-permute-start | bytes 663560 | tf_op jit(solution)/shard_map/ppermute | solution.py:27
  208.9 39.8 %collective-permute-start.38 = (bf16[4,288,256]{2,1,0:T(8,128)(2,1)}, bf16[4,288,256]{2,1,0:T(8,128)(2,1)}, u32[]{:S(2)}, u32[]{:S(2)}) collective-permute-start(bf16[4,288,256]{2,1,0:T(8,128)(2,1)} %get-tuple-element.446), channel_id=1, source_target_pairs={{0,1},{1,0},{2,3},{3,2},{4,5},{5,4},{6,7},{7,6},{8,9},{9,8},{10,11... | collective-permute-start | bytes 1769480 | tf_op jit(solution)/shard_map/ppermute | solution.py:27
  208.9 33.6 %collective-permute-start.35 = (bf16[1,144,1536]{2,1,0:T(8,128)(2,1)}, bf16[1,144,1536]{2,1,0:T(8,128)(2,1)}, u32[]{:S(2)}, u32[]{:S(2)}) collective-permute-start(bf16[1,144,1536]{2,1,0:T(8,128)(2,1)} %get-tuple-element.394), channel_id=1, source_target_pairs={{0,8},{4,12},{8,0},{12,4},{16,24},{20,28},{24,16},{28,20},{1,9},{5... | collective-permute-start | bytes 1327112 | tf_op jit(solution)/shard_map/ppermute | solution.py:27
  209.2 41.3 %collective-permute-start.39 = (bf16[4,288,256]{2,1,0:T(8,128)(2,1)}, bf16[4,288,256]{2,1,0:T(8,128)(2,1)}, u32[]{:S(2)}, u32[]{:S(2)}) collective-permute-start(bf16[4,288,256]{2,1,0:T(8,128)(2,1)} %shard_map.233), channel_id=1, source_target_pairs={{0,2},{1,3},{2,0},{3,1},{4,6},{5,7},{6,4},{7,5},{8,10},{9,11},{10,... | collective-permute-start | bytes 1769480 | tf_op jit(solution)/shard_map/ppermute | solution.py:27
  245.8 33.4 %collective-permute-start.43 = (bf16[4,288,256]{2,1,0:T(8,128)(2,1)S(1)}, bf16[4,288,256]{2,1,0:T(8,128)(2,1)S(1)}, u32[]{:S(2)}, u32[]{:S(2)}) collective-permute-start(bf16[4,288,256]{2,1,0:T(8,128)(2,1)S(1)} %copy-done.74), channel_id=1, source_target_pairs={{0,1},{1,0},{2,3},{3,2},{4,5},{5,4},{6,7},{7,6},{8,9},{9,8},{10,11... | collective-permute-start | bytes 1769480 | tf_op jit(solution)/shard_map/ppermute | solution.py:27
  246.6 26.3 %collective-permute-start.41 = (bf16[2,144,1152]{2,1,0:T(8,128)(2,1)S(1)}, bf16[2,144,1152]{2,1,0:T(8,128)(2,1)S(1)}, u32[]{:S(2)}, u32[]{:S(2)}) collective-permute-start(bf16[2,144,1152]{2,1,0:T(8,128)(2,1)S(1)} %get-tuple-element.433), channel_id=1, source_target_pairs={{0,8},{4,12},{8,0},{12,4},{16,24},{20,28},{24,16},{28,20},{1,9},{5... | collective-permute-start | bytes 1990664 | tf_op jit(solution)/shard_map/ppermute | solution.py:27
  248.7 26.4 %collective-permute-start.42 = (bf16[2,144,1152]{2,1,0:T(8,128)(2,1)S(1)}, bf16[2,144,1152]{2,1,0:T(8,128)(2,1)S(1)}, u32[]{:S(2)}, u32[]{:S(2)}) collective-permute-start(bf16[2,144,1152]{2,1,0:T(8,128)(2,1)S(1)} %get-tuple-element.435), channel_id=1, source_target_pairs={{0,4},{4,0},{8,12},{12,8},{16,20},{20,16},{24,28},{28,24},{1,5},{5... | collective-permute-start | bytes 1990664 | tf_op jit(solution)/shard_map/ppermute | solution.py:27
  250.5 34.7 %collective-permute-start.45 = (bf16[1,72,1536]{2,1,0:T(8,128)(2,1)S(1)}, bf16[1,72,1536]{2,1,0:T(8,128)(2,1)S(1)}, u32[]{:S(2)}, u32[]{:S(2)}) collective-permute-start(bf16[1,72,1536]{2,1,0:T(8,128)(2,1)S(1)} %get-tuple-element.439), channel_id=1, source_target_pairs={{0,16},{4,20},{8,24},{12,28},{16,0},{20,4},{24,8},{28,12},{1,17},{... | collective-permute-start | bytes 663560 | tf_op jit(solution)/shard_map/ppermute | solution.py:27
  256.1 24.3 %collective-permute-start.44 = (bf16[4,304,256]{2,1,0:T(8,128)(2,1)S(1)}, bf16[4,304,256]{2,1,0:T(8,128)(2,1)S(1)}, u32[]{:S(2)}, u32[]{:S(2)}) collective-permute-start(bf16[4,304,256]{2,1,0:T(8,128)(2,1)S(1)} %shard_map.240), channel_id=1, source_target_pairs={{0,2},{1,3},{2,0},{3,1},{4,6},{5,7},{6,4},{7,5},{8,10},{9,11},{10,... | collective-permute-start | bytes 1867784 | tf_op jit(solution)/shard_map/ppermute | solution.py:27
  272.9 46.0 %collective-permute-start.49 = (bf16[1,96,1152]{2,1,0:T(8,128)(2,1)}, bf16[1,96,1152]{2,1,0:T(8,128)(2,1)}, u32[]{:S(2)}, u32[]{:S(2)}) collective-permute-start(bf16[1,96,1152]{2,1,0:T(8,128)(2,1)} %add_convert_fusion.1), channel_id=1, source_target_pairs={{0,16},{4,20},{8,24},{12,28},{16,0},{20,4},{24,8},{28,12},{1,17},{... | collective-permute-start | bytes 663560 | tf_op jit(solution)/shard_map/ppermute | solution.py:27
  280.4 38.0 %collective-permute-start.48 = (bf16[2,72,1152]{2,1,0:T(8,128)(2,1)}, bf16[2,72,1152]{2,1,0:T(8,128)(2,1)S(1)}, u32[]{:S(2)}, u32[]{:S(2)}) collective-permute-start(bf16[2,72,1152]{2,1,0:T(8,128)(2,1)} %get-tuple-element.460), channel_id=1, source_target_pairs={{0,4},{4,0},{8,12},{12,8},{16,20},{20,16},{24,28},{28,24},{1,5},{5... | collective-permute-start | bytes 995336 | tf_op jit(solution)/shard_map/ppermute | solution.py:27
  285.1 35.3 %collective-permute-start.50 = (bf16[2,72,1152]{2,1,0:T(8,128)(2,1)}, bf16[2,72,1152]{2,1,0:T(8,128)(2,1)S(1)}, u32[]{:S(2)}, u32[]{:S(2)}) collective-permute-start(bf16[2,72,1152]{2,1,0:T(8,128)(2,1)} %get-tuple-element.464), channel_id=1, source_target_pairs={{0,8},{4,12},{8,0},{12,4},{16,24},{20,28},{24,16},{28,20},{1,9},{5... | collective-permute-start | bytes 995336 | tf_op jit(solution)/shard_map/ppermute | solution.py:27
  292.8 30.0 %collective-permute-start.51 = (bf16[1,72,1536]{2,1,0:T(8,128)(2,1)}, bf16[1,72,1536]{2,1,0:T(8,128)(2,1)}, u32[]{:S(2)}, u32[]{:S(2)}) collective-permute-start(bf16[1,72,1536]{2,1,0:T(8,128)(2,1)} %add_convert_fusion), channel_id=1, source_target_pairs={{0,16},{4,20},{8,24},{12,28},{16,0},{20,4},{24,8},{28,12},{1,17},{... | collective-permute-start | bytes 663560 | tf_op jit(solution)/shard_map/ppermute | solution.py:27
  298.0 87.7 %collective-permute-start.62 = (bf16[1,288,1536]{2,1,0:T(8,128)(2,1)S(1)}, bf16[1,288,1536]{2,1,0:T(8,128)(2,1)S(1)}, u32[]{:S(2)}, u32[]{:S(2)}) collective-permute-start(bf16[1,288,1536]{2,1,0:T(8,128)(2,1)S(1)} %maximum_select_fusion.refs_0_), channel_id=1, source_target_pairs={{0,4},{4,0},{8,12},{12,8},{16,20},{20,16},{24,28},{28,24},{1,5},{5... | collective-permute-start | bytes 2654216 | tf_op jit(solution)/shard_map/ppermute | solution.py:27
  320.4 34.5 %collective-permute-start.56 = (bf16[1,192,1152]{2,1,0:T(8,128)(2,1)S(1)}, bf16[1,192,1152]{2,1,0:T(8,128)(2,1)S(1)}, u32[]{:S(2)}, u32[]{:S(2)}) collective-permute-start(bf16[1,192,1152]{2,1,0:T(8,128)(2,1)S(1)} %maximum_select_fusion.6), channel_id=1, source_target_pairs={{0,4},{4,0},{8,12},{12,8},{16,20},{20,16},{24,28},{28,24},{1,5},{5... | collective-permute-start | bytes 1327112 | tf_op jit(solution)/shard_map/ppermute | solution.py:27
  333.4 26.3 %collective-permute-start.57 = (bf16[1,144,1536]{2,1,0:T(8,128)(2,1)S(1)}, bf16[1,144,1536]{2,1,0:T(8,128)(2,1)S(1)}, u32[]{:S(2)}, u32[]{:S(2)}) collective-permute-start(bf16[1,144,1536]{2,1,0:T(8,128)(2,1)S(1)} %maximum_select_fusion.7), channel_id=1, source_target_pairs={{0,8},{4,12},{8,0},{12,4},{16,24},{20,28},{24,16},{28,20},{1,9},{5... | collective-permute-start | bytes 1327112 | tf_op jit(solution)/shard_map/ppermute | solution.py:27
  335.0 26.8 %collective-permute-start.58 = (bf16[2,25,288]{2,1,0:T(8,128)(2,1)S(1)}, bf16[2,25,288]{2,1,0:T(8,128)(2,1)S(1)}, u32[]{:S(2)}, u32[]{:S(2)}) collective-permute-start(bf16[2,25,288]{2,1,0:T(8,128)(2,1)S(1)} %maximum_select_fusion.19), channel_id=1, source_target_pairs={{0,8},{4,12},{8,0},{12,4},{16,24},{20,28},{24,16},{28,20},{1,9},{5... | collective-permute-start | bytes 86408 | tf_op jit(solution)/shard_map/ppermute | solution.py:27
  359.8 24.0 %collective-permute-start.61 = (bf16[1,384,1152]{2,1,0:T(8,128)(2,1)S(1)}, bf16[1,384,1152]{2,1,0:T(8,128)(2,1)S(1)}, u32[]{:S(2)}, u32[]{:S(2)}) collective-permute-start(bf16[1,384,1152]{2,1,0:T(8,128)(2,1)S(1)} %maximum_select_fusion.1.refs_0_), channel_id=1, source_target_pairs={{0,8},{4,12},{8,0},{12,4},{16,24},{20,28},{24,16},{28,20},{1,9},{5... | collective-permute-start | bytes 2654216 | tf_op jit(solution)/shard_map/ppermute | solution.py:27
  361.9 23.8 %collective-permute-start.63 = (bf16[1,288,1536]{2,1,0:T(8,128)(2,1)S(1)}, bf16[1,288,1536]{2,1,0:T(8,128)(2,1)S(1)}, u32[]{:S(2)}, u32[]{:S(2)}) collective-permute-start(bf16[1,288,1536]{2,1,0:T(8,128)(2,1)S(1)} %maximum_select_fusion.2.refs_2_), channel_id=1, source_target_pairs={{0,4},{4,0},{8,12},{12,8},{16,20},{20,16},{24,28},{28,24},{1,5},{5... | collective-permute-start | bytes 2654216 | tf_op jit(solution)/shard_map/ppermute | solution.py:27
  364.8 25.2 %collective-permute-start.64 = (bf16[2,72,1152]{2,1,0:T(8,128)(2,1)S(1)}, bf16[2,72,1152]{2,1,0:T(8,128)(2,1)S(1)}, u32[]{:S(2)}, u32[]{:S(2)}) collective-permute-start(bf16[2,72,1152]{2,1,0:T(8,128)(2,1)S(1)} %maximum_select_fusion.8), channel_id=1, source_target_pairs={{0,4},{4,0},{8,12},{12,8},{16,20},{20,16},{24,28},{28,24},{1,5},{5... | collective-permute-start | bytes 995336 | tf_op jit(solution)/shard_map/ppermute | solution.py:27
  365.0 26.4 %collective-permute-start.65 = (bf16[2,72,1152]{2,1,0:T(8,128)(2,1)S(1)}, bf16[2,72,1152]{2,1,0:T(8,128)(2,1)S(1)}, u32[]{:S(2)}, u32[]{:S(2)}) collective-permute-start(bf16[2,72,1152]{2,1,0:T(8,128)(2,1)S(1)} %maximum_select_fusion.9), channel_id=1, source_target_pairs={{0,8},{4,12},{8,0},{12,4},{16,24},{20,28},{24,16},{28,20},{1,9},{5... | collective-permute-start | bytes 995336 | tf_op jit(solution)/shard_map/ppermute | solution.py:27
  (139 other events, 1489.6 us)
